TPU v7x, 256 devices: a whole 4x4x8 slice. The times are simulated.
256 devices in a mesh: blk: 64 (over x, z, y_hi), head: 4 (over y_lo, core).
Axes of the slice: x: 4, y: 4 (y_hi: 2, y_lo: 2; y = y_hi * 2 + y_lo), z: 8, core: 2. Of those that a mesh axis runs over, the one named last changes fastest.
Arguments:
- queries: bfloat16 [32768, 1024], P('blk', 'head'), may hold values from -18 to 18, as said below
- key_rows: bfloat16 [32768, 128], P('blk'), may hold values from -18 to 18, as said below
- value_rows: bfloat16 [32768, 128], P('blk'), may hold values from -6 to 6
- grad_out: bfloat16 [32768, 1024], P('blk', 'head'), may hold values from -6 to 6
- positions: int32 [32768], replicated, may hold values from 0 to 32767, each once
Outputs:
- grad_queries: bfloat16 [32768, 1024], P('blk', 'head')
- grad_keys: bfloat16 [32768, 128], P(('blk', 'head'))
- grad_values: bfloat16 [32768, 128], P(('blk', 'head'))
Inputs may be any that keep to these rules, and one draw needn't show every extreme that they name: `queries`: values of order one. `key_rows`: values of order one. `positions`: A permutation of 0 .. 32767.
All inputs are finite; a program needn't handle non-finite values.
Results may differ from a plain program's by a relative error of at most 0.0065.
Values may be sent and summed in bfloat16 or wider, within the bound.
No kernel may reach another device: no remote copies, remote signals or barrier semaphores. Data moves between devices by JAX's collectives and lax.ppermute only.
A program may use at most 64 MiB of HBM per device.

v0:
```python
import jax
import jax.numpy as jnp
from jax import lax
from jax.sharding import PartitionSpec as P

HD = 128
SPAN = 4


def from_behind(value, axis, steps):
    count = lax.axis_size(axis)
    pairs = [(source, (source + steps) % count) for source in range(count)]
    return lax.ppermute(value, axis, pairs)


def shards(queries, key_rows, value_rows, grad_out, positions):
    rows_dev = key_rows.shape[0]
    stripes = lax.axis_size("blk")
    here_index = lax.axis_index("blk")
    heads_here = queries.shape[1] // HD
    softmax_scale = 1.0 / HD**0.5

    def places(offset):
        first_row = (here_index + offset) % stripes * rows_dev
        return lax.dynamic_slice_in_dim(positions, first_row, rows_dev)

    def split_heads(flat_rows):
        return flat_rows.reshape(rows_dev, heads_here, HD)

    def masked_scores(query_tile, key_tile, query_places, key_places):
        raw_scores = (
            jnp.einsum("thd,kd->htk", query_tile, key_tile, preferred_element_type=jnp.float32)
            * softmax_scale
        )
        allowed = key_places[None, :] <= query_places[:, None]
        return jnp.where(allowed[None], raw_scores, -jnp.inf)

    own_places = places(0)
    query_heads = split_heads(queries)
    grad_heads = split_heads(grad_out)
    running = jnp.full((heads_here, rows_dev), -jnp.inf, jnp.float32)
    totals = jnp.zeros((heads_here, rows_dev), jnp.float32)
    key_tile, value_tile = (key_rows, value_rows)
    kept_tiles = []
    kept_scores = []
    for offset in range(SPAN):
        kept_tiles.append((key_tile, value_tile))
        scores = masked_scores(query_heads, key_tile, own_places, places(offset))
        kept_scores.append(scores)
        newest = jnp.maximum(running, jnp.max(scores, axis=-1))
        totals = totals * jnp.exp(running - newest) + jnp.sum(
            jnp.exp(scores - newest[:, :, None]), axis=-1
        )
        running = newest
        if offset < SPAN - 1:
            key_tile, value_tile = from_behind((key_tile, value_tile), "blk", -1)
    log_total = running + jnp.log(totals)
    attended = jnp.zeros((heads_here, rows_dev, HD), jnp.float32)
    for offset in range(SPAN):
        attention_low = jnp.exp(kept_scores[offset] - log_total[:, :, None]).astype(jnp.bfloat16)
        attended = attended + jnp.einsum(
            "htk,kd->htd", attention_low, kept_tiles[offset][1], preferred_element_type=jnp.float32
        )
    kept_scores = []
    delta_rows = jnp.sum(
        jnp.transpose(grad_heads.astype(jnp.float32), (1, 0, 2)) * attended, axis=-1
    )
    zero_rows = jnp.zeros((rows_dev, HD), jnp.float32)
    zero_query = jnp.zeros((rows_dev, heads_here * HD), jnp.float32)
    query_flat, grad_flat = (queries, grad_out)
    log_tile, delta_tile, query_acc = (log_total, delta_rows, zero_query)
    key_acc, value_acc = (zero_rows, zero_rows)
    for offset in range(SPAN):
        gradients_query_tile = split_heads(query_flat)
        grad_tile = split_heads(grad_flat)
        gradients_scores = masked_scores(
            gradients_query_tile, key_rows, places(-offset), own_places
        )
        attention = jnp.exp(gradients_scores - log_tile[:, :, None])
        gradients_attention_low = attention.astype(jnp.bfloat16)
        grad_value = jnp.einsum(
            "htk,thd->kd", gradients_attention_low, grad_tile, preferred_element_type=jnp.float32
        )
        grad_weights = jnp.einsum(
            "thd,kd->htk", grad_tile, value_rows, preferred_element_type=jnp.float32
        )
        grad_scores = (attention * (grad_weights - delta_tile[:, :, None]) * softmax_scale).astype(
            jnp.bfloat16
        )
        grad_query = jnp.einsum(
            "htk,kd->thd", grad_scores, key_rows, preferred_element_type=jnp.float32
        )
        grad_key = jnp.einsum(
            "htk,thd->kd", grad_scores, gradients_query_tile, preferred_element_type=jnp.float32
        )
        grad_query, grad_key, grad_value = (
            grad_query.reshape(rows_dev, heads_here * HD),
            grad_key,
            grad_value,
        )
        query_acc = query_acc + grad_query
        key_acc = key_acc + grad_key
        value_acc = value_acc + grad_value
        if offset < SPAN - 1:
            query_flat, grad_flat = from_behind((query_flat, grad_flat), "blk", 1)
            log_tile, delta_tile, query_acc = from_behind(
                (log_tile, delta_tile, query_acc), "blk", 1
            )
    query_total = from_behind(query_acc, "blk", -(SPAN - 1))
    key_sum, value_sum = (
        lax.psum_scatter(key_acc, "head", scatter_dimension=0, tiled=True),
        lax.psum_scatter(value_acc, "head", scatter_dimension=0, tiled=True),
    )
    return (
        query_total.astype(jnp.bfloat16),
        key_sum.astype(jnp.bfloat16),
        value_sum.astype(jnp.bfloat16),
    )


def solution(mesh):
    return jax.shard_map(
        shards,
        mesh=mesh,
        in_specs=(P("blk", "head"), P("blk", None), P("blk", None), P("blk", "head"), P()),
        out_specs=(P("blk", "head"), P(("blk", "head"), None), P(("blk", "head"), None)),
        check_vma=False,
    )
```

profile of v0, /device:TPU:1, one launch (start us, length us, event | category | flops | bytes accessed | tf_op | source)
XLA Modules:
  0.0 175.2 jit_solution(11534035665794819122)
XLA Ops:
  8.3 11.3 %collective-permute-start.3 = (bf16[512,128]{0,1:T(8,128)(2,1)S(1)}, bf16[512,128]{0,1:T(8,128)(2,1)S(1)}, u32[]{:S(2)}, u32[]{:S(2)}) collective-permute-start(bf16[512,128]{0,1:T(8,128)(2,1)S(1)} %copy.42), channel_id=1, source_target_pairs={{0,252},{4,0},{8,4},{12,8},{16,12},{20,16},{24,20},{28,24},{32,28}... | collective-permute-start | bytes 393224 | tf_op jit(solution)/shard_map/ppermute | solution.py:13
  19.7 1.1 copy.49
  20.8 3.0 %collective-permute-start.7 = (bf16[512,256]{0,1:T(8,128)(2,1)S(1)}, bf16[512,256]{0,1:T(8,128)(2,1)S(1)}, u32[]{:S(2)}, u32[]{:S(2)}) collective-permute-start(bf16[512,256]{0,1:T(8,128)(2,1)S(1)} %copy.49), channel_id=1, source_target_pairs={{0,4},{4,8},{8,12},{12,16},{16,20},{20,24},{24,28},{28,32},{32,36}... | collective-permute-start | bytes 786440 | tf_op jit(solution)/shard_map/ppermute | solution.py:13
  26.0 1.8 %broadcast_compare_fusion = (pred[512,512]{0,1:T(8,128)(4,1)}, pred[512,512]{0,1:T(8,128)(4,1)}, pred[512,512]{0,1:T(8,128)(4,1)S(1)}, pred[512,512]{0,1:T(8,128...) fusion(s32[512]{0:T(512)S(1)} %get-tuple-element.6, ...), kind=kLoop, calls=%fused_computation.72 | loop fusion | flops 1835008 | bytes 1849344 | tf_op jit(solution)/shard_map/le | solution.py:35
  28.4 7.1 %collective-permute-start.4 = (bf16[512,128]{0,1:T(8,128)(2,1)S(1)}, bf16[512,128]{0,1:T(8,128)(2,1)S(1)}, u32[]{:S(2)}, u32[]{:S(2)}) collective-permute-start(bf16[512,128]{0,1:T(8,128)(2,1)S(1)} %collective-permute-done.3), channel_id=1, source_target_pairs={{0,252},{4,0},{8,4},{12,8},{16,12},{20,16},{24,20},{28,24},{32,28}... | collective-permute-start | bytes 393224 | tf_op jit(solution)/shard_map/ppermute | solution.py:13
  36.1 7.1 %collective-permute-done.4 = bf16[512,128]{0,1:T(8,128)(2,1)S(1)} collective-permute-done((bf16[512,128]{0,1:T(8,128)(2,1)S(1)}, bf16[512,128]{0,1:T(8,128)(2,1)S(1)}, u32[]{:S(2)}, u32[]{:S(2)}) %collective-permute-start.4) | collective-permute-done | bytes 131104 | tf_op jit(solution)/shard_map/ppermute | solution.py:13
  43.3 1.8 %collective-permute-start.5 = (bf16[512,128]{0,1:T(8,128)(2,1)S(1)}, bf16[512,128]{0,1:T(8,128)(2,1)S(1)}, u32[]{:S(2)}, u32[]{:S(2)}) collective-permute-start(bf16[512,128]{0,1:T(8,128)(2,1)S(1)} %collective-permute-done.4), channel_id=1, source_target_pairs={{0,252},{4,0},{8,4},{12,8},{16,12},{20,16},{24,20},{28,24},{32,28}... | collective-permute-start | bytes 393224 | tf_op jit(solution)/shard_map/ppermute | solution.py:13
  46.1 1.1 collective-permute-start.2
  47.2 1.8 %collective-permute-start.12 = (bf16[512,256]{0,1:T(8,128)(2,1)S(1)}, bf16[512,256]{0,1:T(8,128)(2,1)}, u32[]{:S(2)}, u32[]{:S(2)}) collective-permute-start(bf16[512,256]{0,1:T(8,128)(2,1)S(1)} %collective-permute-done.7), channel_id=1, source_target_pairs={{0,4},{4,8},{8,12},{12,16},{16,20},{20,24},{24,28},{28,32},{32,36}... | collective-permute-start | bytes 786440 | tf_op jit(solution)/shard_map/ppermute | solution.py:13
  49.5 1.3 collective-permute-start.14
  53.2 1.5 collective-permute-start.8
  56.1 1.1 convolution_bitcast_fusion.3
  60.5 2.9 %collective-permute-done.8 = f32[2,512]{1,0:T(2,128)S(1)} collective-permute-done((f32[2,512]{1,0:T(2,128)S(1)}, f32[2,512]{1,0:T(2,128)S(1)}, u32[]{:S(2)}, u32[]{:S(2)}) %collective-permute-start.8) | collective-permute-done | bytes 4128 | tf_op jit(solution)/shard_map/ppermute | solution.py:13
  63.4 3.6 %collective-permute-done.10 = f32[2,512]{1,0:T(2,128)S(1)} collective-permute-done((f32[2,512]{1,0:T(2,128)S(1)}, f32[2,512]{1,0:T(2,128)S(1)}, u32[]{:S(2)}, u32[]{:S(2)}) %collective-permute-start.10) | collective-permute-done | bytes 4128 | tf_op jit(solution)/shard_map/ppermute | solution.py:13
  67.0 1.9 %fusion.12 = bf16[2,512,512]{1,2,0:T(8,128)(2,1)S(1)} fusion(f32[512,512,2]{1,0,2:T(8,128)S(1)} %fusion.90, f32[2,512]{1,0:T(2,128)S(1)} %collective-permute-done.10, f32[2,512]{1,0:T(2,128)S(1)} %collective-permute-done.8, pred[512,512]{0,1:T(8,128)(4,1)} %get-tuple-element.19, bf16[512,2,128]{0,2,1:T(8,128)(2,1)} %bitcast.21, ...), kind=kOutput, calls=%fused_computation.17 | convolution fusion | flops 137887744 | bytes 3809280 | tf_op jit(solution)/shard_map/thd,kd->htk/dot_general | solution.py:84
  69.6 2.4 %fusion.27 = f32[512,128]{1,0:T(8,128)} fusion(f32[512,128]{1,0:T(8,128)S(1)} %copy-done.10, bf16[512,2,128]{0,2,1:T(8,128)(2,1)} %bitcast.21, f32[512,512,2]{1,0,2:T(8,128)S(1)} %fusion.90, f32[2,512]{1,0:T(2,128)S(1)} %collective-permute-done.8, pred[512,512]{0,1:T(8,128)(4,1)S(1)} %copy-done.9), kind=kOutput, calls=%fused_computation.57 | convolution fusion | flops 136380416 | bytes 3149824 | tf_op jit(solution)/shard_map/htk,thd->kd/dot_general | solution.py:81
  72.5 5.6 %collective-permute-done.13 = f32[2,512]{1,0:T(2,128)S(1)} collective-permute-done((f32[2,512]{1,0:T(2,128)S(1)}, f32[2,512]{1,0:T(2,128)S(1)}, u32[]{:S(2)}, u32[]{:S(2)}) %collective-permute-start.13) | collective-permute-done | bytes 4128 | tf_op jit(solution)/shard_map/ppermute | solution.py:13
  78.2 1.4 fusion.88
  79.6 2.0 %fusion.7 = bf16[2,512,512]{1,2,0:T(8,128)(2,1)S(1)} fusion(f32[512,512,2]{1,0,2:T(8,128)S(1)} %fusion.88, f32[2,512]{1,0:T(2,128)S(1)} %collective-permute-done.15, f32[2,512]{1,0:T(2,128)S(1)} %collective-permute-done.13, pred[512,512]{0,1:T(8,128)(4,1)S(1)} %copy-done.8, bf16[512,2,128]{0,2,1:T(8,128)(2,1)} %bitcast.28, bf16[512,128]{1,0:T(8,128)(2,1)S(1)} %copy-done.4), kind=kOutput, calls=%fused_computation.10 | convolution fusion | flops 137887744 | bytes 3809280 | tf_op jit(solution)/shard_map/thd,kd->htk/dot_general | solution.py:84
  82.4 1.4 fusion.25
  83.8 9.8 %collective-permute-done.17 = bf16[512,256]{0,1:T(8,128)(2,1)S(1)} collective-permute-done((bf16[512,256]{0,1:T(8,128)(2,1)}, bf16[512,256]{0,1:T(8,128)(2,1)S(1)}, u32[]{:S(2)}, u32[]{:S(2)}) %collective-permute-start.17) | collective-permute-done | bytes 262176 | tf_op jit(solution)/shard_map/ppermute | solution.py:13
  94.0 2.7 %collective-permute-done.19 = bf16[512,256]{0,1:T(8,128)(2,1)S(1)} collective-permute-done((bf16[512,256]{0,1:T(8,128)(2,1)}, bf16[512,256]{0,1:T(8,128)(2,1)S(1)}, u32[]{:S(2)}, u32[]{:S(2)}) %collective-permute-start.19) | collective-permute-done | bytes 262176 | tf_op jit(solution)/shard_map/ppermute | solution.py:13
  97.6 1.1 add.162
  98.8 1.1 fusion.26
  100.0 2.6 %fusion.28 = f32[512,128]{1,0:T(8,128)S(1)} fusion(f32[512,128]{1,0:T(8,128)} %fusion.27, bf16[512,2,128]{0,2,1:T(8,128)(2,1)} %bitcast.28, f32[512,512,2]{1,0,2:T(8,128)} %copy-done.1, f32[2,512]{1,0:T(2,128)S(1)} %collective-permute-done.13, pred[512,512]{0,1:T(8,128)(4,1)} %get-tuple-element.14), kind=kOutput, calls=%fused_computation.58 | convolution fusion | flops 136380416 | bytes 3149824 | tf_op jit(solution)/shard_map/htk,thd->kd/dot_general | solution.py:81
  102.6 9.9 %collective-permute-done.11 = f32[512,256]{1,0:T(8,128)S(1)} collective-permute-done((f32[512,256]{1,0:T(8,128)S(1)}, f32[512,256]{1,0:T(8,128)S(1)}, u32[]{:S(2)}, u32[]{:S(2)}) %collective-permute-start.11) | collective-permute-done | bytes 524320 | tf_op jit(solution)/shard_map/ppermute | solution.py:13
  112.7 1.4 fusion.29
  114.7 11.9 %collective-permute-done.16 = f32[512,256]{1,0:T(8,128)S(1)} collective-permute-done((f32[512,256]{1,0:T(8,128)S(1)}, f32[512,256]{1,0:T(8,128)S(1)}, u32[]{:S(2)}, u32[]{:S(2)}) %collective-permute-start.16) | collective-permute-done | bytes 524320 | tf_op jit(solution)/shard_map/ppermute | solution.py:13
  126.7 4.1 %reduce-scatter.3.cloned.1.call-done = f32[128,128]{1,0:T(8,128)} async-done(((f32[512,128]{1,0:T(8,128)}), f32[128,128]{1,0:T(8,128)}) %reduce-scatter.3.cloned.1.call-update) | async-done | bytes 65552 | tf_op jit(solution)/shard_map/reduce_scatter | solution.py:111
  130.8 1.5 convert_element_type.53
  132.3 33.9 %reduce-scatter.5.cloned.1.call-done = f32[128,128]{1,0:T(8,128)} async-done(((f32[512,128]{1,0:T(8,128)}), f32[128,128]{1,0:T(8,128)}) %reduce-scatter.5.cloned.1.call-update) | async-done | bytes 65552 | tf_op jit(solution)/shard_map/reduce_scatter | solution.py:112
  166.2 1.5 convert_element_type.57
  (90 shorter events, 17.8 us)
Async XLA Ops:
  7.2 20.6 %copy-start = (bf16[512,128]{1,0:T(8,128)(2,1)S(1)}, bf16[512,128]{1,0:T(8,128)(2,1)}, u32[]{:S(2)}) copy-start(bf16[512,128]{1,0:T(8,128)(2,1)} %param.6) | copy-start | bytes 393220
  7.2 20.6 %copy-start.5 = (bf16[512,256]{1,0:T(8,128)(2,1)S(1)}, bf16[512,256]{1,0:T(8,128)(2,1)}, u32[]{:S(2)}) copy-start(bf16[512,256]{1,0:T(8,128)(2,1)} %param.5) | copy-start | bytes 786436
  7.2 123.7 %reduce-scatter.3.cloned.1.call-start = ((), (), s32[]{:S(2)}) async-start(), calls=%async_computation.2 | async-start | bytes 327680 | tf_op jit(solution)/shard_map/reduce_scatter | solution.py:111
  8.3 20.0 %collective-permute-start.3 = (bf16[512,128]{0,1:T(8,128)(2,1)S(1)}, bf16[512,128]{0,1:T(8,128)(2,1)S(1)}, u32[]{:S(2)}, u32[]{:S(2)}) collective-permute-start(bf16[512,128]{0,1:T(8,128)(2,1)S(1)} %copy.42), channel_id=1, source_target_pairs={{0,252},{4,0},{8,4},{12,8},{16,12},{20,16},{24,20},{28,24},{32,28}... | collective-permute-start | bytes 393224 | tf_op jit(solution)/shard_map/ppermute | solution.py:13
  19.6 15.9 %collective-permute-start = (bf16[512,128]{1,0:T(8,128)(2,1)}, bf16[512,128]{1,0:T(8,128)(2,1)S(1)}, u32[]{:S(2)}, u32[]{:S(2)}) collective-permute-start(bf16[512,128]{1,0:T(8,128)(2,1)} %param.6), channel_id=1, source_target_pairs={{0,252},{4,0},{8,4},{12,8},{16,12},{20,16},{24,20},{28,24},{32,28}... | collective-permute-start | bytes 393224 | tf_op jit(solution)/shard_map/ppermute | solution.py:13
  20.8 26.4 %collective-permute-start.7 = (bf16[512,256]{0,1:T(8,128)(2,1)S(1)}, bf16[512,256]{0,1:T(8,128)(2,1)S(1)}, u32[]{:S(2)}, u32[]{:S(2)}) collective-permute-start(bf16[512,256]{0,1:T(8,128)(2,1)S(1)} %copy.49), channel_id=1, source_target_pairs={{0,4},{4,8},{8,12},{12,16},{16,20},{20,24},{24,28},{28,32},{32,36}... | collective-permute-start | bytes 786440 | tf_op jit(solution)/shard_map/ppermute | solution.py:13
  24.9 24.6 %collective-permute-start.9 = (bf16[512,256]{0,1:T(8,128)(2,1)S(1)}, bf16[512,256]{0,1:T(8,128)(2,1)}, u32[]{:S(2)}, u32[]{:S(2)}) collective-permute-start(bf16[512,256]{0,1:T(8,128)(2,1)S(1)} %copy.38), channel_id=1, source_target_pairs={{0,4},{4,8},{8,12},{12,16},{16,20},{20,24},{24,28},{28,32},{32,36}... | collective-permute-start | bytes 786440 | tf_op jit(solution)/shard_map/ppermute | solution.py:13
  28.4 14.9 %collective-permute-start.4 = (bf16[512,128]{0,1:T(8,128)(2,1)S(1)}, bf16[512,128]{0,1:T(8,128)(2,1)S(1)}, u32[]{:S(2)}, u32[]{:S(2)}) collective-permute-start(bf16[512,128]{0,1:T(8,128)(2,1)S(1)} %collective-permute-done.3), channel_id=1, source_target_pairs={{0,252},{4,0},{8,4},{12,8},{16,12},{20,16},{24,20},{28,24},{32,28}... | collective-permute-start | bytes 393224 | tf_op jit(solution)/shard_map/ppermute | solution.py:13
  35.5 10.6 %collective-permute-start.1 = (bf16[512,128]{1,0:T(8,128)(2,1)S(1)}, bf16[512,128]{1,0:T(8,128)(2,1)S(1)}, u32[]{:S(2)}, u32[]{:S(2)}) collective-permute-start(bf16[512,128]{1,0:T(8,128)(2,1)S(1)} %collective-permute-done), channel_id=1, source_target_pairs={{0,252},{4,0},{8,4},{12,8},{16,12},{20,16},{24,20},{28,24},{32,28}... | collective-permute-start | bytes 393224 | tf_op jit(solution)/shard_map/ppermute | solution.py:13
  43.3 14.0 %collective-permute-start.5 = (bf16[512,128]{0,1:T(8,128)(2,1)S(1)}, bf16[512,128]{0,1:T(8,128)(2,1)S(1)}, u32[]{:S(2)}, u32[]{:S(2)}) collective-permute-start(bf16[512,128]{0,1:T(8,128)(2,1)S(1)} %collective-permute-done.4), channel_id=1, source_target_pairs={{0,252},{4,0},{8,4},{12,8},{16,12},{20,16},{24,20},{28,24},{32,28}... | collective-permute-start | bytes 393224 | tf_op jit(solution)/shard_map/ppermute | solution.py:13
  46.1 5.3 %collective-permute-start.2 = (bf16[512,128]{1,0:T(8,128)(2,1)S(1)}, bf16[512,128]{1,0:T(8,128)(2,1)S(1)}, u32[]{:S(2)}, u32[]{:S(2)}) collective-permute-start(bf16[512,128]{1,0:T(8,128)(2,1)S(1)} %collective-permute-done.1), channel_id=1, source_target_pairs={{0,252},{4,0},{8,4},{12,8},{16,12},{20,16},{24,20},{28,24},{32,28}... | collective-permute-start | bytes 393224 | tf_op jit(solution)/shard_map/ppermute | solution.py:13
  47.2 31.0 %collective-permute-start.12 = (bf16[512,256]{0,1:T(8,128)(2,1)S(1)}, bf16[512,256]{0,1:T(8,128)(2,1)}, u32[]{:S(2)}, u32[]{:S(2)}) collective-permute-start(bf16[512,256]{0,1:T(8,128)(2,1)S(1)} %collective-permute-done.7), channel_id=1, source_target_pairs={{0,4},{4,8},{8,12},{12,16},{16,20},{20,24},{24,28},{28,32},{32,36}... | collective-permute-start | bytes 786440 | tf_op jit(solution)/shard_map/ppermute | solution.py:13
  49.5 30.1 %collective-permute-start.14 = (bf16[512,256]{0,1:T(8,128)(2,1)}, bf16[512,256]{0,1:T(8,128)(2,1)}, u32[]{:S(2)}, u32[]{:S(2)}) collective-permute-start(bf16[512,256]{0,1:T(8,128)(2,1)} %collective-permute-done.9), channel_id=1, source_target_pairs={{0,4},{4,8},{8,12},{12,16},{16,20},{20,24},{24,28},{28,32},{32,36}... | collective-permute-start | bytes 786440 | tf_op jit(solution)/shard_map/ppermute | solution.py:13
  53.2 10.3 %collective-permute-start.8 = (f32[2,512]{1,0:T(2,128)S(1)}, f32[2,512]{1,0:T(2,128)S(1)}, u32[]{:S(2)}, u32[]{:S(2)}) collective-permute-start(f32[2,512]{1,0:T(2,128)S(1)} %log_add_fusion), channel_id=1, source_target_pairs={{0,4},{4,8},{8,12},{12,16},{16,20},{20,24},{24,28},{28,32},{32,36}... | collective-permute-start | bytes 12296 | tf_op jit(solution)/shard_map/ppermute | solution.py:13
  58.4 8.6 %collective-permute-start.10 = (f32[2,512]{1,0:T(2,128)S(1)}, f32[2,512]{1,0:T(2,128)S(1)}, u32[]{:S(2)}, u32[]{:S(2)}) collective-permute-start(f32[2,512]{1,0:T(2,128)S(1)} %fusion.23), channel_id=1, source_target_pairs={{0,4},{4,8},{8,12},{12,16},{16,20},{20,24},{24,28},{28,32},{32,36}... | collective-permute-start | bytes 12296 | tf_op jit(solution)/shard_map/ppermute | solution.py:13
  60.5 37.1 %collective-permute-start.6 = (f32[512,256]{1,0:T(8,128)}, f32[512,256]{1,0:T(8,128)}, u32[]{:S(2)}, u32[]{:S(2)}) collective-permute-start(f32[512,256]{1,0:T(8,128)} %copy.48), channel_id=1, source_target_pairs={{0,4},{4,8},{8,12},{12,16},{16,20},{20,24},{24,28},{28,32},{32,36}... | collective-permute-start | bytes 1572872 | tf_op jit(solution)/shard_map/ppermute | solution.py:13
  67.0 2.6 %copy-start.10 = (f32[512,128]{1,0:T(8,128)S(1)}, f32[512,128]{1,0:T(8,128)}, u32[]{:S(2)}) copy-start(f32[512,128]{1,0:T(8,128)} %convolution_bitcast_fusion.3) | copy-start | bytes 786436
  69.4 8.8 %collective-permute-start.13 = (f32[2,512]{1,0:T(2,128)S(1)}, f32[2,512]{1,0:T(2,128)S(1)}, u32[]{:S(2)}, u32[]{:S(2)}) collective-permute-start(f32[2,512]{1,0:T(2,128)S(1)} %collective-permute-done.8), channel_id=1, source_target_pairs={{0,4},{4,8},{8,12},{12,16},{16,20},{20,24},{24,28},{28,32},{32,36}... | collective-permute-start | bytes 12296 | tf_op jit(solution)/shard_map/ppermute | solution.py:13
  69.5 8.8 %collective-permute-start.15 = (f32[2,512]{1,0:T(2,128)S(1)}, f32[2,512]{1,0:T(2,128)S(1)}, u32[]{:S(2)}, u32[]{:S(2)}) collective-permute-start(f32[2,512]{1,0:T(2,128)S(1)} %collective-permute-done.10), channel_id=1, source_target_pairs={{0,4},{4,8},{8,12},{12,16},{16,20},{20,24},{24,28},{28,32},{32,36}... | collective-permute-start | bytes 12296 | tf_op jit(solution)/shard_map/ppermute | solution.py:13
  72.3 7.3 %copy-start.8 = (pred[512,512]{0,1:T(8,128)(4,1)S(1)}, pred[512,512]{0,1:T(8,128)(4,1)}, u32[]{:S(2)}) copy-start(pred[512,512]{0,1:T(8,128)(4,1)} %get-tuple-element.14) | copy-start | bytes 786436
  78.1 15.8 %collective-permute-start.18 = (f32[2,512]{1,0:T(2,128)S(1)}, f32[2,512]{1,0:T(2,128)S(1)}, u32[]{:S(2)}, u32[]{:S(2)}) collective-permute-start(f32[2,512]{1,0:T(2,128)S(1)} %collective-permute-done.13), channel_id=1, source_target_pairs={{0,4},{4,8},{8,12},{12,16},{16,20},{20,24},{24,28},{28,32},{32,36}... | collective-permute-start | bytes 12296 | tf_op jit(solution)/shard_map/ppermute | solution.py:13
  78.2 15.8 %collective-permute-start.20 = (f32[2,512]{1,0:T(2,128)S(1)}, f32[2,512]{1,0:T(2,128)S(1)}, u32[]{:S(2)}, u32[]{:S(2)}) collective-permute-start(f32[2,512]{1,0:T(2,128)S(1)} %collective-permute-done.15), channel_id=1, source_target_pairs={{0,4},{4,8},{8,12},{12,16},{16,20},{20,24},{24,28},{28,32},{32,36}... | collective-permute-start | bytes 12296 | tf_op jit(solution)/shard_map/ppermute | solution.py:13
  82.2 14.5 %copy-start.7 = (pred[512,512]{0,1:T(8,128)(4,1)S(1)}, pred[512,512]{0,1:T(8,128)(4,1)}, u32[]{:S(2)}) copy-start(pred[512,512]{0,1:T(8,128)(4,1)} %get-tuple-element.13) | copy-start | bytes 786436
  82.2 11.3 %collective-permute-start.17 = (bf16[512,256]{0,1:T(8,128)(2,1)}, bf16[512,256]{0,1:T(8,128)(2,1)S(1)}, u32[]{:S(2)}, u32[]{:S(2)}) collective-permute-start(bf16[512,256]{0,1:T(8,128)(2,1)} %collective-permute-done.12), channel_id=1, source_target_pairs={{0,4},{4,8},{8,12},{12,16},{16,20},{20,24},{24,28},{28,32},{32,36}... | collective-permute-start | bytes 786440 | tf_op jit(solution)/shard_map/ppermute | solution.py:13
  82.3 14.4 %collective-permute-start.19 = (bf16[512,256]{0,1:T(8,128)(2,1)}, bf16[512,256]{0,1:T(8,128)(2,1)S(1)}, u32[]{:S(2)}, u32[]{:S(2)}) collective-permute-start(bf16[512,256]{0,1:T(8,128)(2,1)} %collective-permute-done.14), channel_id=1, source_target_pairs={{0,4},{4,8},{8,12},{12,16},{16,20},{20,24},{24,28},{28,32},{32,36}... | collective-permute-start | bytes 786440 | tf_op jit(solution)/shard_map/ppermute | solution.py:13
  94.0 3.6 %copy-start.2 = (f32[512,512,2]{1,0,2:T(8,128)}, f32[512,512,2]{1,0,2:T(8,128)S(1)}, u32[]{:S(2)}) copy-start(f32[512,512,2]{1,0,2:T(8,128)S(1)} %fusion.86) | copy-start | bytes 6291460
  98.7 13.8 %collective-permute-start.11 = (f32[512,256]{1,0:T(8,128)S(1)}, f32[512,256]{1,0:T(8,128)S(1)}, u32[]{:S(2)}, u32[]{:S(2)}) collective-permute-start(f32[512,256]{1,0:T(8,128)S(1)} %add.162), channel_id=1, source_target_pairs={{0,4},{4,8},{8,12},{12,16},{16,20},{20,24},{24,28},{28,32},{32,36}... | collective-permute-start | bytes 1572872 | tf_op jit(solution)/shard_map/ppermute | solution.py:13
  100.0 66.2 %reduce-scatter.5.cloned.1.call-start = ((), (), s32[]{:S(2)}) async-start(), calls=%async_computation.3 | async-start | bytes 327680 | tf_op jit(solution)/shard_map/reduce_scatter | solution.py:112
  100.0 12.7 %copy-start.3 = (f32[512,512,2]{1,0,2:T(8,128)S(1)}, f32[512,512,2]{1,0,2:T(8,128)}, u32[]{:S(2)}) copy-start(f32[512,512,2]{1,0,2:T(8,128)} %copy-done.2) | copy-start | bytes 6291460
  100.0 12.7 %copy-start.12 = (bf16[512,256]{0,1:T(8,128)(2,1)S(1)}, bf16[512,256]{0,1:T(8,128)(2,1)}, u32[]{:S(2)}) copy-start(bf16[512,256]{0,1:T(8,128)(2,1)} %copy-done.11) | copy-start | bytes 786436
  112.6 13.9 %collective-permute-start.16 = (f32[512,256]{1,0:T(8,128)S(1)}, f32[512,256]{1,0:T(8,128)S(1)}, u32[]{:S(2)}, u32[]{:S(2)}) collective-permute-start(f32[512,256]{1,0:T(8,128)S(1)} %add.166), channel_id=1, source_target_pairs={{0,4},{4,8},{8,12},{12,16},{16,20},{20,24},{24,28},{28,32},{32,36}... | collective-permute-start | bytes 1572872 | tf_op jit(solution)/shard_map/ppermute | solution.py:13
  126.6 41.0 %collective-permute-start.21 = (bf16[512,256]{1,0:T(8,128)(2,1)S(1)}, bf16[512,256]{1,0:T(8,128)(2,1)S(1)}, u32[]{:S(2)}, u32[]{:S(2)}) collective-permute-start(bf16[512,256]{1,0:T(8,128)(2,1)S(1)} %add.170), channel_id=1, source_target_pairs={{0,244},{4,248},{8,252},{12,0},{16,4},{20,8},{24,12},{28,16},{32,2... | collective-permute-start | bytes 786440 | tf_op jit(solution)/shard_map/ppermute | solution.py:13
  (5 other events, 8.8 us)
Sparse Core Ops, SparseCore 0:
  100.1 30.7 reduce-scatter.2
  133.5 32.6 reduce-scatter.4
where the time goes:
time: 176 us; the launch traced here: 175 us
  waiting for transfers between devices  92.7 us (53%)
  starting transfers between devices  30.2 us (17%)
  matrix products  24 us (14%)
  between operations  14.6 us (8%)
  other arithmetic  7.2 us (4%)
  local copies, waits for them, and re-layouts  6.49 us (4%)
    ppermute x22, waiting for transfers between devices, from_behind(): return lax.ppermute(value, axis, pairs)  54.6 us
    reduce_scatter x1, waiting for transfers between devices, shards(): lax.psum_scatter(value_acc, 'head', scatter_dimension=0, tiled=True)  33.9 us
    ppermute x22, starting transfers between devices, from_behind(): return lax.ppermute(value, axis, pairs)  30.2 us
    dot_general x4, matrix products, shards(): jnp.einsum('htk,thd->kd', gradients_attention_low, grad_tile, preferred_e...  7.47 us
    dot_general x4, matrix products, shards(): jnp.einsum('thd,kd->htk', grad_tile, value_rows, preferred_element_type=j...  5.34 us
    dot_general x7, matrix products, masked_scores(): jnp.einsum('thd,kd->htk', query_tile, key_tile, preferred_element_type=jn...  4.36 us
    reduce_scatter x1, waiting for transfers between devices, shards(): lax.psum_scatter(key_acc, 'head', scatter_dimension=0, tiled=True)  4.13 us
    unnamed x30, local copies, waits for them, and re-layouts  4.01 us
  transfers between devices with their start and end apart: 24, of which 13 were waited for; matrix products, arithmetic and copies ran while one was open for 20% of the time, Pallas kernels for 0%

commit v1 on v0

v1 whole, which is shorter than its diff:
```python
import jax
import jax.numpy as jnp
from jax import lax
from jax.experimental import pallas as pl
from jax.experimental.pallas import tpu as pltpu
from jax.sharding import PartitionSpec as P

HD = 128
SPAN = 4
HEADS_CHIP = 4
NEG = -1e30
SCALE = 1.0 / HD**0.5
LOG2_SCALE = SCALE * 1.4426950408889634
F32 = jnp.float32
BF16 = jnp.bfloat16

NT = (((1,), (1,)), ((), ()))
NN = (((1,), (0,)), ((), ()))
TN = (((0,), (0,)), ((), ()))


def dot(a, b, dims):
    return lax.dot_general(a, b, dims, preferred_element_type=F32)


def call(body, outs, args, smem=0, flops=0, exps=0):
    specs = [pl.BlockSpec(memory_space=pltpu.SMEM)] * smem
    specs += [pl.BlockSpec(memory_space=pltpu.VMEM)] * (len(args) - smem)
    return pl.pallas_call(
        body,
        out_shape=outs,
        in_specs=specs,
        out_specs=[pl.BlockSpec(memory_space=pltpu.VMEM)] * len(outs),
        compiler_params=pltpu.CompilerParams(vmem_limit_bytes=40 * 1024 * 1024),
        cost_estimate=pl.CostEstimate(flops=flops, bytes_accessed=1 << 20, transcendentals=exps),
    )(*args)


def head_of(refs, head, first):
    ref = refs[head // 2]
    at = first + (head % 2) * HD
    return ref[:, at : at + HD]


def prepare(place, q_ref, g_ref, k_ref, v_ref, qg_ref, kv_ref):
    wide = q_ref.shape[1]
    qg_ref[:, :wide] = q_ref[...]
    qg_ref[:, wide:] = g_ref[...]
    core = place[1]
    for half in range(2):
        rows = pl.ds(pl.multiple_of(half * 256 + core * 128, 128), 128)
        kv_ref[half * 128 : (half + 1) * 128, :HD] = k_ref[rows, :]
        kv_ref[half * 128 : (half + 1) * 128, HD:] = v_ref[rows, :]


def scores_body(offset, place, pos_ref, kv_ref, qa_ref, qb_ref, *refs):
    prev_ref = refs[0] if offset else None
    p_ref, dp_ref, stats_ref = refs[-3:]
    rows = kv_ref.shape[0]
    toks = qa_ref.shape[0]
    key_row = place[2 + offset]
    query_row = place[0]
    columns = []
    for half in range(2):
        row = pos_ref[pl.ds(key_row + 2 * half, 1), :].astype(F32)
        columns.append(jnp.transpose(jnp.broadcast_to(row, (HD, HD))))
    key_pos = jnp.concatenate(columns, axis=0)
    biases = []
    for block in range(toks // HD):
        row = pos_ref[pl.ds(query_row + block, 1), :].astype(F32)
        biases.append(jnp.where(key_pos <= row, 0.0, NEG))
    bias = jnp.concatenate(biases, axis=1)
    keys = kv_ref[:, :HD]
    values = kv_ref[:, HD:]
    for head in range(HEADS_CHIP):
        cols = slice(head * toks, (head + 1) * toks)
        s = dot(keys, head_of((qa_ref, qb_ref), head, 0), NT) + bias
        dp = dot(values, head_of((qa_ref, qb_ref), head, 2 * HD), NT)
        top = jnp.max(s, axis=0, keepdims=True)
        if offset:
            before = prev_ref[0:1, cols]
            top = jnp.maximum(top, before)
        p = jnp.exp2((s - top) * LOG2_SCALE)
        total = jnp.sum(p, axis=0, keepdims=True)
        delta = jnp.sum(p * dp, axis=0, keepdims=True)
        if offset:
            fade = jnp.exp2((before - top) * LOG2_SCALE)
            total = total + prev_ref[1:2, cols] * fade
            delta = delta + prev_ref[2:3, cols] * fade
        p_ref[:, cols] = p
        dp_ref[:, cols] = dp
        stats_ref[0:1, cols] = top
        stats_ref[1:2, cols] = total
        stats_ref[2:3, cols] = delta


def grads_body(offset, first, last, *refs):
    p_ref, dp_ref, stats_ref, own_ref, mate_ref, kv_ref, qa_ref, qb_ref = refs[:8]
    refs = refs[8:]
    prev_ref = None
    if not first:
        prev_ref, refs = refs[0], refs[1:]
    dkv_ref, refs = refs[0], refs[1:]
    toks = qa_ref.shape[0]
    keys = kv_ref[:, :HD]
    dk = None
    for head in range(HEADS_CHIP):
        cols = slice(head * toks, (head + 1) * toks)
        other = (head + 2) % HEADS_CHIP
        across = slice(other * toks, (other + 1) * toks)
        top_own, top_mate = own_ref[0:1, cols], mate_ref[0:1, across]
        top = jnp.maximum(top_own, top_mate)
        fade_own = jnp.exp2((top_own - top) * LOG2_SCALE)
        fade_mate = jnp.exp2((top_mate - top) * LOG2_SCALE)
        total = own_ref[1:2, cols] * fade_own + mate_ref[1:2, across] * fade_mate
        delta = own_ref[2:3, cols] * fade_own + mate_ref[2:3, across] * fade_mate
        inverse = 1.0 / total
        delta = delta * inverse
        factor = jnp.exp2((stats_ref[0:1, cols] - top) * LOG2_SCALE) * inverse
        a = p_ref[:, cols] * factor
        ds = (a * (dp_ref[:, cols] - delta)).astype(BF16)
        dv_here = dot(a.astype(BF16), head_of((qa_ref, qb_ref), head, 2 * HD), NN)
        dk_here = dot(ds, head_of((qa_ref, qb_ref), head, 0), NN)
        dk = dk_here if dk is None else dk + dk_here
        dv = dv_here if head == 0 else dv + dv_here
        dq = dot(keys, ds, TN)
        if prev_ref is not None:
            dq = dq + prev_ref[head * HD : (head + 1) * HD, :]
        if last:
            out = refs[head // 2]
            at = (head % 2) * HD
            out[:, at : at + HD] = (jnp.transpose(dq) * SCALE).astype(out.dtype)
        else:
            refs[0][head * HD : (head + 1) * HD, :] = dq
    dkv_ref[:, :HD] = (dk * SCALE).astype(dkv_ref.dtype)
    dkv_ref[:, HD:] = dv.astype(dkv_ref.dtype)


def gather_body(place, own_ref, one_ref, two_ref, three_ref, mine_ref, theirs_ref):
    chip = place[6]

    def summed(half):
        rows = pl.ds(pl.multiple_of(half * 128, 128), 128)
        near = own_ref[rows, :] + one_ref[rows, :].astype(F32)
        return near + two_ref[rows, :].astype(F32) + three_ref[rows, :].astype(F32)

    mine_ref[...] = summed(chip)
    theirs_ref[...] = summed(1 - chip).astype(BF16)


def finish_body(mine_ref, got_ref, dq_own_ref, dq_got_ref, dq_ref, dk_ref, dv_ref):
    total = mine_ref[...] + got_ref[...].astype(F32)
    dk_ref[...] = total[:, :HD].astype(BF16)
    dv_ref[...] = total[:, HD:].astype(BF16)
    dq_ref[...] = (dq_own_ref[...] + dq_got_ref[...].astype(F32)).astype(BF16)


def shards(queries, key_rows, value_rows, grad_out, positions):
    toks, wide = queries.shape
    stripes = lax.axis_size("blk")
    heads = lax.axis_size("head")
    here = lax.axis_index("blk")
    head = lax.axis_index("head")
    core, chip = head % 2, head // 2
    step = toks // HD
    place = jnp.stack(
        [here * step, core]
        + [(here + k) % stripes * step + core for k in range(SPAN)]
        + [chip, core]
    ).astype(jnp.int32)
    pos = positions.reshape(-1, HD)

    def route(value, offset):
        flip = 2 if offset % 2 else 0
        pairs = [
            (s * heads + h, (s + offset) % stripes * heads + (h ^ flip))
            for s in range(stripes)
            for h in range(heads)
        ]
        return lax.ppermute(value, ("blk", "head"), pairs)

    def swap(value, bit):
        return lax.ppermute(value, "head", [(h, h ^ bit) for h in range(heads)])

    def vmem(shape, dtype):
        return pltpu.VMEM(shape, dtype)

    half = toks // 2
    lanes = HEADS_CHIP * toks
    qg, kv = call(
        prepare,
        [vmem((toks, 2 * wide), BF16), vmem((half, 2 * HD), BF16)],
        (place, queries, grad_out, key_rows, value_rows),
        smem=1,
    )
    qg_mate = swap(qg, 1)
    window = [kv] + [route(kv, -k) for k in range(1, SPAN)]
    kept = []
    stats = None
    flops = 2 * 2 * HD * half * lanes
    for k in range(SPAN):
        args = (place, pos, window[k], qg, qg_mate) + ((stats,) if k else ())
        p, dp, stats = call(
            lambda *refs, k=k: scores_body(k, *refs),
            [vmem((half, lanes), F32), vmem((half, lanes), F32), vmem((8, lanes), F32)],
            args,
            smem=1,
            flops=flops,
            exps=half * lanes,
        )
        kept.append((p, dp, stats))
    stats_mate = swap(stats, 1)
    sent = []
    dq = None
    for k in reversed(range(SPAN)):
        p, dp, own = kept[k]
        args = (p, dp, own, stats, stats_mate, window[k], qg, qg_mate)
        outs = [vmem((half, 2 * HD), BF16 if k else F32)]
        if k:
            outs += [vmem((HEADS_CHIP * HD, toks), F32)]
        else:
            outs += [vmem((toks, wide), F32), vmem((toks, wide), BF16)]
        got = call(
            lambda *refs, k=k: grads_body(k, k == SPAN - 1, k == 0, *refs),
            outs,
            args if dq is None else args + (dq,),
            flops=flops * 3 // 2,
        )
        dq = got[1]
        sent.append(route(got[0], k) if k else got[0])
    dq_own, dq_far = got[1:]
    dq_got = swap(dq_far, 1)
    mine, theirs = call(
        gather_body,
        [vmem((half // 2, 2 * HD), F32), vmem((half // 2, 2 * HD), BF16)],
        (place, sent[3], sent[2], sent[1], sent[0]),
        smem=1,
    )
    got = swap(theirs, 2)
    return tuple(
        call(
            finish_body,
            [
                jax.ShapeDtypeStruct((toks, wide), BF16),
                jax.ShapeDtypeStruct((half // 2, HD), BF16),
                jax.ShapeDtypeStruct((half // 2, HD), BF16),
            ],
            (mine, got, dq_own, dq_got),
        )
    )


def solution(mesh):
    return jax.shard_map(
        shards,
        mesh=mesh,
        in_specs=(P("blk", "head"), P("blk", None), P("blk", None), P("blk", "head"), P()),
        out_specs=(P("blk", "head"), P(("blk", "head"), None), P(("blk", "head"), None)),
        check_vma=False,
    )
```

time: 176 us -> 61.4 us (0.35)
  waiting for transfers between devices: 92.7 us -> 26.9 us
  matrix products: 24 us -> 0 us
  between operations: 14.6 us -> 0.79 us
  starting transfers between devices: 30.2 us -> 17 us
  Pallas kernels: 0 us -> 11.9 us
  other arithmetic: 7.2 us -> 0 us
  local copies, waits for them, and re-layouts: 6.49 us -> 4.7 us
    reduce_scatter x2 -> x0, waiting for transfers between devices: 38 us -> none  [the longest x1 33.9 us: shards(): lax.psum_scatter(value_acc, 'head', scatter_dimension=0, tiled=True)]
    ppermute x22 -> x10, waiting for transfers between devices: 54.6 us -> 26.9 us  [the longest x6 22.8 us: route(): return lax.ppermute(value, ('blk', 'head'), pairs)]
    dot_general x27 -> x0, matrix products: 24 us -> none  [the longest x4 7.47 us: shards(): jnp.einsum('htk,thd->kd', gradients_attention_low, grad_tile, preferred_e...]
    ppermute x22 -> x10, starting transfers between devices: 30.2 us -> 17 us  [the longest x6 12 us: route(): return lax.ppermute(value, ('blk', 'head'), pairs)]
    pallas_call x0 -> x11, Pallas kernels: none -> 11.9 us  [call(): pl.pallas_call(body, out_shape=outs, in_specs=specs, out_specs=[pl.BlockS...]
    convert_element_type x2 -> x0, other arithmetic: 2.91 us -> none  [the longest x1 1.46 us: shards(): key_sum.astype(jnp.bfloat16)]
    le x1 -> x0, other arithmetic: 1.83 us -> none  [masked_scores(): allowed = key_places[None, :] <= query_places[:, None]]
    unnamed x30 -> x10, local copies, waits for them, and re-layouts: 4.01 us -> 4.61 us
  transfers between devices with their start and end apart: 24 -> 10, of which waited for: 13 -> 6; matrix products, arithmetic and copies ran while one was open for 20% -> 0% of each run, Pallas kernels for 0% -> 8%
where the time goes in v1:
time: 61.4 us; the launch traced here: 61.2 us
  waiting for transfers between devices  26.9 us (44%)
  starting transfers between devices  17 us (28%)
  Pallas kernels  11.9 us (19%)
  local copies, waits for them, and re-layouts  4.7 us (8%)
  between operations  0.79 us (1%)
    ppermute x6, waiting for transfers between devices, route(): return lax.ppermute(value, ('blk', 'head'), pairs)  22.8 us
    ppermute x6, starting transfers between devices, route(): return lax.ppermute(value, ('blk', 'head'), pairs)  12 us
    pallas_call x11, Pallas kernels, call(): pl.pallas_call(body, out_shape=outs, in_specs=specs, out_specs=[pl.BlockS...  11.9 us
    ppermute x4, starting transfers between devices, swap(): return lax.ppermute(value, 'head', [(h, h ^ bit) for h in range(heads)])  4.96 us
    unnamed x10, local copies, waits for them, and re-layouts  4.61 us
    ppermute x4, waiting for transfers between devices, swap(): return lax.ppermute(value, 'head', [(h, h ^ bit) for h in range(heads)])  4.01 us
  transfers between devices with their start and end apart: 10, of which 6 were waited for; matrix products, arithmetic and copies ran while one was open for 0% of the time, Pallas kernels for 8%

profile of v1, /device:TPU:1, one launch (start us, length us, event | category | flops | bytes accessed | tf_op | source)
XLA Modules:
  0.0 61.2 jit_solution(12630245174397778582)
XLA Ops:
  0.7 0.1 stack.32.place.refs_0_
  0.8 1.0 %copy-done.1 = bf16[512,256]{1,0:T(8,128)(2,1)S(1)} copy-done((bf16[512,256]{1,0:T(8,128)(2,1)S(1)}, bf16[512,256]{1,0:T(8,128)(2,1)}, u32[]{:S(2)}) %copy-start.1) | copy-done | bytes 262168
  1.7 0.9 %copy-done.2 = bf16[512,256]{1,0:T(8,128)(2,1)S(1)} copy-done((bf16[512,256]{1,0:T(8,128)(2,1)S(1)}, bf16[512,256]{1,0:T(8,128)(2,1)}, u32[]{:S(2)}) %copy-start.2) | copy-done | bytes 262168
  2.7 0.9 %copy-done.3 = bf16[512,128]{1,0:T(8,128)(2,1)S(1)} copy-done((bf16[512,128]{1,0:T(8,128)(2,1)S(1)}, bf16[512,128]{1,0:T(8,128)(2,1)}, u32[]{:S(2)}) %copy-start.3) | copy-done | bytes 131096
  3.6 0.9 %copy-done.4 = bf16[512,128]{1,0:T(8,128)(2,1)S(1)} copy-done((bf16[512,128]{1,0:T(8,128)(2,1)S(1)}, bf16[512,128]{1,0:T(8,128)(2,1)}, u32[]{:S(2)}) %copy-start.4) | copy-done | bytes 131096
  4.5 0.6 shard_map.76
  5.1 3.3 %collective-permute-start = (bf16[512,512]{1,0:T(8,128)(2,1)S(1)}, bf16[512,512]{1,0:T(8,128)(2,1)S(1)}, u32[]{:S(2)}, u32[]{:S(2)}) collective-permute-start(bf16[512,512]{1,0:T(8,128)(2,1)S(1)} %get-tuple-element.29.refs_3_.refs_6_), channel_id=1, source_target_pairs={{0,1},{1,0},{2,3},{3,2},{4,5},{5,4},{6,7},{7,6},{8,9},{9,8},{10,11... | collective-permute-start | bytes 1572872 | tf_op jit(solution)/shard_map/ppermute | solution.py:183
  8.4 8.5 %collective-permute-start.3 = (bf16[256,256]{1,0:T(8,128)(2,1)S(1)}, bf16[256,256]{1,0:T(8,128)(2,1)S(1)}, u32[]{:S(2)}, u32[]{:S(2)}) collective-permute-start(bf16[256,256]{1,0:T(8,128)(2,1)S(1)} %get-tuple-element.28.refs_2_.refs_5_), channel_id=1, source_target_pairs={{0,254},{1,255},{2,252},{3,253},{4,2},{5,3},{6,0},{7,1},{8,6},{9,7... | collective-permute-start | bytes 393224 | tf_op jit(solution)/shard_map/ppermute | solution.py:180
  16.9 0.7 %collective-permute-start.2 = (bf16[256,256]{1,0:T(8,128)(2,1)S(1)}, bf16[256,256]{1,0:T(8,128)(2,1)S(1)}, u32[]{:S(2)}, u32[]{:S(2)}) collective-permute-start(bf16[256,256]{1,0:T(8,128)(2,1)S(1)} %get-tuple-element.28.refs_2_.refs_5_), channel_id=1, source_target_pairs={{0,248},{1,249},{2,250},{3,251},{4,252},{5,253},{6,254},{7,255},{8... | collective-permute-start | bytes 393224 | tf_op jit(solution)/shard_map/ppermute | solution.py:180
  17.6 0.4 collective-permute-start.1
  18.1 0.9 %copy-done = s32[32768]{0:T(1024)S(1)} copy-done((s32[32768]{0:T(1024)S(1)}, s32[32768]{0:T(1024)}, u32[]{:S(2)}) %copy-start) | copy-done | bytes 131096
  19.0 1.5 %shard_map.77 = (f32[256,2048]{1,0:T(8,128)S(1)}, f32[256,2048]{1,0:T(8,128)S(1)}, f32[8,2048]{1,0:T(8,128)S(1)}) custom-call(s32[8]{0:T(128)S(1)} %stack.32.place.refs_0_, s32[256,128]{1,0:T(8,128)S(1)} %bitcast.8, bf16[256,256]{1,0:T(8,128)(2,1)S(1)} %get-tuple-element.28.refs_2_.refs_5_, bf16[512,512]{1,0:T(8,128)(2,1)S(1)} %get-tuple-element.29.refs_3_.refs_6_, ...), custom_call_target="tpu_custom_call" | custom-call | flops 268435456 | bytes 1048576 | tf_op jit(solution)/shard_map/pallas_call | solution.py:29
  20.5 1.5 %shard_map.78 = (f32[256,2048]{1,0:T(8,128)S(1)}, f32[256,2048]{1,0:T(8,128)S(1)}, f32[8,2048]{1,0:T(8,128)S(1)}) custom-call(s32[8]{0:T(128)S(1)} %stack.32.place.refs_0_, s32[256,128]{1,0:T(8,128)S(1)} %bitcast.9, bf16[256,256]{1,0:T(8,128)(2,1)S(1)} %collective-permute-done.3.refs_2_.refs_5_, bf16[512,512]{1,0:T(8,128)(2,1)S(1)} %get-tuple-element.29.refs_3_.refs_6_, ...), custom_call_target="tpu_custom_call" | custom-call | flops 268435456 | bytes 1048576 | tf_op jit(solution)/shard_map/pallas_call | solution.py:29
  22.0 1.0 %collective-permute-done.2.refs_2_.refs_5_ = bf16[256,256]{1,0:T(8,128)(2,1)S(1)} collective-permute-done((bf16[256,256]{1,0:T(8,128)(2,1)S(1)}, bf16[256,256]{1,0:T(8,128)(2,1)S(1)}, u32[]{:S(2)}, u32[]{:S(2)}) %collective-permute-start.2) | collective-permute-done | bytes 131104 | tf_op jit(solution)/shard_map/ppermute | solution.py:180
  23.0 1.5 %shard_map.79 = (f32[256,2048]{1,0:T(8,128)S(1)}, f32[256,2048]{1,0:T(8,128)S(1)}, f32[8,2048]{1,0:T(8,128)S(1)}) custom-call(s32[8]{0:T(128)S(1)} %stack.32.place.refs_0_, s32[256,128]{1,0:T(8,128)S(1)} %bitcast.10, bf16[256,256]{1,0:T(8,128)(2,1)S(1)} %collective-permute-done.2.refs_2_.refs_5_, bf16[512,512]{1,0:T(8,128)(2,1)S(1)} %get-tuple-element.29.refs_3_.refs_6_, ...), custom_call_target="tpu_custom_call" | custom-call | flops 268435456 | bytes 1048576 | tf_op jit(solution)/shard_map/pallas_call | solution.py:29
  24.5 3.6 %collective-permute-done.1.refs_2_.refs_5_ = bf16[256,256]{1,0:T(8,128)(2,1)S(1)} collective-permute-done((bf16[256,256]{1,0:T(8,128)(2,1)S(1)}, bf16[256,256]{1,0:T(8,128)(2,1)S(1)}, u32[]{:S(2)}, u32[]{:S(2)}) %collective-permute-start.1) | collective-permute-done | bytes 131104 | tf_op jit(solution)/shard_map/ppermute | solution.py:180
  28.0 1.5 %shard_map.80 = (f32[256,2048]{1,0:T(8,128)S(1)}, f32[256,2048]{1,0:T(8,128)S(1)}, f32[8,2048]{1,0:T(8,128)S(1)}) custom-call(s32[8]{0:T(128)S(1)} %stack.32.place.refs_0_, s32[256,128]{1,0:T(8,128)S(1)} %bitcast.11, bf16[256,256]{1,0:T(8,128)(2,1)S(1)} %collective-permute-done.1.refs_2_.refs_5_, bf16[512,512]{1,0:T(8,128)(2,1)S(1)} %get-tuple-element.29.refs_3_.refs_6_, ...), custom_call_target="tpu_custom_call" | custom-call | flops 268435456 | bytes 1048576 | tf_op jit(solution)/shard_map/pallas_call | solution.py:29
  29.6 1.1 %collective-permute-start.4 = (f32[8,2048]{1,0:T(8,128)S(1)}, f32[8,2048]{1,0:T(8,128)S(1)}, u32[]{:S(2)}, u32[]{:S(2)}) collective-permute-start(f32[8,2048]{1,0:T(8,128)S(1)} %get-tuple-element.35.refs_2_.refs_3_), channel_id=1, source_target_pairs={{0,1},{1,0},{2,3},{3,2},{4,5},{5,4},{6,7},{7,6},{8,9},{9,8},{10,11... | collective-permute-start | bytes 196616 | tf_op jit(solution)/shard_map/ppermute | solution.py:183
  30.7 0.9 %collective-permute-done.4.refs_4_ = f32[8,2048]{1,0:T(8,128)S(1)} collective-permute-done((f32[8,2048]{1,0:T(8,128)S(1)}, f32[8,2048]{1,0:T(8,128)S(1)}, u32[]{:S(2)}, u32[]{:S(2)}) %collective-permute-start.4) | collective-permute-done | bytes 65568 | tf_op jit(solution)/shard_map/ppermute | solution.py:183
  31.6 1.0 %shard_map.81 = (bf16[256,256]{1,0:T(8,128)(2,1)S(1)}, f32[512,512]{1,0:T(8,128)S(1)}) custom-call(f32[256,2048]{1,0:T(8,128)S(1)} %get-tuple-element.40.refs_0_, f32[256,2048]{1,0:T(8,128)S(1)} %get-tuple-element.41.refs_1_, f32[8,2048]{1,0:T(8,128)S(1)} %get-tuple-element.35.refs_2_.refs_3_, f32[8,2048]{1,0:T(8,128)S(1)} %get-tuple-element.35.refs_2_.refs_3_, ...), custom_call_target="tpu_custom_call" | custom-call | flops 402653184 | bytes 1048576 | tf_op jit(solution)/shard_map/pallas_call | solution.py:29
  32.6 1.0 %shard_map.82 = (bf16[256,256]{1,0:T(8,128)(2,1)S(1)}, f32[512,512]{1,0:T(8,128)S(1)}) custom-call(f32[256,2048]{1,0:T(8,128)S(1)} %get-tuple-element.38.refs_0_, f32[256,2048]{1,0:T(8,128)S(1)} %get-tuple-element.39.refs_1_, f32[8,2048]{1,0:T(8,128)S(1)} %get-tuple-element.34.refs_5_.refs_2_, f32[8,2048]{1,0:T(8,128)S(1)} %get-tuple-element.35.refs_2_.refs_3_, ...), custom_call_target="tpu_custom_call" | custom-call | flops 402653184 | bytes 1048576 | tf_op jit(solution)/shard_map/pallas_call | solution.py:29
  33.6 0.9 %shard_map.83 = (bf16[256,256]{1,0:T(8,128)(2,1)S(1)}, f32[512,512]{1,0:T(8,128)S(1)}) custom-call(f32[256,2048]{1,0:T(8,128)S(1)} %get-tuple-element.36.refs_0_, f32[256,2048]{1,0:T(8,128)S(1)} %get-tuple-element.37.refs_1_, f32[8,2048]{1,0:T(8,128)S(1)} %get-tuple-element.33.refs_5_.refs_2_, f32[8,2048]{1,0:T(8,128)S(1)} %get-tuple-element.35.refs_2_.refs_3_, ...), custom_call_target="tpu_custom_call" | custom-call | flops 402653184 | bytes 1048576 | tf_op jit(solution)/shard_map/pallas_call | solution.py:29
  34.5 1.0 %shard_map.84 = (f32[256,256]{1,0:T(8,128)S(1)}, f32[512,256]{1,0:T(8,128)S(1)}, bf16[512,256]{1,0:T(8,128)(2,1)S(1)}) custom-call(f32[256,2048]{1,0:T(8,128)S(1)} %get-tuple-element.30.refs_0_, f32[256,2048]{1,0:T(8,128)S(1)} %get-tuple-element.31.refs_1_, f32[8,2048]{1,0:T(8,128)S(1)} %get-tuple-element.32.refs_5_.refs_2_, ...), custom_call_target="tpu_custom_call" | custom-call | flops 402653184 | bytes 1048576 | tf_op jit(solution)/shard_map/pallas_call | solution.py:29
  35.6 0.4 collective-permute-start.9
  36.0 0.0 collective-permute-start.6
  36.0 2.4 %collective-permute-start.7 = (bf16[256,256]{1,0:T(8,128)(2,1)S(1)}, bf16[256,256]{1,0:T(8,128)(2,1)S(1)}, u32[]{:S(2)}, u32[]{:S(2)}) collective-permute-start(bf16[256,256]{1,0:T(8,128)(2,1)S(1)} %get-tuple-element.48), channel_id=1, source_target_pairs={{0,14},{1,15},{2,12},{3,13},{4,18},{5,19},{6,16},{7,17},{8,22},{9,... | collective-permute-start | bytes 393224 | tf_op jit(solution)/shard_map/ppermute | solution.py:180
  38.4 7.9 %collective-permute-done.5.one_ref = bf16[256,256]{1,0:T(8,128)(2,1)S(1)} collective-permute-done((bf16[256,256]{1,0:T(8,128)(2,1)S(1)}, bf16[256,256]{1,0:T(8,128)(2,1)S(1)}, u32[]{:S(2)}, u32[]{:S(2)}) %collective-permute-start.5) | collective-permute-done | bytes 131104 | tf_op jit(solution)/shard_map/ppermute | solution.py:180
  46.3 10.4 %collective-permute-done.7.three_ref = bf16[256,256]{1,0:T(8,128)(2,1)S(1)} collective-permute-done((bf16[256,256]{1,0:T(8,128)(2,1)S(1)}, bf16[256,256]{1,0:T(8,128)(2,1)S(1)}, u32[]{:S(2)}, u32[]{:S(2)}) %collective-permute-start.7) | collective-permute-done | bytes 131104 | tf_op jit(solution)/shard_map/ppermute | solution.py:180
  56.6 0.6 shard_map.85
  57.3 0.1 collective-permute-start.8
  57.4 3.1 %collective-permute-done.8.got_ref = bf16[128,256]{1,0:T(8,128)(2,1)S(1)} collective-permute-done((bf16[128,256]{1,0:T(8,128)(2,1)S(1)}, bf16[128,256]{1,0:T(8,128)(2,1)S(1)}, u32[]{:S(2)}, u32[]{:S(2)}) %collective-permute-start.8) | collective-permute-done | bytes 65568 | tf_op jit(solution)/shard_map/ppermute | solution.py:183
  60.5 0.8 %shard_map.86 = (bf16[512,256]{1,0:T(8,128)(2,1)}, bf16[128,128]{1,0:T(8,128)(2,1)}, bf16[128,128]{1,0:T(8,128)(2,1)}) custom-call(f32[128,256]{1,0:T(8,128)S(1)} %get-tuple-element.49.mine_ref, bf16[128,256]{1,0:T(8,128)(2,1)S(1)} %collective-permute-done.8.got_ref, f32[512,256]{1,0:T(8,128)S(1)} %get-tuple-element.51.dq_own_ref, ...), custom_call_target="tpu_custom_call" | custom-call | bytes 1048576 | tf_op jit(solution)/shard_map/pallas_call | solution.py:29
  (10 shorter events, 0.0 us)
Async XLA Ops:
  0.8 1.0 %copy-start.1 = (bf16[512,256]{1,0:T(8,128)(2,1)S(1)}, bf16[512,256]{1,0:T(8,128)(2,1)}, u32[]{:S(2)}) copy-start(bf16[512,256]{1,0:T(8,128)(2,1)} %q_ref.1) | copy-start | bytes 786436
  1.7 0.9 %copy-start.2 = (bf16[512,256]{1,0:T(8,128)(2,1)S(1)}, bf16[512,256]{1,0:T(8,128)(2,1)}, u32[]{:S(2)}) copy-start(bf16[512,256]{1,0:T(8,128)(2,1)} %g_ref.1) | copy-start | bytes 786436
  2.7 0.9 %copy-start.3 = (bf16[512,128]{1,0:T(8,128)(2,1)S(1)}, bf16[512,128]{1,0:T(8,128)(2,1)}, u32[]{:S(2)}) copy-start(bf16[512,128]{1,0:T(8,128)(2,1)} %k_ref.1) | copy-start | bytes 393220
  3.6 0.9 %copy-start.4 = (bf16[512,128]{1,0:T(8,128)(2,1)S(1)}, bf16[512,128]{1,0:T(8,128)(2,1)}, u32[]{:S(2)}) copy-start(bf16[512,128]{1,0:T(8,128)(2,1)} %v_ref.1) | copy-start | bytes 393220
  5.1 13.0 %collective-permute-start = (bf16[512,512]{1,0:T(8,128)(2,1)S(1)}, bf16[512,512]{1,0:T(8,128)(2,1)S(1)}, u32[]{:S(2)}, u32[]{:S(2)}) collective-permute-start(bf16[512,512]{1,0:T(8,128)(2,1)S(1)} %get-tuple-element.29.refs_3_.refs_6_), channel_id=1, source_target_pairs={{0,1},{1,0},{2,3},{3,2},{4,5},{5,4},{6,7},{7,6},{8,9},{9,8},{10,11... | collective-permute-start | bytes 1572872 | tf_op jit(solution)/shard_map/ppermute | solution.py:183
  8.4 12.0 %collective-permute-start.3 = (bf16[256,256]{1,0:T(8,128)(2,1)S(1)}, bf16[256,256]{1,0:T(8,128)(2,1)S(1)}, u32[]{:S(2)}, u32[]{:S(2)}) collective-permute-start(bf16[256,256]{1,0:T(8,128)(2,1)S(1)} %get-tuple-element.28.refs_2_.refs_5_), channel_id=1, source_target_pairs={{0,254},{1,255},{2,252},{3,253},{4,2},{5,3},{6,0},{7,1},{8,6},{9,7... | collective-permute-start | bytes 393224 | tf_op jit(solution)/shard_map/ppermute | solution.py:180
  16.9 6.1 %collective-permute-start.2 = (bf16[256,256]{1,0:T(8,128)(2,1)S(1)}, bf16[256,256]{1,0:T(8,128)(2,1)S(1)}, u32[]{:S(2)}, u32[]{:S(2)}) collective-permute-start(bf16[256,256]{1,0:T(8,128)(2,1)S(1)} %get-tuple-element.28.refs_2_.refs_5_), channel_id=1, source_target_pairs={{0,248},{1,249},{2,250},{3,251},{4,252},{5,253},{6,254},{7,255},{8... | collective-permute-start | bytes 393224 | tf_op jit(solution)/shard_map/ppermute | solution.py:180
  17.6 10.4 %collective-permute-start.1 = (bf16[256,256]{1,0:T(8,128)(2,1)S(1)}, bf16[256,256]{1,0:T(8,128)(2,1)S(1)}, u32[]{:S(2)}, u32[]{:S(2)}) collective-permute-start(bf16[256,256]{1,0:T(8,128)(2,1)S(1)} %get-tuple-element.28.refs_2_.refs_5_), channel_id=1, source_target_pairs={{0,246},{1,247},{2,244},{3,245},{4,250},{5,251},{6,248},{7,249},{8... | collective-permute-start | bytes 393224 | tf_op jit(solution)/shard_map/ppermute | solution.py:180
  18.1 0.9 %copy-start = (s32[32768]{0:T(1024)S(1)}, s32[32768]{0:T(1024)}, u32[]{:S(2)}) copy-start(s32[32768]{0:T(1024)} %param.9) | copy-start | bytes 393220
  29.6 2.0 %collective-permute-start.4 = (f32[8,2048]{1,0:T(8,128)S(1)}, f32[8,2048]{1,0:T(8,128)S(1)}, u32[]{:S(2)}, u32[]{:S(2)}) collective-permute-start(f32[8,2048]{1,0:T(8,128)S(1)} %get-tuple-element.35.refs_2_.refs_3_), channel_id=1, source_target_pairs={{0,1},{1,0},{2,3},{3,2},{4,5},{5,4},{6,7},{7,6},{8,9},{9,8},{10,11... | collective-permute-start | bytes 196616 | tf_op jit(solution)/shard_map/ppermute | solution.py:183
  35.6 24.9 %collective-permute-start.9 = (bf16[512,256]{1,0:T(8,128)(2,1)S(1)}, bf16[512,256]{1,0:T(8,128)(2,1)S(1)}, u32[]{:S(2)}, u32[]{:S(2)}) collective-permute-start(bf16[512,256]{1,0:T(8,128)(2,1)S(1)} %get-tuple-element.52), channel_id=1, source_target_pairs={{0,1},{1,0},{2,3},{3,2},{4,5},{5,4},{6,7},{7,6},{8,9},{9,8},{10,11... | collective-permute-start | bytes 786440 | tf_op jit(solution)/shard_map/ppermute | solution.py:183
  36.0 10.3 %collective-permute-start.5 = (bf16[256,256]{1,0:T(8,128)(2,1)S(1)}, bf16[256,256]{1,0:T(8,128)(2,1)S(1)}, u32[]{:S(2)}, u32[]{:S(2)}) collective-permute-start(bf16[256,256]{1,0:T(8,128)(2,1)S(1)} %get-tuple-element.46), channel_id=1, source_target_pairs={{0,6},{1,7},{2,4},{3,5},{4,10},{5,11},{6,8},{7,9},{8,14},{9,15},{1... | collective-permute-start | bytes 393224 | tf_op jit(solution)/shard_map/ppermute | solution.py:180
  36.0 10.3 %collective-permute-start.6 = (bf16[256,256]{1,0:T(8,128)(2,1)S(1)}, bf16[256,256]{1,0:T(8,128)(2,1)S(1)}, u32[]{:S(2)}, u32[]{:S(2)}) collective-permute-start(bf16[256,256]{1,0:T(8,128)(2,1)S(1)} %get-tuple-element.47), channel_id=1, source_target_pairs={{0,8},{1,9},{2,10},{3,11},{4,12},{5,13},{6,14},{7,15},{8,16},{9,17... | collective-permute-start | bytes 393224 | tf_op jit(solution)/shard_map/ppermute | solution.py:180
  36.0 20.6 %collective-permute-start.7 = (bf16[256,256]{1,0:T(8,128)(2,1)S(1)}, bf16[256,256]{1,0:T(8,128)(2,1)S(1)}, u32[]{:S(2)}, u32[]{:S(2)}) collective-permute-start(bf16[256,256]{1,0:T(8,128)(2,1)S(1)} %get-tuple-element.48), channel_id=1, source_target_pairs={{0,14},{1,15},{2,12},{3,13},{4,18},{5,19},{6,16},{7,17},{8,22},{9,... | collective-permute-start | bytes 393224 | tf_op jit(solution)/shard_map/ppermute | solution.py:180
  57.3 3.2 %collective-permute-start.8 = (bf16[128,256]{1,0:T(8,128)(2,1)S(1)}, bf16[128,256]{1,0:T(8,128)(2,1)S(1)}, u32[]{:S(2)}, u32[]{:S(2)}) collective-permute-start(bf16[128,256]{1,0:T(8,128)(2,1)S(1)} %get-tuple-element.50), channel_id=1, source_target_pairs={{0,2},{1,3},{2,0},{3,1},{4,6},{5,7},{6,4},{7,5},{8,10},{9,11},{10,... | collective-permute-start | bytes 196616 | tf_op jit(solution)/shard_map/ppermute | solution.py:183

commit v2 on v1

v2 whole, which is shorter than its diff:
```python
import jax
import jax.numpy as jnp
from jax import lax
from jax.experimental import pallas as pl
from jax.experimental.pallas import tpu as pltpu
from jax.sharding import PartitionSpec as P

HD = 128
SPAN = 4
HEADS_CHIP = 4
NEG = -1e30
SCALE = 1.0 / HD**0.5
LOG2_SCALE = SCALE * 1.4426950408889634
F32 = jnp.float32
BF16 = jnp.bfloat16

NT = (((1,), (1,)), ((), ()))
NN = (((1,), (0,)), ((), ()))
TN = (((0,), (0,)), ((), ()))


def dot(a, b, dims):
    return lax.dot_general(a, b, dims, preferred_element_type=F32)


def call(body, outs, args, flops=0, exps=0):
    whole = pl.BlockSpec(memory_space=pltpu.VMEM)
    return pl.pallas_call(
        body,
        out_shape=outs,
        in_specs=[whole] * len(args),
        out_specs=[whole] * len(outs),
        compiler_params=pltpu.CompilerParams(vmem_limit_bytes=16 * 1024 * 1024),
        cost_estimate=pl.CostEstimate(flops=flops, bytes_accessed=1 << 20, transcendentals=exps),
    )(*args)


def head_of(refs, head, first):
    ref = refs[head // 2]
    at = first + (head % 2) * HD
    return ref[:, at : at + HD]


def prepare(q_hbm, g_hbm, k_hbm, v_hbm, pos_hbm, qg_ref, kv_ref, pos_ref, sems):
    wide = q_hbm.shape[1]
    core = lax.axis_index("head") % 2
    block = lax.axis_index("blk") * (q_hbm.shape[0] // HD) // 8
    blocks = pos_hbm.shape[0] // 8
    copies = []
    for half in range(2):
        source = pl.ds(pl.multiple_of(half * 256 + core * 128, 128), 128)
        target = pl.ds(half * 128, 128)
        copies.append((k_hbm.at[source, :], kv_ref.at[target, pl.ds(0, HD)]))
        copies.append((v_hbm.at[source, :], kv_ref.at[target, pl.ds(HD, HD)]))
    copies.append((q_hbm, qg_ref.at[:, pl.ds(0, wide)]))
    copies.append((g_hbm, qg_ref.at[:, pl.ds(wide, wide)]))
    for i in range(3):
        row = pl.multiple_of((block + i) % blocks * 8, 8)
        copies.append((pos_hbm.at[pl.ds(row, 8), :], pos_ref.at[pl.ds(i * 8, 8), :]))
    copies = [
        pltpu.make_async_copy(source, target, sems.at[i])
        for i, (source, target) in enumerate(copies)
    ]
    for copy in copies:
        copy.start()
    for copy in copies:
        copy.wait()


def mask_body(pos_ref, bias_ref, flag_ref):
    core = lax.axis_index("head") % 2
    chip = lax.axis_index("head") // 2
    toks = bias_ref.shape[1]
    query_row = lax.axis_index("blk") * (toks // HD) % 8
    queries = [
        pos_ref[pl.ds(query_row + i, 1), :].astype(F32) for i in range(toks // HD)
    ]
    for k in range(SPAN):
        for half in range(2):
            row = pos_ref[pl.ds(query_row + k * (toks // HD) + 2 * half + core, 1), :]
            keys = jnp.transpose(jnp.broadcast_to(row.astype(F32), (HD, HD)))
            rows = slice((2 * k + half) * HD, (2 * k + half + 1) * HD)
            for i, query in enumerate(queries):
                bias_ref[rows, i * HD : (i + 1) * HD] = jnp.where(keys <= query, 0.0, NEG)
    flag_ref[...] = jnp.full(flag_ref.shape, chip, F32)


def scores_body(offset, bias_ref, kv_ref, qa_ref, qb_ref, *refs):
    prev_ref = refs[0] if len(refs) == 4 else None
    p_ref, dp_ref, stats_ref = refs[-3:]
    rows = kv_ref.shape[0]
    toks = qa_ref.shape[0]
    bias = bias_ref[offset * rows : (offset + 1) * rows, :]
    keys = kv_ref[:, :HD]
    values = kv_ref[:, HD:]
    for head in range(HEADS_CHIP):
        cols = slice(head * toks, (head + 1) * toks)
        s = dot(keys, head_of((qa_ref, qb_ref), head, 0), NT) + bias
        dp = dot(values, head_of((qa_ref, qb_ref), head, 2 * HD), NT)
        top = jnp.max(s, axis=0, keepdims=True)
        if prev_ref is not None:
            before = prev_ref[0:1, cols]
            top = jnp.maximum(top, before)
        p = jnp.exp2((s - top) * LOG2_SCALE)
        total = jnp.sum(p, axis=0, keepdims=True)
        delta = jnp.sum(p * dp, axis=0, keepdims=True)
        if prev_ref is not None:
            fade = jnp.exp2((before - top) * LOG2_SCALE)
            total = total + prev_ref[1:2, cols] * fade
            delta = delta + prev_ref[2:3, cols] * fade
        p_ref[:, cols] = p
        dp_ref[:, cols] = dp
        stats_ref[0:1, cols] = top
        stats_ref[1:2, cols] = total
        stats_ref[2:3, cols] = delta


def grads_body(flip, flag_ref, p_ref, dp_ref, stats_ref, own_ref, mate_ref, qa_ref, qb_ref, *outs):
    ds_ref, keep_ref, give_ref = outs
    toks = qa_ref.shape[0]
    for head in range(HEADS_CHIP):
        cols = slice(head * toks, (head + 1) * toks)
        other = (head + 2) % HEADS_CHIP
        across = slice(other * toks, (other + 1) * toks)
        top_own, top_mate = own_ref[0:1, cols], mate_ref[0:1, across]
        top = jnp.maximum(top_own, top_mate)
        fade_own = jnp.exp2((top_own - top) * LOG2_SCALE)
        fade_mate = jnp.exp2((top_mate - top) * LOG2_SCALE)
        total = own_ref[1:2, cols] * fade_own + mate_ref[1:2, across] * fade_mate
        delta = own_ref[2:3, cols] * fade_own + mate_ref[2:3, across] * fade_mate
        inverse = 1.0 / total
        delta = delta * inverse
        factor = jnp.exp2((stats_ref[0:1, cols] - top) * LOG2_SCALE) * inverse
        a = p_ref[:, cols] * factor
        ds = (a * (dp_ref[:, cols] - delta)).astype(BF16)
        ds_ref[:, cols] = ds
        dv_here = dot(a.astype(BF16), head_of((qa_ref, qb_ref), head, 2 * HD), NN)
        dk_here = dot(ds, head_of((qa_ref, qb_ref), head, 0), NN)
        dk = dk_here if head == 0 else dk + dk_here
        dv = dv_here if head == 0 else dv + dv_here
    both = jnp.concatenate([dk * SCALE, dv], axis=1)
    half = both.shape[0] // 2
    first, second = (both[half:], both[:half]) if flip else (both[:half], both[half:])
    upper = flag_ref[0:1, :] > 0
    upper = jnp.concatenate([upper, upper], axis=1)
    keep_ref[...] = jnp.where(upper, second, first)
    give_ref[...] = jnp.where(upper, first, second).astype(BF16)


def query_body(heads, ds_refs, kv_refs, out_ref):
    toks = out_ref.shape[0]
    for i, head in enumerate(heads):
        dq = None
        for ds_ref, kv_ref in zip(ds_refs, kv_refs):
            here = dot(kv_ref[:, :HD], ds_ref[:, head * toks : (head + 1) * toks], TN)
            dq = here if dq is None else dq + here
        out_ref[:, i * HD : (i + 1) * HD] = (jnp.transpose(dq) * SCALE).astype(out_ref.dtype)


def finish_body(mine_ref, got_ref, one_ref, two_ref, three_ref, dk_ref, dv_ref):
    total = mine_ref[...] + got_ref[...].astype(F32) + one_ref[...].astype(F32)
    total = total + two_ref[...].astype(F32) + three_ref[...].astype(F32)
    dk_ref[...] = total[:, :HD].astype(BF16)
    dv_ref[...] = total[:, HD:].astype(BF16)


def query_sum_body(own_ref, got_ref, dq_ref):
    dq_ref[...] = (own_ref[...] + got_ref[...].astype(F32)).astype(BF16)


def shards(queries, key_rows, value_rows, grad_out, positions):
    toks, wide = queries.shape
    stripes = lax.axis_size("blk")
    heads = lax.axis_size("head")
    pos = positions.reshape(-1, HD)

    def route(value, offset):
        flip = 2 if offset % 2 else 0
        pairs = [
            (s * heads + h, (s + offset) % stripes * heads + (h ^ flip))
            for s in range(stripes)
            for h in range(heads)
        ]
        return lax.ppermute(value, ("blk", "head"), pairs)

    def swap(value, bit):
        return lax.ppermute(value, "head", [(h, h ^ bit) for h in range(heads)])

    def vmem(shape, dtype):
        return pltpu.VMEM(shape, dtype)

    half = toks // 2
    lanes = HEADS_CHIP * toks
    hbm = pl.BlockSpec(memory_space=pltpu.HBM)
    whole = pl.BlockSpec(memory_space=pltpu.VMEM)
    qg, kv, pos = pl.pallas_call(
        prepare,
        out_shape=[
            vmem((toks, 2 * wide), BF16),
            vmem((half, 2 * HD), BF16),
            vmem((24, HD), jnp.int32),
        ],
        in_specs=[hbm] * 5,
        out_specs=[whole] * 3,
        scratch_shapes=[pltpu.SemaphoreType.DMA((9,))],
        compiler_params=pltpu.CompilerParams(vmem_limit_bytes=16 * 1024 * 1024),
    )(*(pltpu.with_memory_space_constraint(v, pltpu.HBM) for v in (queries, grad_out, key_rows, value_rows, pos)))
    qg_mate = swap(qg, 1)
    bias, flag = call(mask_body, [vmem((SPAN * half, toks), F32), vmem((8, HD), F32)], (pos,))
    window = {0: kv}
    for k in (2, 1, 3):
        window[k] = route(kv, -k)
    kept = {}
    stats = None
    flops = 2 * 2 * HD * half * lanes
    for k in (0, 2, 1, 3):
        args = (bias, window[k], qg, qg_mate) + (() if stats is None else (stats,))
        p, dp, stats = call(
            lambda *refs, k=k: scores_body(k, *refs),
            [vmem((half, lanes), F32), vmem((half, lanes), F32), vmem((8, lanes), F32)],
            args,
            flops=flops,
            exps=half * lanes,
        )
        kept[k] = (p, dp, stats)
    stats_mate = swap(stats, 1)
    grads = {}
    for k in (3, 2, 1, 0):
        p, dp, own = kept[k]

        grads[k] = call(
            lambda *refs, k=k: grads_body(k % 2, *refs),
            [
                vmem((half, lanes), BF16),
                vmem((half // 2, 2 * HD), F32),
                vmem((half // 2, 2 * HD), BF16),
            ],
            (flag, p, dp, own, stats, stats_mate, qg, qg_mate),
            flops=flops,
        )
    pushed = {}
    for k in (3, 2, 1, 0):
        _, keep, give = grads[k]
        got = swap(give, 2)
        pushed[k] = (keep, got)
        if k:
            pushed[k] = route((keep + got.astype(F32)).astype(BF16), k)

    def query_part(heads, kind):
        def body(*refs):
            query_body(heads, refs[:SPAN], refs[SPAN : 2 * SPAN], refs[2 * SPAN])

        args = [grads[k][0] for k in range(SPAN)] + [window[k] for k in range(SPAN)]
        return call(body, [vmem((toks, wide), kind)], args, flops=flops)[0]

    dq_got = swap(query_part((2, 3), BF16), 1)
    dq_own = query_part((0, 1), F32)
    [dq] = call(query_sum_body, [jax.ShapeDtypeStruct((toks, wide), BF16)], (dq_own, dq_got))
    dk, dv = call(
        finish_body,
        [jax.ShapeDtypeStruct((half // 2, HD), BF16)] * 2,
        (*pushed[0], pushed[1], pushed[2], pushed[3]),
    )
    return dq, dk, dv


def solution(mesh):
    return jax.shard_map(
        shards,
        mesh=mesh,
        in_specs=(P("blk", "head"), P("blk", None), P("blk", None), P("blk", "head"), P()),
        out_specs=(P("blk", "head"), P(("blk", "head"), None), P(("blk", "head"), None)),
        check_vma=False,
    )
```

time: 61.4 us -> 51.6 us (0.84)
  waiting for transfers between devices: 26.9 us -> 15.8 us
  starting transfers between devices: 17 us -> 24 us
  local copies, waits for them, and re-layouts: 4.7 us -> 0 us
  Pallas kernels: 11.9 us -> 10.9 us
    ppermute x6, waiting for transfers between devices: 22.8 us -> 14.9 us  [route(): return lax.ppermute(value, ('blk', 'head'), pairs)]
    ppermute x4 -> x7, starting transfers between devices: 4.96 us -> 10.5 us  [swap(): return lax.ppermute(value, 'head', [(h, h ^ bit) for h in range(heads)])]
    unnamed x10 -> x0, local copies, waits for them, and re-layouts: 4.61 us -> none
    ppermute x4 -> x7, waiting for transfers between devices: 4.01 us -> 0.92 us  [swap(): return lax.ppermute(value, 'head', [(h, h ^ bit) for h in range(heads)])]
    ppermute x6, starting transfers between devices: 12 us -> 13.5 us  [route(): return lax.ppermute(value, ('blk', 'head'), pairs)]
    pallas_call x11 -> x14, Pallas kernels: 11.9 us -> 10.9 us  [the longest x13 9.68 us: call(): pl.pallas_call(body, out_shape=outs, in_specs=[whole] * len(args), out_sp...]
  transfers between devices with their start and end apart: 10 -> 13, of which waited for: 6 -> 6; matrix products, arithmetic and copies ran while one was open for 0% -> 0% of each run, Pallas kernels for 8% -> 14%
where the time goes in v2:
time: 51.6 us; the launch traced here: 51.5 us
  starting transfers between devices  24 us (47%)
  waiting for transfers between devices  15.8 us (31%)
  Pallas kernels  10.9 us (21%)
  between operations  0.77 us (1%)
    ppermute x6, waiting for transfers between devices, route(): return lax.ppermute(value, ('blk', 'head'), pairs)  14.9 us
    ppermute x6, starting transfers between devices, route(): return lax.ppermute(value, ('blk', 'head'), pairs)  13.5 us
    ppermute x7, starting transfers between devices, swap(): return lax.ppermute(value, 'head', [(h, h ^ bit) for h in range(heads)])  10.5 us
    pallas_call x13, Pallas kernels, call(): pl.pallas_call(body, out_shape=outs, in_specs=[whole] * len(args), out_sp...  9.68 us
    pallas_call x1, Pallas kernels, shards(): pl.pallas_call(prepare, out_shape=[vmem((toks, 2 * wide), BF16), vmem((ha...  1.21 us
  transfers between devices with their start and end apart: 13, of which 6 were waited for; matrix products, arithmetic and copies ran while one was open for 0% of the time, Pallas kernels for 14%

profile of v2, /device:TPU:1, one launch (start us, length us, event | category | flops | bytes accessed | tf_op | source)
XLA Modules:
  0.0 51.5 jit_solution(17438350864619773105)
XLA Ops:
  0.6 1.2 %shard_map.76 = (bf16[512,512]{1,0:T(8,128)(2,1)S(1)}, bf16[256,256]{1,0:T(8,128)(2,1)S(1)}, s32[24,128]{1,0:T(8,128)S(1)}) custom-call(bf16[512,256]{1,0:T(8,128)(2,1)} %q_hbm.1, bf16[512,256]{1,0:T(8,128)(2,1)} %g_hbm.1, bf16[512,128]{1,0:T(8,128)(2,1)} %k_hbm.1, bf16[512,128]{1,0:T(8,128)(2,1)} %v_hbm.1, s32[256,128]{1,0:T(8,128)} %bitcast.1), custom_call_target="tpu_custom_call" | custom-call | tf_op jit(solution)/shard_map/pallas_call | solution.py:196
  1.8 3.3 %collective-permute-start = (bf16[512,512]{1,0:T(8,128)(2,1)S(1)}, bf16[512,512]{1,0:T(8,128)(2,1)S(1)}, u32[]{:S(2)}, u32[]{:S(2)}) collective-permute-start(bf16[512,512]{1,0:T(8,128)(2,1)S(1)} %get-tuple-element.38.refs_2_.refs_6_), channel_id=1, source_target_pairs={{0,1},{1,0},{2,3},{3,2},{4,5},{5,4},{6,7},{7,6},{8,9},{9,8},{10,11... | collective-permute-start | bytes 1572872 | tf_op jit(solution)/shard_map/ppermute | solution.py:187
  5.2 6.0 %collective-permute-start.3 = (bf16[256,256]{1,0:T(8,128)(2,1)S(1)}, bf16[256,256]{1,0:T(8,128)(2,1)S(1)}, u32[]{:S(2)}, u32[]{:S(2)}) collective-permute-start(bf16[256,256]{1,0:T(8,128)(2,1)S(1)} %get-tuple-element.37.refs_1_.refs_4_), channel_id=1, source_target_pairs={{0,248},{1,249},{2,250},{3,251},{4,252},{5,253},{6,254},{7,255},{8... | collective-permute-start | bytes 393224 | tf_op jit(solution)/shard_map/ppermute | solution.py:184
  11.2 3.2 %collective-permute-start.2 = (bf16[256,256]{1,0:T(8,128)(2,1)S(1)}, bf16[256,256]{1,0:T(8,128)(2,1)S(1)}, u32[]{:S(2)}, u32[]{:S(2)}) collective-permute-start(bf16[256,256]{1,0:T(8,128)(2,1)S(1)} %get-tuple-element.37.refs_1_.refs_4_), channel_id=1, source_target_pairs={{0,254},{1,255},{2,252},{3,253},{4,2},{5,3},{6,0},{7,1},{8,6},{9,7... | collective-permute-start | bytes 393224 | tf_op jit(solution)/shard_map/ppermute | solution.py:184
  14.4 0.4 collective-permute-start.1
  14.8 0.2 shard_map.77
  15.1 0.9 %shard_map.78 = (f32[256,2048]{1,0:T(8,128)S(1)}, f32[256,2048]{1,0:T(8,128)S(1)}, f32[8,2048]{1,0:T(8,128)S(1)}) custom-call(f32[1024,512]{1,0:T(8,128)S(1)} %get-tuple-element.36.refs_0_, bf16[256,256]{1,0:T(8,128)(2,1)S(1)} %get-tuple-element.37.refs_1_.refs_4_, bf16[512,512]{1,0:T(8,128)(2,1)S(1)} %get-tuple-element.38.refs_2_.refs_6_, ...), custom_call_target="tpu_custom_call" | custom-call | flops 268435456 | bytes 1048576 | tf_op jit(solution)/shard_map/pallas_call | solution.py:28
  16.0 0.9 %shard_map.79 = (f32[256,2048]{1,0:T(8,128)S(1)}, f32[256,2048]{1,0:T(8,128)S(1)}, f32[8,2048]{1,0:T(8,128)S(1)}) custom-call(f32[1024,512]{1,0:T(8,128)S(1)} %get-tuple-element.36.refs_0_, bf16[256,256]{1,0:T(8,128)(2,1)S(1)} %collective-permute-done.3.refs_1_.refs_6_, bf16[512,512]{1,0:T(8,128)(2,1)S(1)} %get-tuple-element.38.refs_2_.refs_6_, ...), custom_call_target="tpu_custom_call" | custom-call | flops 268435456 | bytes 1048576 | tf_op jit(solution)/shard_map/pallas_call | solution.py:28
  16.9 0.4 collective-permute-done.2.refs_1_.refs_5_
  17.3 0.9 %shard_map.80 = (f32[256,2048]{1,0:T(8,128)S(1)}, f32[256,2048]{1,0:T(8,128)S(1)}, f32[8,2048]{1,0:T(8,128)S(1)}) custom-call(f32[1024,512]{1,0:T(8,128)S(1)} %get-tuple-element.36.refs_0_, bf16[256,256]{1,0:T(8,128)(2,1)S(1)} %collective-permute-done.2.refs_1_.refs_5_, bf16[512,512]{1,0:T(8,128)(2,1)S(1)} %get-tuple-element.38.refs_2_.refs_6_, ...), custom_call_target="tpu_custom_call" | custom-call | flops 268435456 | bytes 1048576 | tf_op jit(solution)/shard_map/pallas_call | solution.py:28
  18.2 2.7 %collective-permute-done.1.refs_1_.refs_7_ = bf16[256,256]{1,0:T(8,128)(2,1)S(1)} collective-permute-done((bf16[256,256]{1,0:T(8,128)(2,1)S(1)}, bf16[256,256]{1,0:T(8,128)(2,1)S(1)}, u32[]{:S(2)}, u32[]{:S(2)}) %collective-permute-start.1) | collective-permute-done | bytes 131104 | tf_op jit(solution)/shard_map/ppermute | solution.py:184
  20.9 0.9 %shard_map.81 = (f32[256,2048]{1,0:T(8,128)S(1)}, f32[256,2048]{1,0:T(8,128)S(1)}, f32[8,2048]{1,0:T(8,128)S(1)}) custom-call(f32[1024,512]{1,0:T(8,128)S(1)} %get-tuple-element.36.refs_0_, bf16[256,256]{1,0:T(8,128)(2,1)S(1)} %collective-permute-done.1.refs_1_.refs_7_, bf16[512,512]{1,0:T(8,128)(2,1)S(1)} %get-tuple-element.38.refs_2_.refs_6_, ...), custom_call_target="tpu_custom_call" | custom-call | flops 268435456 | bytes 1048576 | tf_op jit(solution)/shard_map/pallas_call | solution.py:28
  21.9 1.6 %collective-permute-start.4 = (f32[8,2048]{1,0:T(8,128)S(1)}, f32[8,2048]{1,0:T(8,128)S(1)}, u32[]{:S(2)}, u32[]{:S(2)}) collective-permute-start(f32[8,2048]{1,0:T(8,128)S(1)} %get-tuple-element.44.refs_4_.refs_3_), channel_id=1, source_target_pairs={{0,1},{1,0},{2,3},{3,2},{4,5},{5,4},{6,7},{7,6},{8,9},{9,8},{10,11... | collective-permute-start | bytes 196616 | tf_op jit(solution)/shard_map/ppermute | solution.py:187
  23.5 0.9 %collective-permute-done.4.refs_5_ = f32[8,2048]{1,0:T(8,128)S(1)} collective-permute-done((f32[8,2048]{1,0:T(8,128)S(1)}, f32[8,2048]{1,0:T(8,128)S(1)}, u32[]{:S(2)}, u32[]{:S(2)}) %collective-permute-start.4) | collective-permute-done | bytes 65568 | tf_op jit(solution)/shard_map/ppermute | solution.py:187
  24.4 0.8 %shard_map.84 = (bf16[256,2048]{1,0:T(8,128)(2,1)S(1)}, f32[128,256]{1,0:T(8,128)S(1)}, bf16[128,256]{1,0:T(8,128)(2,1)S(1)}) custom-call(f32[8,128]{1,0:T(8,128)S(1)} %get-tuple-element.35.refs_0_, f32[256,2048]{1,0:T(8,128)S(1)} %get-tuple-element.49.refs_1_, f32[256,2048]{1,0:T(8,128)S(1)} %get-tuple-element.50.refs_2_, ...), custom_call_target="tpu_custom_call" | custom-call | flops 268435456 | bytes 1048576 | tf_op jit(solution)/shard_map/pallas_call | solution.py:28
  25.2 2.4 %collective-permute-start.9 = (bf16[128,256]{1,0:T(8,128)(2,1)S(1)}, bf16[128,256]{1,0:T(8,128)(2,1)S(1)}, u32[]{:S(2)}, u32[]{:S(2)}) collective-permute-start(bf16[128,256]{1,0:T(8,128)(2,1)S(1)} %get-tuple-element.60), channel_id=1, source_target_pairs={{0,2},{1,3},{2,0},{3,1},{4,6},{5,7},{6,4},{7,5},{8,10},{9,11},{10,... | collective-permute-start | bytes 196616 | tf_op jit(solution)/shard_map/ppermute | solution.py:187
  27.6 0.8 %shard_map.83 = (bf16[256,2048]{1,0:T(8,128)(2,1)S(1)}, f32[128,256]{1,0:T(8,128)S(1)}, bf16[128,256]{1,0:T(8,128)(2,1)S(1)}) custom-call(f32[8,128]{1,0:T(8,128)S(1)} %get-tuple-element.35.refs_0_, f32[256,2048]{1,0:T(8,128)S(1)} %get-tuple-element.46.refs_1_, f32[256,2048]{1,0:T(8,128)S(1)} %get-tuple-element.47.refs_2_, ...), custom_call_target="tpu_custom_call" | custom-call | flops 268435456 | bytes 1048576 | tf_op jit(solution)/shard_map/pallas_call | solution.py:28
  28.4 0.1 collective-permute-start.7
  28.5 0.8 %shard_map.82 = (bf16[256,2048]{1,0:T(8,128)(2,1)S(1)}, f32[128,256]{1,0:T(8,128)S(1)}, bf16[128,256]{1,0:T(8,128)(2,1)S(1)}) custom-call(f32[8,128]{1,0:T(8,128)S(1)} %get-tuple-element.35.refs_0_, f32[256,2048]{1,0:T(8,128)S(1)} %get-tuple-element.39.refs_1_, f32[256,2048]{1,0:T(8,128)S(1)} %get-tuple-element.40.refs_2_, ...), custom_call_target="tpu_custom_call" | custom-call | flops 268435456 | bytes 1048576 | tf_op jit(solution)/shard_map/pallas_call | solution.py:28
  29.3 1.7 %collective-permute-start.6 = (bf16[128,256]{1,0:T(8,128)(2,1)S(1)}, bf16[128,256]{1,0:T(8,128)(2,1)S(1)}, u32[]{:S(2)}, u32[]{:S(2)}) collective-permute-start(bf16[128,256]{1,0:T(8,128)(2,1)S(1)} %get-tuple-element.56), channel_id=1, source_target_pairs={{0,2},{1,3},{2,0},{3,1},{4,6},{5,7},{6,4},{7,5},{8,10},{9,11},{10,... | collective-permute-start | bytes 196616 | tf_op jit(solution)/shard_map/ppermute | solution.py:187
  31.0 0.8 %shard_map.85 = (bf16[256,2048]{1,0:T(8,128)(2,1)S(1)}, f32[128,256]{1,0:T(8,128)S(1)}, bf16[128,256]{1,0:T(8,128)(2,1)S(1)}) custom-call(f32[8,128]{1,0:T(8,128)S(1)} %get-tuple-element.35.refs_0_, f32[256,2048]{1,0:T(8,128)S(1)} %get-tuple-element.52.refs_1_, f32[256,2048]{1,0:T(8,128)S(1)} %get-tuple-element.53.refs_2_, ...), custom_call_target="tpu_custom_call" | custom-call | flops 268435456 | bytes 1048576 | tf_op jit(solution)/shard_map/pallas_call | solution.py:28
  31.8 0.1 collective-permute-start.11
  31.9 0.6 %shard_map.87 = bf16[512,256]{1,0:T(8,128)(2,1)S(1)} custom-call(bf16[256,2048]{1,0:T(8,128)(2,1)S(1)} %get-tuple-element.45.refs_0_, bf16[256,2048]{1,0:T(8,128)(2,1)S(1)} %get-tuple-element.48.refs_1_, bf16[256,2048]{1,0:T(8,128)(2,1)S(1)} %get-tuple-element.51.refs_2_, bf16[256,2048]{1,0:T(8,128)(2,1)S(1)} %get-tuple-element.54.refs_3_, ...), custom_call_target="tpu_custom_call" | custom-call | flops 268435456 | bytes 1048576 | tf_op jit(solution)/shard_map/pallas_call | solution.py:28
  32.5 1.3 %collective-permute-start.5 = (bf16[512,256]{1,0:T(8,128)(2,1)S(1)}, bf16[512,256]{1,0:T(8,128)(2,1)S(1)}, u32[]{:S(2)}, u32[]{:S(2)}) collective-permute-start(bf16[512,256]{1,0:T(8,128)(2,1)S(1)} %shard_map.87), channel_id=1, source_target_pairs={{0,1},{1,0},{2,3},{3,2},{4,5},{5,4},{6,7},{7,6},{8,9},{9,8},{10,11... | collective-permute-start | bytes 786440 | tf_op jit(solution)/shard_map/ppermute | solution.py:187
  33.8 1.6 %collective-permute-start.10 = (bf16[128,256]{1,0:T(8,128)(2,1)S(1)}, bf16[128,256]{1,0:T(8,128)(2,1)S(1)}, u32[]{:S(2)}, u32[]{:S(2)}) collective-permute-start(bf16[128,256]{1,0:T(8,128)(2,1)S(1)} %add_convert_fusion.1), channel_id=1, source_target_pairs={{0,8},{1,9},{2,10},{3,11},{4,12},{5,13},{6,14},{7,15},{8,16},{9,17... | collective-permute-start | bytes 196616 | tf_op jit(solution)/shard_map/ppermute | solution.py:184
  35.4 2.2 %collective-permute-start.8 = (bf16[128,256]{1,0:T(8,128)(2,1)S(1)}, bf16[128,256]{1,0:T(8,128)(2,1)S(1)}, u32[]{:S(2)}, u32[]{:S(2)}) collective-permute-start(bf16[128,256]{1,0:T(8,128)(2,1)S(1)} %add_convert_fusion.2), channel_id=1, source_target_pairs={{0,6},{1,7},{2,4},{3,5},{4,10},{5,11},{6,8},{7,9},{8,14},{9,15},{1... | collective-permute-start | bytes 196616 | tf_op jit(solution)/shard_map/ppermute | solution.py:184
  37.7 0.6 %shard_map.86.own_ref = f32[512,256]{1,0:T(8,128)S(1)} custom-call(bf16[256,2048]{1,0:T(8,128)(2,1)S(1)} %get-tuple-element.45.refs_0_, bf16[256,2048]{1,0:T(8,128)(2,1)S(1)} %get-tuple-element.48.refs_1_, bf16[256,2048]{1,0:T(8,128)(2,1)S(1)} %get-tuple-element.51.refs_2_, bf16[256,2048]{1,0:T(8,128)(2,1)S(1)} %get-tuple-element.54.refs_3_, ...), custom_call_target="tpu_custom_call" | custom-call | flops 268435456 | bytes 1048576 | tf_op jit(solution)/shard_map/pallas_call | solution.py:28
  38.2 2.6 %collective-permute-done.10.two_ref = bf16[128,256]{1,0:T(8,128)(2,1)S(1)} collective-permute-done((bf16[128,256]{1,0:T(8,128)(2,1)S(1)}, bf16[128,256]{1,0:T(8,128)(2,1)S(1)}, u32[]{:S(2)}, u32[]{:S(2)}) %collective-permute-start.10) | collective-permute-done | bytes 65568 | tf_op jit(solution)/shard_map/ppermute | solution.py:184
  40.9 5.7 %collective-permute-done.8.one_ref = bf16[128,256]{1,0:T(8,128)(2,1)S(1)} collective-permute-done((bf16[128,256]{1,0:T(8,128)(2,1)S(1)}, bf16[128,256]{1,0:T(8,128)(2,1)S(1)}, u32[]{:S(2)}, u32[]{:S(2)}) %collective-permute-start.8) | collective-permute-done | bytes 65568 | tf_op jit(solution)/shard_map/ppermute | solution.py:184
  46.5 3.6 %collective-permute-done.12.three_ref = bf16[128,256]{1,0:T(8,128)(2,1)S(1)} collective-permute-done((bf16[128,256]{1,0:T(8,128)(2,1)S(1)}, bf16[128,256]{1,0:T(8,128)(2,1)S(1)}, u32[]{:S(2)}, u32[]{:S(2)}) %collective-permute-start.12) | collective-permute-done | bytes 65568 | tf_op jit(solution)/shard_map/ppermute | solution.py:184
  50.1 0.7 %shard_map.89 = (bf16[128,128]{1,0:T(8,128)(2,1)}, bf16[128,128]{1,0:T(8,128)(2,1)}) custom-call(f32[128,256]{1,0:T(8,128)S(1)} %get-tuple-element.55.mine_ref, bf16[128,256]{1,0:T(8,128)(2,1)S(1)} %collective-permute-done.6.got_ref, bf16[128,256]{1,0:T(8,128)(2,1)S(1)} %collective-permute-done.8.one_ref, ...), custom_call_target="tpu_custom_call" | custom-call | bytes 1048576 | tf_op jit(solution)/shard_map/pallas_call | solution.py:28
  50.8 0.7 %shard_map.88 = bf16[512,256]{1,0:T(8,128)(2,1)} custom-call(f32[512,256]{1,0:T(8,128)S(1)} %shard_map.86.own_ref, bf16[512,256]{1,0:T(8,128)(2,1)S(1)} %collective-permute-done.5.got_ref), custom_call_target="tpu_custom_call" | custom-call | bytes 1048576 | tf_op jit(solution)/shard_map/pallas_call | solution.py:28
  (11 shorter events, 0.1 us)
Async XLA Ops:
  1.8 13.2 %collective-permute-start = (bf16[512,512]{1,0:T(8,128)(2,1)S(1)}, bf16[512,512]{1,0:T(8,128)(2,1)S(1)}, u32[]{:S(2)}, u32[]{:S(2)}) collective-permute-start(bf16[512,512]{1,0:T(8,128)(2,1)S(1)} %get-tuple-element.38.refs_2_.refs_6_), channel_id=1, source_target_pairs={{0,1},{1,0},{2,3},{3,2},{4,5},{5,4},{6,7},{7,6},{8,9},{9,8},{10,11... | collective-permute-start | bytes 1572872 | tf_op jit(solution)/shard_map/ppermute | solution.py:187
  5.2 10.8 %collective-permute-start.3 = (bf16[256,256]{1,0:T(8,128)(2,1)S(1)}, bf16[256,256]{1,0:T(8,128)(2,1)S(1)}, u32[]{:S(2)}, u32[]{:S(2)}) collective-permute-start(bf16[256,256]{1,0:T(8,128)(2,1)S(1)} %get-tuple-element.37.refs_1_.refs_4_), channel_id=1, source_target_pairs={{0,248},{1,249},{2,250},{3,251},{4,252},{5,253},{6,254},{7,255},{8... | collective-permute-start | bytes 393224 | tf_op jit(solution)/shard_map/ppermute | solution.py:184
  11.2 6.1 %collective-permute-start.2 = (bf16[256,256]{1,0:T(8,128)(2,1)S(1)}, bf16[256,256]{1,0:T(8,128)(2,1)S(1)}, u32[]{:S(2)}, u32[]{:S(2)}) collective-permute-start(bf16[256,256]{1,0:T(8,128)(2,1)S(1)} %get-tuple-element.37.refs_1_.refs_4_), channel_id=1, source_target_pairs={{0,254},{1,255},{2,252},{3,253},{4,2},{5,3},{6,0},{7,1},{8,6},{9,7... | collective-permute-start | bytes 393224 | tf_op jit(solution)/shard_map/ppermute | solution.py:184
  14.4 6.5 %collective-permute-start.1 = (bf16[256,256]{1,0:T(8,128)(2,1)S(1)}, bf16[256,256]{1,0:T(8,128)(2,1)S(1)}, u32[]{:S(2)}, u32[]{:S(2)}) collective-permute-start(bf16[256,256]{1,0:T(8,128)(2,1)S(1)} %get-tuple-element.37.refs_1_.refs_4_), channel_id=1, source_target_pairs={{0,246},{1,247},{2,244},{3,245},{4,250},{5,251},{6,248},{7,249},{8... | collective-permute-start | bytes 393224 | tf_op jit(solution)/shard_map/ppermute | solution.py:184
  21.9 2.5 %collective-permute-start.4 = (f32[8,2048]{1,0:T(8,128)S(1)}, f32[8,2048]{1,0:T(8,128)S(1)}, u32[]{:S(2)}, u32[]{:S(2)}) collective-permute-start(f32[8,2048]{1,0:T(8,128)S(1)} %get-tuple-element.44.refs_4_.refs_3_), channel_id=1, source_target_pairs={{0,1},{1,0},{2,3},{3,2},{4,5},{5,4},{6,7},{7,6},{8,9},{9,8},{10,11... | collective-permute-start | bytes 196616 | tf_op jit(solution)/shard_map/ppermute | solution.py:187
  25.2 8.5 %collective-permute-start.9 = (bf16[128,256]{1,0:T(8,128)(2,1)S(1)}, bf16[128,256]{1,0:T(8,128)(2,1)S(1)}, u32[]{:S(2)}, u32[]{:S(2)}) collective-permute-start(bf16[128,256]{1,0:T(8,128)(2,1)S(1)} %get-tuple-element.60), channel_id=1, source_target_pairs={{0,2},{1,3},{2,0},{3,1},{4,6},{5,7},{6,4},{7,5},{8,10},{9,11},{10,... | collective-permute-start | bytes 196616 | tf_op jit(solution)/shard_map/ppermute | solution.py:187
  28.4 7.0 %collective-permute-start.7 = (bf16[128,256]{1,0:T(8,128)(2,1)S(1)}, bf16[128,256]{1,0:T(8,128)(2,1)S(1)}, u32[]{:S(2)}, u32[]{:S(2)}) collective-permute-start(bf16[128,256]{1,0:T(8,128)(2,1)S(1)} %get-tuple-element.58), channel_id=1, source_target_pairs={{0,2},{1,3},{2,0},{3,1},{4,6},{5,7},{6,4},{7,5},{8,10},{9,11},{10,... | collective-permute-start | bytes 196616 | tf_op jit(solution)/shard_map/ppermute | solution.py:187
  29.3 9.0 %collective-permute-start.6 = (bf16[128,256]{1,0:T(8,128)(2,1)S(1)}, bf16[128,256]{1,0:T(8,128)(2,1)S(1)}, u32[]{:S(2)}, u32[]{:S(2)}) collective-permute-start(bf16[128,256]{1,0:T(8,128)(2,1)S(1)} %get-tuple-element.56), channel_id=1, source_target_pairs={{0,2},{1,3},{2,0},{3,1},{4,6},{5,7},{6,4},{7,5},{8,10},{9,11},{10,... | collective-permute-start | bytes 196616 | tf_op jit(solution)/shard_map/ppermute | solution.py:187
  31.8 5.8 %collective-permute-start.11 = (bf16[128,256]{1,0:T(8,128)(2,1)S(1)}, bf16[128,256]{1,0:T(8,128)(2,1)S(1)}, u32[]{:S(2)}, u32[]{:S(2)}) collective-permute-start(bf16[128,256]{1,0:T(8,128)(2,1)S(1)} %get-tuple-element.62), channel_id=1, source_target_pairs={{0,2},{1,3},{2,0},{3,1},{4,6},{5,7},{6,4},{7,5},{8,10},{9,11},{10,... | collective-permute-start | bytes 196616 | tf_op jit(solution)/shard_map/ppermute | solution.py:187
  32.5 18.3 %collective-permute-start.5 = (bf16[512,256]{1,0:T(8,128)(2,1)S(1)}, bf16[512,256]{1,0:T(8,128)(2,1)S(1)}, u32[]{:S(2)}, u32[]{:S(2)}) collective-permute-start(bf16[512,256]{1,0:T(8,128)(2,1)S(1)} %shard_map.87), channel_id=1, source_target_pairs={{0,1},{1,0},{2,3},{3,2},{4,5},{5,4},{6,7},{7,6},{8,9},{9,8},{10,11... | collective-permute-start | bytes 786440 | tf_op jit(solution)/shard_map/ppermute | solution.py:187
  33.8 7.1 %collective-permute-start.10 = (bf16[128,256]{1,0:T(8,128)(2,1)S(1)}, bf16[128,256]{1,0:T(8,128)(2,1)S(1)}, u32[]{:S(2)}, u32[]{:S(2)}) collective-permute-start(bf16[128,256]{1,0:T(8,128)(2,1)S(1)} %add_convert_fusion.1), channel_id=1, source_target_pairs={{0,8},{1,9},{2,10},{3,11},{4,12},{5,13},{6,14},{7,15},{8,16},{9,17... | collective-permute-start | bytes 196616 | tf_op jit(solution)/shard_map/ppermute | solution.py:184
  35.4 11.2 %collective-permute-start.8 = (bf16[128,256]{1,0:T(8,128)(2,1)S(1)}, bf16[128,256]{1,0:T(8,128)(2,1)S(1)}, u32[]{:S(2)}, u32[]{:S(2)}) collective-permute-start(bf16[128,256]{1,0:T(8,128)(2,1)S(1)} %add_convert_fusion.2), channel_id=1, source_target_pairs={{0,6},{1,7},{2,4},{3,5},{4,10},{5,11},{6,8},{7,9},{8,14},{9,15},{1... | collective-permute-start | bytes 196616 | tf_op jit(solution)/shard_map/ppermute | solution.py:184
  37.6 12.6 %collective-permute-start.12 = (bf16[128,256]{1,0:T(8,128)(2,1)S(1)}, bf16[128,256]{1,0:T(8,128)(2,1)S(1)}, u32[]{:S(2)}, u32[]{:S(2)}) collective-permute-start(bf16[128,256]{1,0:T(8,128)(2,1)S(1)} %add_convert_fusion), channel_id=1, source_target_pairs={{0,14},{1,15},{2,12},{3,13},{4,18},{5,19},{6,16},{7,17},{8,22},{9,... | collective-permute-start | bytes 196616 | tf_op jit(solution)/shard_map/ppermute | solution.py:184

commit v3 on v2

--- a/solution.py
+++ b/solution.py
@@ -115,9 +115,12 @@
         stats_ref[2:3, cols] = delta
 
 
-def grads_body(flip, flag_ref, p_ref, dp_ref, stats_ref, own_ref, mate_ref, qa_ref, qb_ref, *outs):
-    ds_ref, keep_ref, give_ref = outs
+def grads_body(flips, flag_ref, own_ref, mate_ref, qa_ref, qb_ref, *refs):
+    pairs = len(flips)
+    kept, refs = refs[: 3 * pairs], refs[3 * pairs :]
+    ds_refs, keep_refs, give_ref = refs[:pairs], refs[pairs : 2 * pairs], refs[2 * pairs]
     toks = qa_ref.shape[0]
+    sums = [None] * pairs
     for head in range(HEADS_CHIP):
         cols = slice(head * toks, (head + 1) * toks)
         other = (head + 2) % HEADS_CHIP
@@ -130,21 +133,26 @@
         delta = own_ref[2:3, cols] * fade_own + mate_ref[2:3, across] * fade_mate
         inverse = 1.0 / total
         delta = delta * inverse
-        factor = jnp.exp2((stats_ref[0:1, cols] - top) * LOG2_SCALE) * inverse
-        a = p_ref[:, cols] * factor
-        ds = (a * (dp_ref[:, cols] - delta)).astype(BF16)
-        ds_ref[:, cols] = ds
-        dv_here = dot(a.astype(BF16), head_of((qa_ref, qb_ref), head, 2 * HD), NN)
-        dk_here = dot(ds, head_of((qa_ref, qb_ref), head, 0), NN)
-        dk = dk_here if head == 0 else dk + dk_here
-        dv = dv_here if head == 0 else dv + dv_here
-    both = jnp.concatenate([dk * SCALE, dv], axis=1)
-    half = both.shape[0] // 2
-    first, second = (both[half:], both[:half]) if flip else (both[:half], both[half:])
+        for i in range(pairs):
+            p_ref, dp_ref, stats_ref = kept[3 * i : 3 * i + 3]
+            factor = jnp.exp2((stats_ref[0:1, cols] - top) * LOG2_SCALE) * inverse
+            a = p_ref[:, cols] * factor
+            ds = (a * (dp_ref[:, cols] - delta)).astype(BF16)
+            ds_refs[i][:, cols] = ds
+            dv = dot(a.astype(BF16), head_of((qa_ref, qb_ref), head, 2 * HD), NN)
+            dk = dot(ds, head_of((qa_ref, qb_ref), head, 0), NN)
+            if sums[i] is None:
+                sums[i] = (dk, dv)
+            else:
+                sums[i] = (sums[i][0] + dk, sums[i][1] + dv)
     upper = flag_ref[0:1, :] > 0
     upper = jnp.concatenate([upper, upper], axis=1)
-    keep_ref[...] = jnp.where(upper, second, first)
-    give_ref[...] = jnp.where(upper, first, second).astype(BF16)
+    for i, flip in enumerate(flips):
+        both = jnp.concatenate([sums[i][0] * SCALE, sums[i][1]], axis=1)
+        half = both.shape[0] // 2
+        first, second = (both[half:], both[:half]) if flip else (both[:half], both[half:])
+        keep_refs[i][...] = jnp.where(upper, second, first)
+        give_ref[i * half : (i + 1) * half, :] = jnp.where(upper, first, second).astype(BF16)
 
 
 def query_body(heads, ds_refs, kv_refs, out_ref):
@@ -157,15 +165,14 @@
         out_ref[:, i * HD : (i + 1) * HD] = (jnp.transpose(dq) * SCALE).astype(out_ref.dtype)
 
 
-def finish_body(mine_ref, got_ref, one_ref, two_ref, three_ref, dk_ref, dv_ref):
-    total = mine_ref[...] + got_ref[...].astype(F32) + one_ref[...].astype(F32)
+def finish_body(mine_ref, got_ref, one_ref, two_ref, three_ref, dq_own_ref, dq_got_ref, *outs):
+    dq_ref, dk_ref, dv_ref = outs
+    dq_ref[...] = (dq_own_ref[...] + dq_got_ref[...].astype(F32)).astype(BF16)
+    rows = mine_ref.shape[0]
+    total = mine_ref[...] + got_ref[rows:, :].astype(F32) + one_ref[...].astype(F32)
     total = total + two_ref[...].astype(F32) + three_ref[...].astype(F32)
     dk_ref[...] = total[:, :HD].astype(BF16)
     dv_ref[...] = total[:, HD:].astype(BF16)
-
-
-def query_sum_body(own_ref, got_ref, dq_ref):
-    dq_ref[...] = (own_ref[...] + got_ref[...].astype(F32)).astype(BF16)
 
 
 def shards(queries, key_rows, value_rows, grad_out, positions):
@@ -224,44 +231,44 @@
         )
         kept[k] = (p, dp, stats)
     stats_mate = swap(stats, 1)
-    grads = {}
-    for k in (3, 2, 1, 0):
-        p, dp, own = kept[k]
-
-        grads[k] = call(
-            lambda *refs, k=k: grads_body(k % 2, *refs),
-            [
-                vmem((half, lanes), BF16),
-                vmem((half // 2, 2 * HD), F32),
-                vmem((half // 2, 2 * HD), BF16),
-            ],
-            (flag, p, dp, own, stats, stats_mate, qg, qg_mate),
-            flops=flops,
+    ds = {}
+    pushed = {}
+    for pair in ((2, 1), (3, 0)):
+        outs = call(
+            lambda *refs, pair=pair: grads_body([k % 2 for k in pair], *refs),
+            [vmem((half, lanes), BF16)] * 2
+            + [vmem((half // 2, 2 * HD), F32)] * 2
+            + [vmem((half, 2 * HD), BF16)],
+            (flag, stats, stats_mate, qg, qg_mate, *kept[pair[0]], *kept[pair[1]]),
+            flops=2 * flops,
         )
-    pushed = {}
-    for k in (3, 2, 1, 0):
-        _, keep, give = grads[k]
+        ds[pair[0]], ds[pair[1]] = outs[:2]
+        keep, give = outs[2:4], outs[4]
         got = swap(give, 2)
-        pushed[k] = (keep, got)
-        if k:
-            pushed[k] = route((keep + got.astype(F32)).astype(BF16), k)
+        for i, k in enumerate(pair):
+            if k:
+                here = got[i * half // 2 : (i + 1) * half // 2].astype(F32)
+                pushed[k] = route((keep[i] + here).astype(BF16), k)
+            else:
+                mine, mine_got = keep[i], got
 
     def query_part(heads, kind):
         def body(*refs):
             query_body(heads, refs[:SPAN], refs[SPAN : 2 * SPAN], refs[2 * SPAN])
 
-        args = [grads[k][0] for k in range(SPAN)] + [window[k] for k in range(SPAN)]
+        args = [ds[k] for k in range(SPAN)] + [window[k] for k in range(SPAN)]
         return call(body, [vmem((toks, wide), kind)], args, flops=flops)[0]
 
     dq_got = swap(query_part((2, 3), BF16), 1)
     dq_own = query_part((0, 1), F32)
-    [dq] = call(query_sum_body, [jax.ShapeDtypeStruct((toks, wide), BF16)], (dq_own, dq_got))
-    dk, dv = call(
-        finish_body,
-        [jax.ShapeDtypeStruct((half // 2, HD), BF16)] * 2,
-        (*pushed[0], pushed[1], pushed[2], pushed[3]),
+    return tuple(
+        call(
+            finish_body,
+            [jax.ShapeDtypeStruct((toks, wide), BF16)]
+            + [jax.ShapeDtypeStruct((half // 2, HD), BF16)] * 2,
+            (mine, mine_got, *(pushed[k] for k in (1, 2, 3)), dq_own, dq_got),
+        )
     )
-    return dq, dk, dv
 
 
 def solution(mesh):

time: 51.6 us -> 46.7 us (0.905)
  waiting for transfers between devices: 15.8 us -> 13.1 us
  starting transfers between devices: 24 us -> 21.6 us
    ppermute x6, waiting for transfers between devices: 14.9 us -> 12 us  [route(): return lax.ppermute(value, ('blk', 'head'), pairs)]
    ppermute x7 -> x5, starting transfers between devices: 10.5 us -> 8.27 us  [swap(): return lax.ppermute(value, 'head', [(h, h ^ bit) for h in range(heads)])]
    ppermute x7 -> x5, waiting for transfers between devices: 0.92 us -> 1.16 us  [swap(): return lax.ppermute(value, 'head', [(h, h ^ bit) for h in range(heads)])]
    pallas_call x13 -> x10, Pallas kernels: 9.68 us -> 9.53 us  [call(): pl.pallas_call(body, out_shape=outs, in_specs=[whole] * len(args), out_sp...]
  transfers between devices with their start and end apart: 13 -> 11, of which waited for: 6 -> 7; matrix products, arithmetic and copies ran while one was open for 0% -> 0% of each run, Pallas kernels for 14% -> 13%
where the time goes in v3:
time: 46.7 us; the launch traced here: 46.2 us
  starting transfers between devices  21.6 us (46%)
  waiting for transfers between devices  13.1 us (28%)
  Pallas kernels  10.7 us (23%)
  between operations  0.74 us (2%)
    ppermute x6, starting transfers between devices, route(): return lax.ppermute(value, ('blk', 'head'), pairs)  13.3 us
    ppermute x6, waiting for transfers between devices, route(): return lax.ppermute(value, ('blk', 'head'), pairs)  12 us
    pallas_call x10, Pallas kernels, call(): pl.pallas_call(body, out_shape=outs, in_specs=[whole] * len(args), out_sp...  9.53 us
    ppermute x5, starting transfers between devices, swap(): return lax.ppermute(value, 'head', [(h, h ^ bit) for h in range(heads)])  8.27 us
    pallas_call x1, Pallas kernels, shards(): pl.pallas_call(prepare, out_shape=[vmem((toks, 2 * wide), BF16), vmem((ha...  1.21 us
    ppermute x5, waiting for transfers between devices, swap(): return lax.ppermute(value, 'head', [(h, h ^ bit) for h in range(heads)])  1.16 us
  transfers between devices with their start and end apart: 11, of which 7 were waited for; matrix products, arithmetic and copies ran while one was open for 0% of the time, Pallas kernels for 13%

profile of v3, /device:TPU:1, one launch (start us, length us, event | category | flops | bytes accessed | tf_op | source)
XLA Modules:
  0.0 46.2 jit_solution(14904143183370314820)
XLA Ops:
  0.6 1.2 %shard_map.76 = (bf16[512,512]{1,0:T(8,128)(2,1)S(1)}, bf16[256,256]{1,0:T(8,128)(2,1)S(1)}, s32[24,128]{1,0:T(8,128)S(1)}) custom-call(bf16[512,256]{1,0:T(8,128)(2,1)} %q_hbm.1, bf16[512,256]{1,0:T(8,128)(2,1)} %g_hbm.1, bf16[512,128]{1,0:T(8,128)(2,1)} %k_hbm.1, bf16[512,128]{1,0:T(8,128)(2,1)} %v_hbm.1, s32[256,128]{1,0:T(8,128)} %bitcast.1), custom_call_target="tpu_custom_call" | custom-call | tf_op jit(solution)/shard_map/pallas_call | solution.py:203
  1.8 3.3 %collective-permute-start.1 = (bf16[512,512]{1,0:T(8,128)(2,1)S(1)}, bf16[512,512]{1,0:T(8,128)(2,1)S(1)}, u32[]{:S(2)}, u32[]{:S(2)}) collective-permute-start(bf16[512,512]{1,0:T(8,128)(2,1)S(1)} %get-tuple-element.34.refs_2_.refs_3_), channel_id=1, source_target_pairs={{0,1},{1,0},{2,3},{3,2},{4,5},{5,4},{6,7},{7,6},{8,9},{9,8},{10,11... | collective-permute-start | bytes 1572872 | tf_op jit(solution)/shard_map/ppermute | solution.py:194
  5.2 6.0 %collective-permute-start.3 = (bf16[256,256]{1,0:T(8,128)(2,1)S(1)}, bf16[256,256]{1,0:T(8,128)(2,1)S(1)}, u32[]{:S(2)}, u32[]{:S(2)}) collective-permute-start(bf16[256,256]{1,0:T(8,128)(2,1)S(1)} %get-tuple-element.33.refs_1_.refs_4_), channel_id=1, source_target_pairs={{0,248},{1,249},{2,250},{3,251},{4,252},{5,253},{6,254},{7,255},{8... | collective-permute-start | bytes 393224 | tf_op jit(solution)/shard_map/ppermute | solution.py:191
  11.2 3.2 %collective-permute-start.2 = (bf16[256,256]{1,0:T(8,128)(2,1)S(1)}, bf16[256,256]{1,0:T(8,128)(2,1)S(1)}, u32[]{:S(2)}, u32[]{:S(2)}) collective-permute-start(bf16[256,256]{1,0:T(8,128)(2,1)S(1)} %get-tuple-element.33.refs_1_.refs_4_), channel_id=1, source_target_pairs={{0,254},{1,255},{2,252},{3,253},{4,2},{5,3},{6,0},{7,1},{8,6},{9,7... | collective-permute-start | bytes 393224 | tf_op jit(solution)/shard_map/ppermute | solution.py:191
  14.4 0.4 collective-permute-start
  14.8 0.2 shard_map.77
  15.1 0.0 collective-permute-done.1.refs_3_.refs_4_
  15.1 0.9 %shard_map.78 = (f32[256,2048]{1,0:T(8,128)S(1)}, f32[256,2048]{1,0:T(8,128)S(1)}, f32[8,2048]{1,0:T(8,128)S(1)}) custom-call(f32[1024,512]{1,0:T(8,128)S(1)} %get-tuple-element.32.refs_0_, bf16[256,256]{1,0:T(8,128)(2,1)S(1)} %get-tuple-element.33.refs_1_.refs_4_, bf16[512,512]{1,0:T(8,128)(2,1)S(1)} %get-tuple-element.34.refs_2_.refs_3_, ...), custom_call_target="tpu_custom_call" | custom-call | flops 268435456 | bytes 1048576 | tf_op jit(solution)/shard_map/pallas_call | solution.py:28
  16.0 0.0 collective-permute-done.3.refs_1_.refs_6_
  16.0 1.0 %shard_map.79 = (f32[256,2048]{1,0:T(8,128)S(1)}, f32[256,2048]{1,0:T(8,128)S(1)}, f32[8,2048]{1,0:T(8,128)S(1)}) custom-call(f32[1024,512]{1,0:T(8,128)S(1)} %get-tuple-element.32.refs_0_, bf16[256,256]{1,0:T(8,128)(2,1)S(1)} %collective-permute-done.3.refs_1_.refs_6_, bf16[512,512]{1,0:T(8,128)(2,1)S(1)} %get-tuple-element.34.refs_2_.refs_3_, ...), custom_call_target="tpu_custom_call" | custom-call | flops 268435456 | bytes 1048576 | tf_op jit(solution)/shard_map/pallas_call | solution.py:28
  17.0 0.3 collective-permute-done.2.refs_1_.refs_5_
  17.3 1.0 %shard_map.80 = (f32[256,2048]{1,0:T(8,128)S(1)}, f32[256,2048]{1,0:T(8,128)S(1)}, f32[8,2048]{1,0:T(8,128)S(1)}) custom-call(f32[1024,512]{1,0:T(8,128)S(1)} %get-tuple-element.32.refs_0_, bf16[256,256]{1,0:T(8,128)(2,1)S(1)} %collective-permute-done.2.refs_1_.refs_5_, bf16[512,512]{1,0:T(8,128)(2,1)S(1)} %get-tuple-element.34.refs_2_.refs_3_, ...), custom_call_target="tpu_custom_call" | custom-call | flops 268435456 | bytes 1048576 | tf_op jit(solution)/shard_map/pallas_call | solution.py:28
  18.3 2.6 %collective-permute-done.refs_1_.refs_7_ = bf16[256,256]{1,0:T(8,128)(2,1)S(1)} collective-permute-done((bf16[256,256]{1,0:T(8,128)(2,1)S(1)}, bf16[256,256]{1,0:T(8,128)(2,1)S(1)}, u32[]{:S(2)}, u32[]{:S(2)}) %collective-permute-start) | collective-permute-done | bytes 131104 | tf_op jit(solution)/shard_map/ppermute | solution.py:191
  20.9 1.0 %shard_map.81 = (f32[256,2048]{1,0:T(8,128)S(1)}, f32[256,2048]{1,0:T(8,128)S(1)}, f32[8,2048]{1,0:T(8,128)S(1)}) custom-call(f32[1024,512]{1,0:T(8,128)S(1)} %get-tuple-element.32.refs_0_, bf16[256,256]{1,0:T(8,128)(2,1)S(1)} %collective-permute-done.refs_1_.refs_7_, bf16[512,512]{1,0:T(8,128)(2,1)S(1)} %get-tuple-element.34.refs_2_.refs_3_, ...), custom_call_target="tpu_custom_call" | custom-call | flops 268435456 | bytes 1048576 | tf_op jit(solution)/shard_map/pallas_call | solution.py:28
  21.9 1.6 %collective-permute-start.4 = (f32[8,2048]{1,0:T(8,128)S(1)}, f32[8,2048]{1,0:T(8,128)S(1)}, u32[]{:S(2)}, u32[]{:S(2)}) collective-permute-start(f32[8,2048]{1,0:T(8,128)S(1)} %get-tuple-element.38.refs_1_.refs_7_), channel_id=1, source_target_pairs={{0,1},{1,0},{2,3},{3,2},{4,5},{5,4},{6,7},{7,6},{8,9},{9,8},{10,11... | collective-permute-start | bytes 196616 | tf_op jit(solution)/shard_map/ppermute | solution.py:194
  23.5 0.9 %collective-permute-done.4.refs_2_ = f32[8,2048]{1,0:T(8,128)S(1)} collective-permute-done((f32[8,2048]{1,0:T(8,128)S(1)}, f32[8,2048]{1,0:T(8,128)S(1)}, u32[]{:S(2)}, u32[]{:S(2)}) %collective-permute-start.4) | collective-permute-done | bytes 65568 | tf_op jit(solution)/shard_map/ppermute | solution.py:194
  24.4 1.7 %shard_map.83 = (bf16[256,2048]{1,0:T(8,128)(2,1)S(1)}, bf16[256,2048]{1,0:T(8,128)(2,1)S(1)}, f32[128,256]{1,0:T(8,128)S(1)}, f32[128,256]{1,0:T(8,128)S(1)}, bf16[256,256]{1,0:T(8,128)(2,1)S(1)}) custom-call(f32[8,128]{1,0:T(8,128)S(1)} %get-tuple-element.31.refs_0_, f32[8,2048]{1,0:T(8,128)S(1)} %get-tuple-element.38.refs_1_.refs_7_, ...), custom_call_target="tpu_custom_call" | custom-call | flops 536870912 | bytes 1048576 | tf_op jit(solution)/shard_map/pallas_call | solution.py:28
  26.1 2.3 %collective-permute-start.6 = (bf16[256,256]{1,0:T(8,128)(2,1)S(1)}, bf16[256,256]{1,0:T(8,128)(2,1)S(1)}, u32[]{:S(2)}, u32[]{:S(2)}) collective-permute-start(bf16[256,256]{1,0:T(8,128)(2,1)S(1)} %get-tuple-element.50), channel_id=1, source_target_pairs={{0,2},{1,3},{2,0},{3,1},{4,6},{5,7},{6,4},{7,5},{8,10},{9,11},{10,... | collective-permute-start | bytes 393224 | tf_op jit(solution)/shard_map/ppermute | solution.py:194
  28.5 1.7 %shard_map.82 = (bf16[256,2048]{1,0:T(8,128)(2,1)S(1)}, bf16[256,2048]{1,0:T(8,128)(2,1)S(1)}, f32[128,256]{1,0:T(8,128)S(1)}, f32[128,256]{1,0:T(8,128)S(1)}, bf16[256,256]{1,0:T(8,128)(2,1)S(1)}) custom-call(f32[8,128]{1,0:T(8,128)S(1)} %get-tuple-element.31.refs_0_, f32[8,2048]{1,0:T(8,128)S(1)} %get-tuple-element.38.refs_1_.refs_7_, ...), custom_call_target="tpu_custom_call" | custom-call | flops 536870912 | bytes 1048576 | tf_op jit(solution)/shard_map/pallas_call | solution.py:28
  30.2 0.1 collective-permute-start.5
  30.3 0.6 %shard_map.85 = bf16[512,256]{1,0:T(8,128)(2,1)S(1)} custom-call(bf16[256,2048]{1,0:T(8,128)(2,1)S(1)} %get-tuple-element.53.refs_0_, bf16[256,2048]{1,0:T(8,128)(2,1)S(1)} %get-tuple-element.54.refs_1_, bf16[256,2048]{1,0:T(8,128)(2,1)S(1)} %get-tuple-element.55.refs_2_, bf16[256,2048]{1,0:T(8,128)(2,1)S(1)} %get-tuple-element.56.refs_3_, ...), custom_call_target="tpu_custom_call" | custom-call | flops 268435456 | bytes 1048576 | tf_op jit(solution)/shard_map/pallas_call | solution.py:28
  30.9 0.9 %collective-permute-start.10 = (bf16[512,256]{1,0:T(8,128)(2,1)S(1)}, bf16[512,256]{1,0:T(8,128)(2,1)S(1)}, u32[]{:S(2)}, u32[]{:S(2)}) collective-permute-start(bf16[512,256]{1,0:T(8,128)(2,1)S(1)} %shard_map.85), channel_id=1, source_target_pairs={{0,1},{1,0},{2,3},{3,2},{4,5},{5,4},{6,7},{7,6},{8,9},{9,8},{10,11... | collective-permute-start | bytes 786440 | tf_op jit(solution)/shard_map/ppermute | solution.py:194
  31.8 0.3 collective-permute-done.6
  32.1 1.3 %collective-permute-start.8 = (bf16[128,256]{1,0:T(8,128)(2,1)S(1)}, bf16[128,256]{1,0:T(8,128)(2,1)S(1)}, u32[]{:S(2)}, u32[]{:S(2)}) collective-permute-start(bf16[128,256]{1,0:T(8,128)(2,1)S(1)} %get-tuple-element.57), channel_id=1, source_target_pairs={{0,8},{1,9},{2,10},{3,11},{4,12},{5,13},{6,14},{7,15},{8,16},{9,17... | collective-permute-start | bytes 196616 | tf_op jit(solution)/shard_map/ppermute | solution.py:191
  33.4 2.2 %collective-permute-start.7 = (bf16[128,256]{1,0:T(8,128)(2,1)S(1)}, bf16[128,256]{1,0:T(8,128)(2,1)S(1)}, u32[]{:S(2)}, u32[]{:S(2)}) collective-permute-start(bf16[128,256]{1,0:T(8,128)(2,1)S(1)} %get-tuple-element.58), channel_id=1, source_target_pairs={{0,6},{1,7},{2,4},{3,5},{4,10},{5,11},{6,8},{7,9},{8,14},{9,15},{1... | collective-permute-start | bytes 196616 | tf_op jit(solution)/shard_map/ppermute | solution.py:191
  35.7 0.1 collective-permute-start.9
  35.8 0.6 %shard_map.84.dq_own_ref = f32[512,256]{1,0:T(8,128)S(1)} custom-call(bf16[256,2048]{1,0:T(8,128)(2,1)S(1)} %get-tuple-element.53.refs_0_, bf16[256,2048]{1,0:T(8,128)(2,1)S(1)} %get-tuple-element.54.refs_1_, bf16[256,2048]{1,0:T(8,128)(2,1)S(1)} %get-tuple-element.55.refs_2_, bf16[256,2048]{1,0:T(8,128)(2,1)S(1)} %get-tuple-element.56.refs_3_, ...), custom_call_target="tpu_custom_call" | custom-call | flops 268435456 | bytes 1048576 | tf_op jit(solution)/shard_map/pallas_call | solution.py:28
  36.4 2.3 %collective-permute-done.8.two_ref = bf16[128,256]{1,0:T(8,128)(2,1)S(1)} collective-permute-done((bf16[128,256]{1,0:T(8,128)(2,1)S(1)}, bf16[128,256]{1,0:T(8,128)(2,1)S(1)}, u32[]{:S(2)}, u32[]{:S(2)}) %collective-permute-start.8) | collective-permute-done | bytes 65568 | tf_op jit(solution)/shard_map/ppermute | solution.py:191
  38.6 4.5 %collective-permute-done.7.one_ref = bf16[128,256]{1,0:T(8,128)(2,1)S(1)} collective-permute-done((bf16[128,256]{1,0:T(8,128)(2,1)S(1)}, bf16[128,256]{1,0:T(8,128)(2,1)S(1)}, u32[]{:S(2)}, u32[]{:S(2)}) %collective-permute-start.7) | collective-permute-done | bytes 65568 | tf_op jit(solution)/shard_map/ppermute | solution.py:191
  43.1 2.3 %collective-permute-done.9.three_ref = bf16[128,256]{1,0:T(8,128)(2,1)S(1)} collective-permute-done((bf16[128,256]{1,0:T(8,128)(2,1)S(1)}, bf16[128,256]{1,0:T(8,128)(2,1)S(1)}, u32[]{:S(2)}, u32[]{:S(2)}) %collective-permute-start.9) | collective-permute-done | bytes 65568 | tf_op jit(solution)/shard_map/ppermute | solution.py:191
  45.5 0.0 collective-permute-done.10.dq_got_ref
  45.5 0.8 %shard_map.86 = (bf16[512,256]{1,0:T(8,128)(2,1)}, bf16[128,128]{1,0:T(8,128)(2,1)}, bf16[128,128]{1,0:T(8,128)(2,1)}) custom-call(f32[128,256]{1,0:T(8,128)S(1)} %get-tuple-element.43.mine_ref, bf16[256,256]{1,0:T(8,128)(2,1)S(1)} %collective-permute-done.5.got_ref, bf16[128,256]{1,0:T(8,128)(2,1)S(1)} %collective-permute-done.7.one_ref, ...), custom_call_target="tpu_custom_call" | custom-call | bytes 1048576 | tf_op jit(solution)/shard_map/pallas_call | solution.py:28
  (3 shorter events, 0.0 us)
Async XLA Ops:
  1.8 13.2 %collective-permute-start.1 = (bf16[512,512]{1,0:T(8,128)(2,1)S(1)}, bf16[512,512]{1,0:T(8,128)(2,1)S(1)}, u32[]{:S(2)}, u32[]{:S(2)}) collective-permute-start(bf16[512,512]{1,0:T(8,128)(2,1)S(1)} %get-tuple-element.34.refs_2_.refs_3_), channel_id=1, source_target_pairs={{0,1},{1,0},{2,3},{3,2},{4,5},{5,4},{6,7},{7,6},{8,9},{9,8},{10,11... | collective-permute-start | bytes 1572872 | tf_op jit(solution)/shard_map/ppermute | solution.py:194
  5.2 10.9 %collective-permute-start.3 = (bf16[256,256]{1,0:T(8,128)(2,1)S(1)}, bf16[256,256]{1,0:T(8,128)(2,1)S(1)}, u32[]{:S(2)}, u32[]{:S(2)}) collective-permute-start(bf16[256,256]{1,0:T(8,128)(2,1)S(1)} %get-tuple-element.33.refs_1_.refs_4_), channel_id=1, source_target_pairs={{0,248},{1,249},{2,250},{3,251},{4,252},{5,253},{6,254},{7,255},{8... | collective-permute-start | bytes 393224 | tf_op jit(solution)/shard_map/ppermute | solution.py:191
  11.2 6.1 %collective-permute-start.2 = (bf16[256,256]{1,0:T(8,128)(2,1)S(1)}, bf16[256,256]{1,0:T(8,128)(2,1)S(1)}, u32[]{:S(2)}, u32[]{:S(2)}) collective-permute-start(bf16[256,256]{1,0:T(8,128)(2,1)S(1)} %get-tuple-element.33.refs_1_.refs_4_), channel_id=1, source_target_pairs={{0,254},{1,255},{2,252},{3,253},{4,2},{5,3},{6,0},{7,1},{8,6},{9,7... | collective-permute-start | bytes 393224 | tf_op jit(solution)/shard_map/ppermute | solution.py:191
  14.4 6.5 %collective-permute-start = (bf16[256,256]{1,0:T(8,128)(2,1)S(1)}, bf16[256,256]{1,0:T(8,128)(2,1)S(1)}, u32[]{:S(2)}, u32[]{:S(2)}) collective-permute-start(bf16[256,256]{1,0:T(8,128)(2,1)S(1)} %get-tuple-element.33.refs_1_.refs_4_), channel_id=1, source_target_pairs={{0,246},{1,247},{2,244},{3,245},{4,250},{5,251},{6,248},{7,249},{8... | collective-permute-start | bytes 393224 | tf_op jit(solution)/shard_map/ppermute | solution.py:191
  21.9 2.5 %collective-permute-start.4 = (f32[8,2048]{1,0:T(8,128)S(1)}, f32[8,2048]{1,0:T(8,128)S(1)}, u32[]{:S(2)}, u32[]{:S(2)}) collective-permute-start(f32[8,2048]{1,0:T(8,128)S(1)} %get-tuple-element.38.refs_1_.refs_7_), channel_id=1, source_target_pairs={{0,1},{1,0},{2,3},{3,2},{4,5},{5,4},{6,7},{7,6},{8,9},{9,8},{10,11... | collective-permute-start | bytes 196616 | tf_op jit(solution)/shard_map/ppermute | solution.py:194
  26.1 5.9 %collective-permute-start.6 = (bf16[256,256]{1,0:T(8,128)(2,1)S(1)}, bf16[256,256]{1,0:T(8,128)(2,1)S(1)}, u32[]{:S(2)}, u32[]{:S(2)}) collective-permute-start(bf16[256,256]{1,0:T(8,128)(2,1)S(1)} %get-tuple-element.50), channel_id=1, source_target_pairs={{0,2},{1,3},{2,0},{3,1},{4,6},{5,7},{6,4},{7,5},{8,10},{9,11},{10,... | collective-permute-start | bytes 393224 | tf_op jit(solution)/shard_map/ppermute | solution.py:194
  30.2 5.4 %collective-permute-start.5 = (bf16[256,256]{1,0:T(8,128)(2,1)S(1)}, bf16[256,256]{1,0:T(8,128)(2,1)S(1)}, u32[]{:S(2)}, u32[]{:S(2)}) collective-permute-start(bf16[256,256]{1,0:T(8,128)(2,1)S(1)} %get-tuple-element.44), channel_id=1, source_target_pairs={{0,2},{1,3},{2,0},{3,1},{4,6},{5,7},{6,4},{7,5},{8,10},{9,11},{10,... | collective-permute-start | bytes 393224 | tf_op jit(solution)/shard_map/ppermute | solution.py:194
  30.9 14.5 %collective-permute-start.10 = (bf16[512,256]{1,0:T(8,128)(2,1)S(1)}, bf16[512,256]{1,0:T(8,128)(2,1)S(1)}, u32[]{:S(2)}, u32[]{:S(2)}) collective-permute-start(bf16[512,256]{1,0:T(8,128)(2,1)S(1)} %shard_map.85), channel_id=1, source_target_pairs={{0,1},{1,0},{2,3},{3,2},{4,5},{5,4},{6,7},{7,6},{8,9},{9,8},{10,11... | collective-permute-start | bytes 786440 | tf_op jit(solution)/shard_map/ppermute | solution.py:194
  32.1 6.5 %collective-permute-start.8 = (bf16[128,256]{1,0:T(8,128)(2,1)S(1)}, bf16[128,256]{1,0:T(8,128)(2,1)S(1)}, u32[]{:S(2)}, u32[]{:S(2)}) collective-permute-start(bf16[128,256]{1,0:T(8,128)(2,1)S(1)} %get-tuple-element.57), channel_id=1, source_target_pairs={{0,8},{1,9},{2,10},{3,11},{4,12},{5,13},{6,14},{7,15},{8,16},{9,17... | collective-permute-start | bytes 196616 | tf_op jit(solution)/shard_map/ppermute | solution.py:191
  33.4 9.7 %collective-permute-start.7 = (bf16[128,256]{1,0:T(8,128)(2,1)S(1)}, bf16[128,256]{1,0:T(8,128)(2,1)S(1)}, u32[]{:S(2)}, u32[]{:S(2)}) collective-permute-start(bf16[128,256]{1,0:T(8,128)(2,1)S(1)} %get-tuple-element.58), channel_id=1, source_target_pairs={{0,6},{1,7},{2,4},{3,5},{4,10},{5,11},{6,8},{7,9},{8,14},{9,15},{1... | collective-permute-start | bytes 196616 | tf_op jit(solution)/shard_map/ppermute | solution.py:191
  35.7 9.8 %collective-permute-start.9 = (bf16[128,256]{1,0:T(8,128)(2,1)S(1)}, bf16[128,256]{1,0:T(8,128)(2,1)S(1)}, u32[]{:S(2)}, u32[]{:S(2)}) collective-permute-start(bf16[128,256]{1,0:T(8,128)(2,1)S(1)} %add_convert_fusion), channel_id=1, source_target_pairs={{0,14},{1,15},{2,12},{3,13},{4,18},{5,19},{6,16},{7,17},{8,22},{9,... | collective-permute-start | bytes 196616 | tf_op jit(solution)/shard_map/ppermute | solution.py:191

commit v4 on v3

--- a/solution.py
+++ b/solution.py
@@ -44,11 +44,12 @@
 def prepare(q_hbm, g_hbm, k_hbm, v_hbm, pos_hbm, qg_ref, kv_ref, pos_ref, sems):
     wide = q_hbm.shape[1]
     core = lax.axis_index("head") % 2
+    chip = lax.axis_index("head") // 2
     block = lax.axis_index("blk") * (q_hbm.shape[0] // HD) // 8
     blocks = pos_hbm.shape[0] // 8
     copies = []
     for half in range(2):
-        source = pl.ds(pl.multiple_of(half * 256 + core * 128, 128), 128)
+        source = pl.ds(pl.multiple_of((chip ^ half) * 256 + core * 128, 128), 128)
         target = pl.ds(half * 128, 128)
         copies.append((k_hbm.at[source, :], kv_ref.at[target, pl.ds(0, HD)]))
         copies.append((v_hbm.at[source, :], kv_ref.at[target, pl.ds(HD, HD)]))
@@ -67,7 +68,7 @@
         copy.wait()
 
 
-def mask_body(pos_ref, bias_ref, flag_ref):
+def mask_body(pos_ref, bias_ref):
     core = lax.axis_index("head") % 2
     chip = lax.axis_index("head") // 2
     toks = bias_ref.shape[1]
@@ -77,22 +78,27 @@
     ]
     for k in range(SPAN):
         for half in range(2):
-            row = pos_ref[pl.ds(query_row + k * (toks // HD) + 2 * half + core, 1), :]
+            place = query_row + k * (toks // HD) + 2 * (chip ^ (k + half) % 2) + core
+            row = pos_ref[pl.ds(place, 1), :]
             keys = jnp.transpose(jnp.broadcast_to(row.astype(F32), (HD, HD)))
             rows = slice((2 * k + half) * HD, (2 * k + half + 1) * HD)
             for i, query in enumerate(queries):
                 bias_ref[rows, i * HD : (i + 1) * HD] = jnp.where(keys <= query, 0.0, NEG)
-    flag_ref[...] = jnp.full(flag_ref.shape, chip, F32)
-
-
-def scores_body(offset, bias_ref, kv_ref, qa_ref, qb_ref, *refs):
+
+
+def joined(refs):
+    return refs[0][...] if len(refs) == 1 else jnp.concatenate([r[...] for r in refs], axis=0)
+
+
+def scores_body(offset, parts, bias_ref, qa_ref, qb_ref, *refs):
+    kv, refs = joined(refs[:parts]), refs[parts:]
     prev_ref = refs[0] if len(refs) == 4 else None
     p_ref, dp_ref, stats_ref = refs[-3:]
-    rows = kv_ref.shape[0]
+    rows = kv.shape[0]
     toks = qa_ref.shape[0]
     bias = bias_ref[offset * rows : (offset + 1) * rows, :]
-    keys = kv_ref[:, :HD]
-    values = kv_ref[:, HD:]
+    keys = kv[:, :HD]
+    values = kv[:, HD:]
     for head in range(HEADS_CHIP):
         cols = slice(head * toks, (head + 1) * toks)
         s = dot(keys, head_of((qa_ref, qb_ref), head, 0), NT) + bias
@@ -115,8 +121,7 @@
         stats_ref[2:3, cols] = delta
 
 
-def grads_body(flips, flag_ref, own_ref, mate_ref, qa_ref, qb_ref, *refs):
-    pairs = len(flips)
+def grads_body(pairs, own_ref, mate_ref, qa_ref, qb_ref, *refs):
     kept, refs = refs[: 3 * pairs], refs[3 * pairs :]
     ds_refs, keep_refs, give_ref = refs[:pairs], refs[pairs : 2 * pairs], refs[2 * pairs]
     toks = qa_ref.shape[0]
@@ -145,32 +150,35 @@
                 sums[i] = (dk, dv)
             else:
                 sums[i] = (sums[i][0] + dk, sums[i][1] + dv)
-    upper = flag_ref[0:1, :] > 0
-    upper = jnp.concatenate([upper, upper], axis=1)
-    for i, flip in enumerate(flips):
+    for i in range(pairs):
         both = jnp.concatenate([sums[i][0] * SCALE, sums[i][1]], axis=1)
         half = both.shape[0] // 2
-        first, second = (both[half:], both[:half]) if flip else (both[:half], both[half:])
-        keep_refs[i][...] = jnp.where(upper, second, first)
-        give_ref[i * half : (i + 1) * half, :] = jnp.where(upper, first, second).astype(BF16)
-
-
-def query_body(heads, ds_refs, kv_refs, out_ref):
+        keep_refs[i][...] = both[:half]
+        give_ref[i * half : (i + 1) * half, :] = both[half:].astype(BF16)
+
+
+def query_body(heads, parts, *refs):
+    ds_refs, refs = refs[: len(parts)], refs[len(parts) :]
+    out_ref = refs[-1]
     toks = out_ref.shape[0]
+    keys = []
+    for count in parts:
+        keys.append(joined(refs[:count])[:, :HD])
+        refs = refs[count:]
     for i, head in enumerate(heads):
         dq = None
-        for ds_ref, kv_ref in zip(ds_refs, kv_refs):
-            here = dot(kv_ref[:, :HD], ds_ref[:, head * toks : (head + 1) * toks], TN)
+        for ds_ref, key in zip(ds_refs, keys):
+            here = dot(key, ds_ref[:, head * toks : (head + 1) * toks], TN)
             dq = here if dq is None else dq + here
         out_ref[:, i * HD : (i + 1) * HD] = (jnp.transpose(dq) * SCALE).astype(out_ref.dtype)
 
 
-def finish_body(mine_ref, got_ref, one_ref, two_ref, three_ref, dq_own_ref, dq_got_ref, *outs):
-    dq_ref, dk_ref, dv_ref = outs
+def finish_body(*refs):
+    *adds, dq_own_ref, dq_got_ref, dq_ref, dk_ref, dv_ref = refs
     dq_ref[...] = (dq_own_ref[...] + dq_got_ref[...].astype(F32)).astype(BF16)
-    rows = mine_ref.shape[0]
-    total = mine_ref[...] + got_ref[rows:, :].astype(F32) + one_ref[...].astype(F32)
-    total = total + two_ref[...].astype(F32) + three_ref[...].astype(F32)
+    total = adds[0][...]
+    for add in adds[1:]:
+        total = total + add[...].astype(F32)
     dk_ref[...] = total[:, :HD].astype(BF16)
     dv_ref[...] = total[:, HD:].astype(BF16)
 
@@ -213,17 +221,17 @@
         compiler_params=pltpu.CompilerParams(vmem_limit_bytes=16 * 1024 * 1024),
     )(*(pltpu.with_memory_space_constraint(v, pltpu.HBM) for v in (queries, grad_out, key_rows, value_rows, pos)))
     qg_mate = swap(qg, 1)
-    bias, flag = call(mask_body, [vmem((SPAN * half, toks), F32), vmem((8, HD), F32)], (pos,))
-    window = {0: kv}
+    [bias] = call(mask_body, [vmem((SPAN * half, toks), F32)], (pos,))
+    window = {0: (kv,)}
     for k in (2, 1, 3):
-        window[k] = route(kv, -k)
+        window[k] = (route(kv, -k),)
     kept = {}
     stats = None
     flops = 2 * 2 * HD * half * lanes
     for k in (0, 2, 1, 3):
-        args = (bias, window[k], qg, qg_mate) + (() if stats is None else (stats,))
+        args = (bias, qg, qg_mate, *window[k]) + (() if stats is None else (stats,))
         p, dp, stats = call(
-            lambda *refs, k=k: scores_body(k, *refs),
+            lambda *refs, k=k: scores_body(k, len(window[k]), *refs),
             [vmem((half, lanes), F32), vmem((half, lanes), F32), vmem((8, lanes), F32)],
             args,
             flops=flops,
@@ -233,30 +241,35 @@
     stats_mate = swap(stats, 1)
     ds = {}
     pushed = {}
-    for pair in ((2, 1), (3, 0)):
+    seen = stats
+    for pair in ((3, 1), (2, 0)):
         outs = call(
-            lambda *refs, pair=pair: grads_body([k % 2 for k in pair], *refs),
+            lambda *refs: grads_body(2, *refs),
             [vmem((half, lanes), BF16)] * 2
             + [vmem((half // 2, 2 * HD), F32)] * 2
             + [vmem((half, 2 * HD), BF16)],
-            (flag, stats, stats_mate, qg, qg_mate, *kept[pair[0]], *kept[pair[1]]),
+            (seen, stats_mate, qg, qg_mate, *kept[pair[0]], *kept[pair[1]]),
             flops=2 * flops,
         )
         ds[pair[0]], ds[pair[1]] = outs[:2]
         keep, give = outs[2:4], outs[4]
         got = swap(give, 2)
         for i, k in enumerate(pair):
+            here = got[i * half // 2 : (i + 1) * half // 2].astype(F32)
             if k:
-                here = got[i * half // 2 : (i + 1) * half // 2].astype(F32)
                 pushed[k] = route((keep[i] + here).astype(BF16), k)
             else:
-                mine, mine_got = keep[i], got
+                mine = keep[i] + here
+
+    part = pushed[3].astype(F32) + pushed[1].astype(F32)
 
     def query_part(heads, kind):
+        parts = [len(window[k]) for k in range(SPAN)]
+
         def body(*refs):
-            query_body(heads, refs[:SPAN], refs[SPAN : 2 * SPAN], refs[2 * SPAN])
-
-        args = [ds[k] for k in range(SPAN)] + [window[k] for k in range(SPAN)]
+            query_body(heads, parts, *refs)
+
+        args = [ds[k] for k in range(SPAN)] + [v for k in range(SPAN) for v in window[k]]
         return call(body, [vmem((toks, wide), kind)], args, flops=flops)[0]
 
     dq_got = swap(query_part((2, 3), BF16), 1)
@@ -266,7 +279,7 @@
             finish_body,
             [jax.ShapeDtypeStruct((toks, wide), BF16)]
             + [jax.ShapeDtypeStruct((half // 2, HD), BF16)] * 2,
-            (mine, mine_got, *(pushed[k] for k in (1, 2, 3)), dq_own, dq_got),
+            (mine, part, *(pushed[k] for k in (2,)), dq_own, dq_got),
         )
     )
 

time: 46.7 us -> 45.8 us (0.981)
  Pallas kernels: 10.7 us -> 9.98 us
    pallas_call x10, Pallas kernels: 9.53 us -> 8.77 us  [call(): pl.pallas_call(body, out_shape=outs, in_specs=[whole] * len(args), out_sp...]
  transfers between devices with their start and end apart: 11 -> 11, of which waited for: 7 -> 5; matrix products, arithmetic and copies ran while one was open for 0% -> 0% of each run, Pallas kernels for 13% -> 12%
where the time goes in v4:
time: 45.8 us; the launch traced here: 45.7 us
  starting transfers between devices  21.7 us (47%)
  waiting for transfers between devices  13.1 us (29%)
  Pallas kernels  9.98 us (22%)
  between operations  0.78 us (2%)
    ppermute x6, starting transfers between devices, route(): return lax.ppermute(value, ('blk', 'head'), pairs)  13.5 us
    ppermute x6, waiting for transfers between devices, route(): return lax.ppermute(value, ('blk', 'head'), pairs)  12.2 us
    pallas_call x10, Pallas kernels, call(): pl.pallas_call(body, out_shape=outs, in_specs=[whole] * len(args), out_sp...  8.77 us
    ppermute x5, starting transfers between devices, swap(): return lax.ppermute(value, 'head', [(h, h ^ bit) for h in range(heads)])  8.27 us
    pallas_call x1, Pallas kernels, shards(): pl.pallas_call(prepare, out_shape=[vmem((toks, 2 * wide), BF16), vmem((ha...  1.21 us
  transfers between devices with their start and end apart: 11, of which 5 were waited for; matrix products, arithmetic and copies ran while one was open for 0% of the time, Pallas kernels for 12%

profile of v4, /device:TPU:1, one launch (start us, length us, event | category | flops | bytes accessed | tf_op | source)
XLA Modules:
  0.0 45.7 jit_solution(7107986227475061072)
XLA Ops:
  0.6 1.2 %shard_map.76 = (bf16[512,512]{1,0:T(8,128)(2,1)S(1)}, bf16[256,256]{1,0:T(8,128)(2,1)S(1)}, s32[24,128]{1,0:T(8,128)S(1)}) custom-call(bf16[512,256]{1,0:T(8,128)(2,1)} %q_hbm.1, bf16[512,256]{1,0:T(8,128)(2,1)} %g_hbm.1, bf16[512,128]{1,0:T(8,128)(2,1)} %k_hbm.1, bf16[512,128]{1,0:T(8,128)(2,1)} %v_hbm.1, s32[256,128]{1,0:T(8,128)} %bitcast.1), custom_call_target="tpu_custom_call" | custom-call | tf_op jit(solution)/shard_map/pallas_call | solution.py:211
  1.8 3.3 %collective-permute-start = (bf16[512,512]{1,0:T(8,128)(2,1)S(1)}, bf16[512,512]{1,0:T(8,128)(2,1)S(1)}, u32[]{:S(2)}, u32[]{:S(2)}) collective-permute-start(bf16[512,512]{1,0:T(8,128)(2,1)S(1)} %get-tuple-element.29.refs_1_.refs_2_), channel_id=1, source_target_pairs={{0,1},{1,0},{2,3},{3,2},{4,5},{5,4},{6,7},{7,6},{8,9},{9,8},{10,11... | collective-permute-start | bytes 1572872 | tf_op jit(solution)/shard_map/ppermute | solution.py:202
  5.2 6.0 %collective-permute-start.3 = (bf16[256,256]{1,0:T(8,128)(2,1)S(1)}, bf16[256,256]{1,0:T(8,128)(2,1)S(1)}, u32[]{:S(2)}, u32[]{:S(2)}) collective-permute-start(bf16[256,256]{1,0:T(8,128)(2,1)S(1)} %get-tuple-element.30.refs_3_.refs_4_), channel_id=1, source_target_pairs={{0,248},{1,249},{2,250},{3,251},{4,252},{5,253},{6,254},{7,255},{8... | collective-permute-start | bytes 393224 | tf_op jit(solution)/shard_map/ppermute | solution.py:199
  11.2 3.2 %collective-permute-start.2 = (bf16[256,256]{1,0:T(8,128)(2,1)S(1)}, bf16[256,256]{1,0:T(8,128)(2,1)S(1)}, u32[]{:S(2)}, u32[]{:S(2)}) collective-permute-start(bf16[256,256]{1,0:T(8,128)(2,1)S(1)} %get-tuple-element.30.refs_3_.refs_4_), channel_id=1, source_target_pairs={{0,254},{1,255},{2,252},{3,253},{4,2},{5,3},{6,0},{7,1},{8,6},{9,7... | collective-permute-start | bytes 393224 | tf_op jit(solution)/shard_map/ppermute | solution.py:199
  14.4 0.4 collective-permute-start.1
  14.9 0.2 shard_map.77.refs_0_
  15.1 0.0 collective-permute-done.refs_2_.refs_3_
  15.1 0.9 %shard_map.78 = (f32[256,2048]{1,0:T(8,128)S(1)}, f32[256,2048]{1,0:T(8,128)S(1)}, f32[8,2048]{1,0:T(8,128)S(1)}) custom-call(f32[1024,512]{1,0:T(8,128)S(1)} %shard_map.77.refs_0_, bf16[512,512]{1,0:T(8,128)(2,1)S(1)} %get-tuple-element.29.refs_1_.refs_2_, bf16[512,512]{1,0:T(8,128)(2,1)S(1)} %collective-permute-done.refs_2_.refs_3_, ...), custom_call_target="tpu_custom_call" | custom-call | flops 268435456 | bytes 1048576 | tf_op jit(solution)/shard_map/pallas_call | solution.py:28
  16.0 0.0 collective-permute-done.3.refs_3_.refs_6_
  16.0 0.9 %shard_map.79 = (f32[256,2048]{1,0:T(8,128)S(1)}, f32[256,2048]{1,0:T(8,128)S(1)}, f32[8,2048]{1,0:T(8,128)S(1)}) custom-call(f32[1024,512]{1,0:T(8,128)S(1)} %shard_map.77.refs_0_, bf16[512,512]{1,0:T(8,128)(2,1)S(1)} %get-tuple-element.29.refs_1_.refs_2_, bf16[512,512]{1,0:T(8,128)(2,1)S(1)} %collective-permute-done.refs_2_.refs_3_, ...), custom_call_target="tpu_custom_call" | custom-call | flops 268435456 | bytes 1048576 | tf_op jit(solution)/shard_map/pallas_call | solution.py:28
  16.9 0.4 collective-permute-done.2.refs_3_.refs_5_
  17.3 0.9 %shard_map.80 = (f32[256,2048]{1,0:T(8,128)S(1)}, f32[256,2048]{1,0:T(8,128)S(1)}, f32[8,2048]{1,0:T(8,128)S(1)}) custom-call(f32[1024,512]{1,0:T(8,128)S(1)} %shard_map.77.refs_0_, bf16[512,512]{1,0:T(8,128)(2,1)S(1)} %get-tuple-element.29.refs_1_.refs_2_, bf16[512,512]{1,0:T(8,128)(2,1)S(1)} %collective-permute-done.refs_2_.refs_3_, ...), custom_call_target="tpu_custom_call" | custom-call | flops 268435456 | bytes 1048576 | tf_op jit(solution)/shard_map/pallas_call | solution.py:28
  18.2 2.7 %collective-permute-done.1.refs_3_.refs_7_ = bf16[256,256]{1,0:T(8,128)(2,1)S(1)} collective-permute-done((bf16[256,256]{1,0:T(8,128)(2,1)S(1)}, bf16[256,256]{1,0:T(8,128)(2,1)S(1)}, u32[]{:S(2)}, u32[]{:S(2)}) %collective-permute-start.1) | collective-permute-done | bytes 131104 | tf_op jit(solution)/shard_map/ppermute | solution.py:199
  20.9 0.9 %shard_map.81 = (f32[256,2048]{1,0:T(8,128)S(1)}, f32[256,2048]{1,0:T(8,128)S(1)}, f32[8,2048]{1,0:T(8,128)S(1)}) custom-call(f32[1024,512]{1,0:T(8,128)S(1)} %shard_map.77.refs_0_, bf16[512,512]{1,0:T(8,128)(2,1)S(1)} %get-tuple-element.29.refs_1_.refs_2_, bf16[512,512]{1,0:T(8,128)(2,1)S(1)} %collective-permute-done.refs_2_.refs_3_, ...), custom_call_target="tpu_custom_call" | custom-call | flops 268435456 | bytes 1048576 | tf_op jit(solution)/shard_map/pallas_call | solution.py:28
  21.9 1.6 %collective-permute-start.4 = (f32[8,2048]{1,0:T(8,128)S(1)}, f32[8,2048]{1,0:T(8,128)S(1)}, u32[]{:S(2)}, u32[]{:S(2)}) collective-permute-start(f32[8,2048]{1,0:T(8,128)S(1)} %get-tuple-element.34.refs_0_.refs_6_), channel_id=1, source_target_pairs={{0,1},{1,0},{2,3},{3,2},{4,5},{5,4},{6,7},{7,6},{8,9},{9,8},{10,11... | collective-permute-start | bytes 196616 | tf_op jit(solution)/shard_map/ppermute | solution.py:202
  23.4 0.9 %collective-permute-done.4.refs_1_ = f32[8,2048]{1,0:T(8,128)S(1)} collective-permute-done((f32[8,2048]{1,0:T(8,128)S(1)}, f32[8,2048]{1,0:T(8,128)S(1)}, u32[]{:S(2)}, u32[]{:S(2)}) %collective-permute-start.4) | collective-permute-done | bytes 65568 | tf_op jit(solution)/shard_map/ppermute | solution.py:202
  24.3 1.5 %shard_map.83 = (bf16[256,2048]{1,0:T(8,128)(2,1)S(1)}, bf16[256,2048]{1,0:T(8,128)(2,1)S(1)}, f32[128,256]{1,0:T(8,128)S(1)}, f32[128,256]{1,0:T(8,128)S(1)}, bf16[256,256]{1,0:T(8,128)(2,1)S(1)}) custom-call(f32[8,2048]{1,0:T(8,128)S(1)} %get-tuple-element.34.refs_0_.refs_6_, f32[8,2048]{1,0:T(8,128)S(1)} %collective-permute-done.4.refs_1_, ...), custom_call_target="tpu_custom_call" | custom-call | flops 536870912 | bytes 1048576 | tf_op jit(solution)/shard_map/pallas_call | solution.py:28
  25.8 2.4 %collective-permute-start.6 = (bf16[256,256]{1,0:T(8,128)(2,1)S(1)}, bf16[256,256]{1,0:T(8,128)(2,1)S(1)}, u32[]{:S(2)}, u32[]{:S(2)}) collective-permute-start(bf16[256,256]{1,0:T(8,128)(2,1)S(1)} %get-tuple-element.46), channel_id=1, source_target_pairs={{0,2},{1,3},{2,0},{3,1},{4,6},{5,7},{6,4},{7,5},{8,10},{9,11},{10,... | collective-permute-start | bytes 393224 | tf_op jit(solution)/shard_map/ppermute | solution.py:202
  28.2 1.5 %shard_map.82 = (bf16[256,2048]{1,0:T(8,128)(2,1)S(1)}, bf16[256,2048]{1,0:T(8,128)(2,1)S(1)}, f32[128,256]{1,0:T(8,128)S(1)}, f32[128,256]{1,0:T(8,128)S(1)}, bf16[256,256]{1,0:T(8,128)(2,1)S(1)}) custom-call(f32[8,2048]{1,0:T(8,128)S(1)} %get-tuple-element.34.refs_0_.refs_6_, f32[8,2048]{1,0:T(8,128)S(1)} %collective-permute-done.4.refs_1_, ...), custom_call_target="tpu_custom_call" | custom-call | flops 536870912 | bytes 1048576 | tf_op jit(solution)/shard_map/pallas_call | solution.py:28
  29.7 0.1 collective-permute-start.5
  29.8 0.6 %shard_map.85 = bf16[512,256]{1,0:T(8,128)(2,1)S(1)} custom-call(bf16[256,2048]{1,0:T(8,128)(2,1)S(1)} %get-tuple-element.49.refs_0_, bf16[256,2048]{1,0:T(8,128)(2,1)S(1)} %get-tuple-element.50.refs_1_, bf16[256,2048]{1,0:T(8,128)(2,1)S(1)} %get-tuple-element.51.refs_2_, bf16[256,2048]{1,0:T(8,128)(2,1)S(1)} %get-tuple-element.52.refs_3_, ...), custom_call_target="tpu_custom_call" | custom-call | flops 268435456 | bytes 1048576 | tf_op jit(solution)/shard_map/pallas_call | solution.py:28
  30.4 0.9 %collective-permute-start.10 = (bf16[512,256]{1,0:T(8,128)(2,1)S(1)}, bf16[512,256]{1,0:T(8,128)(2,1)S(1)}, u32[]{:S(2)}, u32[]{:S(2)}) collective-permute-start(bf16[512,256]{1,0:T(8,128)(2,1)S(1)} %shard_map.85), channel_id=1, source_target_pairs={{0,1},{1,0},{2,3},{3,2},{4,5},{5,4},{6,7},{7,6},{8,9},{9,8},{10,11... | collective-permute-start | bytes 786440 | tf_op jit(solution)/shard_map/ppermute | solution.py:202
  31.3 0.6 %shard_map.84.refs_3_ = f32[512,256]{1,0:T(8,128)S(1)} custom-call(bf16[256,2048]{1,0:T(8,128)(2,1)S(1)} %get-tuple-element.49.refs_0_, bf16[256,2048]{1,0:T(8,128)(2,1)S(1)} %get-tuple-element.50.refs_1_, bf16[256,2048]{1,0:T(8,128)(2,1)S(1)} %get-tuple-element.51.refs_2_, bf16[256,2048]{1,0:T(8,128)(2,1)S(1)} %get-tuple-element.52.refs_3_, ...), custom_call_target="tpu_custom_call" | custom-call | flops 268435456 | bytes 1048576 | tf_op jit(solution)/shard_map/pallas_call | solution.py:28
  31.9 0.0 collective-permute-done.6
  31.9 0.1 collective-permute-start.7
  32.0 3.6 %collective-permute-start.8 = (bf16[128,256]{1,0:T(8,128)(2,1)S(1)}, bf16[128,256]{1,0:T(8,128)(2,1)S(1)}, u32[]{:S(2)}, u32[]{:S(2)}) collective-permute-start(bf16[128,256]{1,0:T(8,128)(2,1)S(1)} %get-tuple-element.56), channel_id=1, source_target_pairs={{0,6},{1,7},{2,4},{3,5},{4,10},{5,11},{6,8},{7,9},{8,14},{9,15},{1... | collective-permute-start | bytes 196616 | tf_op jit(solution)/shard_map/ppermute | solution.py:199
  35.6 0.0 collective-permute-done.5
  35.7 0.1 collective-permute-start.9
  35.8 6.8 %collective-permute-done.7 = bf16[128,256]{1,0:T(8,128)(2,1)S(1)} collective-permute-done((bf16[128,256]{1,0:T(8,128)(2,1)S(1)}, bf16[128,256]{1,0:T(8,128)(2,1)S(1)}, u32[]{:S(2)}, u32[]{:S(2)}) %collective-permute-start.7) | collective-permute-done | bytes 65568 | tf_op jit(solution)/shard_map/ppermute | solution.py:199
  42.6 2.3 %collective-permute-done.8 = bf16[128,256]{1,0:T(8,128)(2,1)S(1)} collective-permute-done((bf16[128,256]{1,0:T(8,128)(2,1)S(1)}, bf16[128,256]{1,0:T(8,128)(2,1)S(1)}, u32[]{:S(2)}, u32[]{:S(2)}) %collective-permute-start.8) | collective-permute-done | bytes 65568 | tf_op jit(solution)/shard_map/ppermute | solution.py:199
  44.9 0.0 collective-permute-done.9.refs_2_
  44.9 0.8 %shard_map.86 = (bf16[512,256]{1,0:T(8,128)(2,1)}, bf16[128,128]{1,0:T(8,128)(2,1)}, bf16[128,128]{1,0:T(8,128)(2,1)}) custom-call(f32[128,256]{1,0:T(8,128)S(1)} %get-tuple-element.54.refs_0_, f32[128,256]{1,0:T(8,128)S(1)} %convert_add_fusion.refs_1_, bf16[128,256]{1,0:T(8,128)(2,1)S(1)} %collective-permute-done.9.refs_2_, ...), custom_call_target="tpu_custom_call" | custom-call | bytes 1048576 | tf_op jit(solution)/shard_map/pallas_call | solution.py:28
  (4 shorter events, 0.1 us)
Async XLA Ops:
  1.8 13.2 %collective-permute-start = (bf16[512,512]{1,0:T(8,128)(2,1)S(1)}, bf16[512,512]{1,0:T(8,128)(2,1)S(1)}, u32[]{:S(2)}, u32[]{:S(2)}) collective-permute-start(bf16[512,512]{1,0:T(8,128)(2,1)S(1)} %get-tuple-element.29.refs_1_.refs_2_), channel_id=1, source_target_pairs={{0,1},{1,0},{2,3},{3,2},{4,5},{5,4},{6,7},{7,6},{8,9},{9,8},{10,11... | collective-permute-start | bytes 1572872 | tf_op jit(solution)/shard_map/ppermute | solution.py:202
  5.2 10.8 %collective-permute-start.3 = (bf16[256,256]{1,0:T(8,128)(2,1)S(1)}, bf16[256,256]{1,0:T(8,128)(2,1)S(1)}, u32[]{:S(2)}, u32[]{:S(2)}) collective-permute-start(bf16[256,256]{1,0:T(8,128)(2,1)S(1)} %get-tuple-element.30.refs_3_.refs_4_), channel_id=1, source_target_pairs={{0,248},{1,249},{2,250},{3,251},{4,252},{5,253},{6,254},{7,255},{8... | collective-permute-start | bytes 393224 | tf_op jit(solution)/shard_map/ppermute | solution.py:199
  11.2 6.1 %collective-permute-start.2 = (bf16[256,256]{1,0:T(8,128)(2,1)S(1)}, bf16[256,256]{1,0:T(8,128)(2,1)S(1)}, u32[]{:S(2)}, u32[]{:S(2)}) collective-permute-start(bf16[256,256]{1,0:T(8,128)(2,1)S(1)} %get-tuple-element.30.refs_3_.refs_4_), channel_id=1, source_target_pairs={{0,254},{1,255},{2,252},{3,253},{4,2},{5,3},{6,0},{7,1},{8,6},{9,7... | collective-permute-start | bytes 393224 | tf_op jit(solution)/shard_map/ppermute | solution.py:199
  14.4 6.5 %collective-permute-start.1 = (bf16[256,256]{1,0:T(8,128)(2,1)S(1)}, bf16[256,256]{1,0:T(8,128)(2,1)S(1)}, u32[]{:S(2)}, u32[]{:S(2)}) collective-permute-start(bf16[256,256]{1,0:T(8,128)(2,1)S(1)} %get-tuple-element.30.refs_3_.refs_4_), channel_id=1, source_target_pairs={{0,246},{1,247},{2,244},{3,245},{4,250},{5,251},{6,248},{7,249},{8... | collective-permute-start | bytes 393224 | tf_op jit(solution)/shard_map/ppermute | solution.py:199
  21.9 2.5 %collective-permute-start.4 = (f32[8,2048]{1,0:T(8,128)S(1)}, f32[8,2048]{1,0:T(8,128)S(1)}, u32[]{:S(2)}, u32[]{:S(2)}) collective-permute-start(f32[8,2048]{1,0:T(8,128)S(1)} %get-tuple-element.34.refs_0_.refs_6_), channel_id=1, source_target_pairs={{0,1},{1,0},{2,3},{3,2},{4,5},{5,4},{6,7},{7,6},{8,9},{9,8},{10,11... | collective-permute-start | bytes 196616 | tf_op jit(solution)/shard_map/ppermute | solution.py:202
  25.8 6.0 %collective-permute-start.6 = (bf16[256,256]{1,0:T(8,128)(2,1)S(1)}, bf16[256,256]{1,0:T(8,128)(2,1)S(1)}, u32[]{:S(2)}, u32[]{:S(2)}) collective-permute-start(bf16[256,256]{1,0:T(8,128)(2,1)S(1)} %get-tuple-element.46), channel_id=1, source_target_pairs={{0,2},{1,3},{2,0},{3,1},{4,6},{5,7},{6,4},{7,5},{8,10},{9,11},{10,... | collective-permute-start | bytes 393224 | tf_op jit(solution)/shard_map/ppermute | solution.py:202
  29.7 5.9 %collective-permute-start.5 = (bf16[256,256]{1,0:T(8,128)(2,1)S(1)}, bf16[256,256]{1,0:T(8,128)(2,1)S(1)}, u32[]{:S(2)}, u32[]{:S(2)}) collective-permute-start(bf16[256,256]{1,0:T(8,128)(2,1)S(1)} %get-tuple-element.40), channel_id=1, source_target_pairs={{0,2},{1,3},{2,0},{3,1},{4,6},{5,7},{6,4},{7,5},{8,10},{9,11},{10,... | collective-permute-start | bytes 393224 | tf_op jit(solution)/shard_map/ppermute | solution.py:202
  30.4 14.5 %collective-permute-start.10 = (bf16[512,256]{1,0:T(8,128)(2,1)S(1)}, bf16[512,256]{1,0:T(8,128)(2,1)S(1)}, u32[]{:S(2)}, u32[]{:S(2)}) collective-permute-start(bf16[512,256]{1,0:T(8,128)(2,1)S(1)} %shard_map.85), channel_id=1, source_target_pairs={{0,1},{1,0},{2,3},{3,2},{4,5},{5,4},{6,7},{7,6},{8,9},{9,8},{10,11... | collective-permute-start | bytes 786440 | tf_op jit(solution)/shard_map/ppermute | solution.py:202
  31.9 10.7 %collective-permute-start.7 = (bf16[128,256]{1,0:T(8,128)(2,1)S(1)}, bf16[128,256]{1,0:T(8,128)(2,1)S(1)}, u32[]{:S(2)}, u32[]{:S(2)}) collective-permute-start(bf16[128,256]{1,0:T(8,128)(2,1)S(1)} %get-tuple-element.55), channel_id=1, source_target_pairs={{0,14},{1,15},{2,12},{3,13},{4,18},{5,19},{6,16},{7,17},{8,22},{9,... | collective-permute-start | bytes 196616 | tf_op jit(solution)/shard_map/ppermute | solution.py:199
  32.0 12.9 %collective-permute-start.8 = (bf16[128,256]{1,0:T(8,128)(2,1)S(1)}, bf16[128,256]{1,0:T(8,128)(2,1)S(1)}, u32[]{:S(2)}, u32[]{:S(2)}) collective-permute-start(bf16[128,256]{1,0:T(8,128)(2,1)S(1)} %get-tuple-element.56), channel_id=1, source_target_pairs={{0,6},{1,7},{2,4},{3,5},{4,10},{5,11},{6,8},{7,9},{8,14},{9,15},{1... | collective-permute-start | bytes 196616 | tf_op jit(solution)/shard_map/ppermute | solution.py:199
  35.7 9.3 %collective-permute-start.9 = (bf16[128,256]{1,0:T(8,128)(2,1)S(1)}, bf16[128,256]{1,0:T(8,128)(2,1)S(1)}, u32[]{:S(2)}, u32[]{:S(2)}) collective-permute-start(bf16[128,256]{1,0:T(8,128)(2,1)S(1)} %get-tuple-element.53), channel_id=1, source_target_pairs={{0,8},{1,9},{2,10},{3,11},{4,12},{5,13},{6,14},{7,15},{8,16},{9,17... | collective-permute-start | bytes 196616 | tf_op jit(solution)/shard_map/ppermute | solution.py:199

commit v5 on v4

--- a/solution.py
+++ b/solution.py
@@ -241,27 +241,35 @@
     stats_mate = swap(stats, 1)
     ds = {}
     pushed = {}
+    quarter = half // 2
+    ready = {}
+    gives = []
     seen = stats
-    for pair in ((3, 1), (2, 0)):
+    for group in ((3,), (2, 1), (0,)):
+        count = len(group)
         outs = call(
-            lambda *refs: grads_body(2, *refs),
-            [vmem((half, lanes), BF16)] * 2
-            + [vmem((half // 2, 2 * HD), F32)] * 2
-            + [vmem((half, 2 * HD), BF16)],
-            (seen, stats_mate, qg, qg_mate, *kept[pair[0]], *kept[pair[1]]),
-            flops=2 * flops,
+            lambda *refs, count=count: grads_body(count, *refs),
+            [vmem((half, lanes), BF16)] * count
+            + [vmem((quarter, 2 * HD), F32)] * count
+            + [vmem((count * quarter, 2 * HD), BF16)],
+            (seen, stats_mate, qg, qg_mate, *(v for k in group for v in kept[k])),
+            flops=count * flops,
         )
-        ds[pair[0]], ds[pair[1]] = outs[:2]
-        keep, give = outs[2:4], outs[4]
+        for i, k in enumerate(group):
+            ds[k] = outs[i]
+        keep, give = outs[count : 2 * count], outs[2 * count]
+        gives.append(give)
         got = swap(give, 2)
-        for i, k in enumerate(pair):
-            here = got[i * half // 2 : (i + 1) * half // 2].astype(F32)
+        for i, k in enumerate(group):
+            total = keep[i] + got[i * quarter : (i + 1) * quarter].astype(F32)
             if k:
-                pushed[k] = route((keep[i] + here).astype(BF16), k)
+                ready[k] = total.astype(BF16)
+                pushed[k] = route(ready[k], k)
             else:
-                mine = keep[i] + here
-
-    part = pushed[3].astype(F32) + pushed[1].astype(F32)
+                mine = total
+        seen, *_ = lax.optimization_barrier((stats, give, *([ready[3]] if len(gives) == 2 else [])))
+
+    part = pushed[3].astype(F32) + pushed[1].astype(F32) + pushed[2].astype(F32)
 
     def query_part(heads, kind):
         parts = [len(window[k]) for k in range(SPAN)]
@@ -279,7 +287,7 @@
             finish_body,
             [jax.ShapeDtypeStruct((toks, wide), BF16)]
             + [jax.ShapeDtypeStruct((half // 2, HD), BF16)] * 2,
-            (mine, part, *(pushed[k] for k in (2,)), dq_own, dq_got),
+            (mine, part, dq_own, dq_got),
         )
     )
 

time: 45.8 us -> 45 us (0.983)
  waiting for transfers between devices: 13.1 us -> 11.8 us
    ppermute x5 -> x6, starting transfers between devices: 8.27 us -> 10.3 us  [swap(): return lax.ppermute(value, 'head', [(h, h ^ bit) for h in range(heads)])]
    ppermute x6, waiting for transfers between devices: 12.2 us -> 10.3 us  [route(): return lax.ppermute(value, ('blk', 'head'), pairs)]
    ppermute x6, starting transfers between devices: 13.5 us -> 11.7 us  [route(): return lax.ppermute(value, ('blk', 'head'), pairs)]
    ppermute x5 -> x6, waiting for transfers between devices: 0.91 us -> 1.49 us  [swap(): return lax.ppermute(value, 'head', [(h, h ^ bit) for h in range(heads)])]
    pallas_call x10 -> x11, Pallas kernels: 8.77 us -> 8.85 us  [call(): pl.pallas_call(body, out_shape=outs, in_specs=[whole] * len(args), out_sp...]
  transfers between devices with their start and end apart: 11 -> 12, of which waited for: 5 -> 7; matrix products, arithmetic and copies ran while one was open for 0% -> 0% of each run, Pallas kernels for 12% -> 14%
where the time goes in v5:
time: 45 us; the launch traced here: 44.7 us
  starting transfers between devices  22 us (49%)
  waiting for transfers between devices  11.8 us (26%)
  Pallas kernels  10.1 us (22%)
  between operations  0.77 us (2%)
    ppermute x6, starting transfers between devices, route(): return lax.ppermute(value, ('blk', 'head'), pairs)  11.7 us
    ppermute x6, waiting for transfers between devices, route(): return lax.ppermute(value, ('blk', 'head'), pairs)  10.3 us
    ppermute x6, starting transfers between devices, swap(): return lax.ppermute(value, 'head', [(h, h ^ bit) for h in range(heads)])  10.3 us
    pallas_call x11, Pallas kernels, call(): pl.pallas_call(body, out_shape=outs, in_specs=[whole] * len(args), out_sp...  8.85 us
    ppermute x6, waiting for transfers between devices, swap(): return lax.ppermute(value, 'head', [(h, h ^ bit) for h in range(heads)])  1.49 us
    pallas_call x1, Pallas kernels, shards(): pl.pallas_call(prepare, out_shape=[vmem((toks, 2 * wide), BF16), vmem((ha...  1.21 us
  transfers between devices with their start and end apart: 12, of which 7 were waited for; matrix products, arithmetic and copies ran while one was open for 0% of the time, Pallas kernels for 14%

profile of v5, /device:TPU:1, one launch (start us, length us, event | category | flops | bytes accessed | tf_op | source)
XLA Modules:
  0.0 44.7 jit_solution(3642280465409827747)
XLA Ops:
  0.6 1.2 %shard_map.76 = (bf16[512,512]{1,0:T(8,128)(2,1)S(1)}, bf16[256,256]{1,0:T(8,128)(2,1)S(1)}, s32[24,128]{1,0:T(8,128)S(1)}) custom-call(bf16[512,256]{1,0:T(8,128)(2,1)} %q_hbm.1, bf16[512,256]{1,0:T(8,128)(2,1)} %g_hbm.1, bf16[512,128]{1,0:T(8,128)(2,1)} %k_hbm.1, bf16[512,128]{1,0:T(8,128)(2,1)} %v_hbm.1, s32[256,128]{1,0:T(8,128)} %bitcast.1), custom_call_target="tpu_custom_call" | custom-call | tf_op jit(solution)/shard_map/pallas_call | solution.py:211
  1.8 3.3 %collective-permute-start = (bf16[512,512]{1,0:T(8,128)(2,1)S(1)}, bf16[512,512]{1,0:T(8,128)(2,1)S(1)}, u32[]{:S(2)}, u32[]{:S(2)}) collective-permute-start(bf16[512,512]{1,0:T(8,128)(2,1)S(1)} %get-tuple-element.32.refs_1_.refs_2_), channel_id=1, source_target_pairs={{0,1},{1,0},{2,3},{3,2},{4,5},{5,4},{6,7},{7,6},{8,9},{9,8},{10,11... | collective-permute-start | bytes 1572872 | tf_op jit(solution)/shard_map/ppermute | solution.py:202
  5.2 6.0 %collective-permute-start.3 = (bf16[256,256]{1,0:T(8,128)(2,1)S(1)}, bf16[256,256]{1,0:T(8,128)(2,1)S(1)}, u32[]{:S(2)}, u32[]{:S(2)}) collective-permute-start(bf16[256,256]{1,0:T(8,128)(2,1)S(1)} %get-tuple-element.33.refs_3_.refs_4_), channel_id=1, source_target_pairs={{0,248},{1,249},{2,250},{3,251},{4,252},{5,253},{6,254},{7,255},{8... | collective-permute-start | bytes 393224 | tf_op jit(solution)/shard_map/ppermute | solution.py:199
  11.2 3.2 %collective-permute-start.2 = (bf16[256,256]{1,0:T(8,128)(2,1)S(1)}, bf16[256,256]{1,0:T(8,128)(2,1)S(1)}, u32[]{:S(2)}, u32[]{:S(2)}) collective-permute-start(bf16[256,256]{1,0:T(8,128)(2,1)S(1)} %get-tuple-element.33.refs_3_.refs_4_), channel_id=1, source_target_pairs={{0,254},{1,255},{2,252},{3,253},{4,2},{5,3},{6,0},{7,1},{8,6},{9,7... | collective-permute-start | bytes 393224 | tf_op jit(solution)/shard_map/ppermute | solution.py:199
  14.4 0.4 collective-permute-start.1
  14.9 0.2 shard_map.77.refs_0_
  15.1 0.0 collective-permute-done.refs_2_.refs_3_
  15.1 0.9 %shard_map.78 = (f32[256,2048]{1,0:T(8,128)S(1)}, f32[256,2048]{1,0:T(8,128)S(1)}, f32[8,2048]{1,0:T(8,128)S(1)}) custom-call(f32[1024,512]{1,0:T(8,128)S(1)} %shard_map.77.refs_0_, bf16[512,512]{1,0:T(8,128)(2,1)S(1)} %get-tuple-element.32.refs_1_.refs_2_, bf16[512,512]{1,0:T(8,128)(2,1)S(1)} %collective-permute-done.refs_2_.refs_3_, ...), custom_call_target="tpu_custom_call" | custom-call | flops 268435456 | bytes 1048576 | tf_op jit(solution)/shard_map/pallas_call | solution.py:28
  16.0 0.0 collective-permute-done.3.refs_3_.refs_6_
  16.0 0.9 %shard_map.79 = (f32[256,2048]{1,0:T(8,128)S(1)}, f32[256,2048]{1,0:T(8,128)S(1)}, f32[8,2048]{1,0:T(8,128)S(1)}) custom-call(f32[1024,512]{1,0:T(8,128)S(1)} %shard_map.77.refs_0_, bf16[512,512]{1,0:T(8,128)(2,1)S(1)} %get-tuple-element.32.refs_1_.refs_2_, bf16[512,512]{1,0:T(8,128)(2,1)S(1)} %collective-permute-done.refs_2_.refs_3_, ...), custom_call_target="tpu_custom_call" | custom-call | flops 268435456 | bytes 1048576 | tf_op jit(solution)/shard_map/pallas_call | solution.py:28
  16.9 0.4 collective-permute-done.2.refs_3_.refs_5_
  17.3 0.9 %shard_map.80 = (f32[256,2048]{1,0:T(8,128)S(1)}, f32[256,2048]{1,0:T(8,128)S(1)}, f32[8,2048]{1,0:T(8,128)S(1)}) custom-call(f32[1024,512]{1,0:T(8,128)S(1)} %shard_map.77.refs_0_, bf16[512,512]{1,0:T(8,128)(2,1)S(1)} %get-tuple-element.32.refs_1_.refs_2_, bf16[512,512]{1,0:T(8,128)(2,1)S(1)} %collective-permute-done.refs_2_.refs_3_, ...), custom_call_target="tpu_custom_call" | custom-call | flops 268435456 | bytes 1048576 | tf_op jit(solution)/shard_map/pallas_call | solution.py:28
  18.2 2.7 %collective-permute-done.1.refs_3_.refs_7_ = bf16[256,256]{1,0:T(8,128)(2,1)S(1)} collective-permute-done((bf16[256,256]{1,0:T(8,128)(2,1)S(1)}, bf16[256,256]{1,0:T(8,128)(2,1)S(1)}, u32[]{:S(2)}, u32[]{:S(2)}) %collective-permute-start.1) | collective-permute-done | bytes 131104 | tf_op jit(solution)/shard_map/ppermute | solution.py:199
  20.9 0.9 %shard_map.81 = (f32[256,2048]{1,0:T(8,128)S(1)}, f32[256,2048]{1,0:T(8,128)S(1)}, f32[8,2048]{1,0:T(8,128)S(1)}) custom-call(f32[1024,512]{1,0:T(8,128)S(1)} %shard_map.77.refs_0_, bf16[512,512]{1,0:T(8,128)(2,1)S(1)} %get-tuple-element.32.refs_1_.refs_2_, bf16[512,512]{1,0:T(8,128)(2,1)S(1)} %collective-permute-done.refs_2_.refs_3_, ...), custom_call_target="tpu_custom_call" | custom-call | flops 268435456 | bytes 1048576 | tf_op jit(solution)/shard_map/pallas_call | solution.py:28
  21.9 1.6 %collective-permute-start.4 = (f32[8,2048]{1,0:T(8,128)S(1)}, f32[8,2048]{1,0:T(8,128)S(1)}, u32[]{:S(2)}, u32[]{:S(2)}) collective-permute-start(f32[8,2048]{1,0:T(8,128)S(1)} %get-tuple-element.48.refs_0_.refs_6_), channel_id=1, source_target_pairs={{0,1},{1,0},{2,3},{3,2},{4,5},{5,4},{6,7},{7,6},{8,9},{9,8},{10,11... | collective-permute-start | bytes 196616 | tf_op jit(solution)/shard_map/ppermute | solution.py:202
  23.4 0.9 %collective-permute-done.4.refs_1_ = f32[8,2048]{1,0:T(8,128)S(1)} collective-permute-done((f32[8,2048]{1,0:T(8,128)S(1)}, f32[8,2048]{1,0:T(8,128)S(1)}, u32[]{:S(2)}, u32[]{:S(2)}) %collective-permute-start.4) | collective-permute-done | bytes 65568 | tf_op jit(solution)/shard_map/ppermute | solution.py:202
  24.3 0.8 %shard_map.82 = (bf16[256,2048]{1,0:T(8,128)(2,1)S(1)}, f32[128,256]{1,0:T(8,128)S(1)}, bf16[128,256]{1,0:T(8,128)(2,1)S(1)}) custom-call(f32[8,2048]{1,0:T(8,128)S(1)} %get-tuple-element.48.refs_0_.refs_6_, f32[8,2048]{1,0:T(8,128)S(1)} %collective-permute-done.4.refs_1_, bf16[512,512]{1,0:T(8,128)(2,1)S(1)} %get-tuple-element.32.refs_1_.refs_2_, ...), custom_call_target="tpu_custom_call" | custom-call | flops 268435456 | bytes 1048576 | tf_op jit(solution)/shard_map/pallas_call | solution.py:28
  25.1 2.4 %collective-permute-start.5 = (bf16[128,256]{1,0:T(8,128)(2,1)S(1)}, bf16[128,256]{1,0:T(8,128)(2,1)S(1)}, u32[]{:S(2)}, u32[]{:S(2)}) collective-permute-start(bf16[128,256]{1,0:T(8,128)(2,1)S(1)} %get-tuple-element.40), channel_id=1, source_target_pairs={{0,2},{1,3},{2,0},{3,1},{4,6},{5,7},{6,4},{7,5},{8,10},{9,11},{10,... | collective-permute-start | bytes 196616 | tf_op jit(solution)/shard_map/ppermute | solution.py:202
  27.5 1.5 %shard_map.83 = (bf16[256,2048]{1,0:T(8,128)(2,1)S(1)}, bf16[256,2048]{1,0:T(8,128)(2,1)S(1)}, f32[128,256]{1,0:T(8,128)S(1)}, f32[128,256]{1,0:T(8,128)S(1)}, bf16[256,256]{1,0:T(8,128)(2,1)S(1)}) custom-call(f32[8,2048]{1,0:T(8,128)S(1)} %get-tuple-element.48.refs_0_.refs_6_, f32[8,2048]{1,0:T(8,128)S(1)} %collective-permute-done.4.refs_1_, ...), custom_call_target="tpu_custom_call" | custom-call | flops 536870912 | bytes 1048576 | tf_op jit(solution)/shard_map/pallas_call | solution.py:28
  29.0 0.1 collective-permute-start.8
  29.1 0.6 %collective-permute-done.5 = bf16[128,256]{1,0:T(8,128)(2,1)S(1)} collective-permute-done((bf16[128,256]{1,0:T(8,128)(2,1)S(1)}, bf16[128,256]{1,0:T(8,128)(2,1)S(1)}, u32[]{:S(2)}, u32[]{:S(2)}) %collective-permute-start.5) | collective-permute-done | bytes 65568 | tf_op jit(solution)/shard_map/ppermute | solution.py:202
  29.7 0.3 collective-permute-start.7
  30.0 0.8 %shard_map.84 = (bf16[256,2048]{1,0:T(8,128)(2,1)S(1)}, f32[128,256]{1,0:T(8,128)S(1)}, bf16[128,256]{1,0:T(8,128)(2,1)S(1)}) custom-call(f32[8,2048]{1,0:T(8,128)S(1)} %get-tuple-element.48.refs_0_.refs_6_, f32[8,2048]{1,0:T(8,128)S(1)} %collective-permute-done.4.refs_1_, bf16[512,512]{1,0:T(8,128)(2,1)S(1)} %get-tuple-element.32.refs_1_.refs_2_, ...), custom_call_target="tpu_custom_call" | custom-call | flops 268435456 | bytes 1048576 | tf_op jit(solution)/shard_map/pallas_call | solution.py:28
  30.8 1.0 %collective-permute-start.6 = (bf16[128,256]{1,0:T(8,128)(2,1)S(1)}, bf16[128,256]{1,0:T(8,128)(2,1)S(1)}, u32[]{:S(2)}, u32[]{:S(2)}) collective-permute-start(bf16[128,256]{1,0:T(8,128)(2,1)S(1)} %get-tuple-element.52), channel_id=1, source_target_pairs={{0,2},{1,3},{2,0},{3,1},{4,6},{5,7},{6,4},{7,5},{8,10},{9,11},{10,... | collective-permute-start | bytes 196616 | tf_op jit(solution)/shard_map/ppermute | solution.py:202
  31.8 0.6 %shard_map.86 = bf16[512,256]{1,0:T(8,128)(2,1)S(1)} custom-call(bf16[256,2048]{1,0:T(8,128)(2,1)S(1)} %get-tuple-element.55.refs_0_, bf16[256,2048]{1,0:T(8,128)(2,1)S(1)} %get-tuple-element.56.refs_1_, bf16[256,2048]{1,0:T(8,128)(2,1)S(1)} %get-tuple-element.57.refs_2_, bf16[256,2048]{1,0:T(8,128)(2,1)S(1)} %get-tuple-element.58.refs_3_, ...), custom_call_target="tpu_custom_call" | custom-call | flops 268435456 | bytes 1048576 | tf_op jit(solution)/shard_map/pallas_call | solution.py:28
  32.4 1.9 %collective-permute-start.11 = (bf16[512,256]{1,0:T(8,128)(2,1)S(1)}, bf16[512,256]{1,0:T(8,128)(2,1)S(1)}, u32[]{:S(2)}, u32[]{:S(2)}) collective-permute-start(bf16[512,256]{1,0:T(8,128)(2,1)S(1)} %shard_map.86), channel_id=1, source_target_pairs={{0,1},{1,0},{2,3},{3,2},{4,5},{5,4},{6,7},{7,6},{8,9},{9,8},{10,11... | collective-permute-start | bytes 786440 | tf_op jit(solution)/shard_map/ppermute | solution.py:202
  34.2 0.6 %shard_map.85.refs_2_ = f32[512,256]{1,0:T(8,128)S(1)} custom-call(bf16[256,2048]{1,0:T(8,128)(2,1)S(1)} %get-tuple-element.55.refs_0_, bf16[256,2048]{1,0:T(8,128)(2,1)S(1)} %get-tuple-element.56.refs_1_, bf16[256,2048]{1,0:T(8,128)(2,1)S(1)} %get-tuple-element.57.refs_2_, bf16[256,2048]{1,0:T(8,128)(2,1)S(1)} %get-tuple-element.58.refs_3_, ...), custom_call_target="tpu_custom_call" | custom-call | flops 268435456 | bytes 1048576 | tf_op jit(solution)/shard_map/pallas_call | solution.py:28
  34.9 1.8 %collective-permute-start.9 = (bf16[128,256]{1,0:T(8,128)(2,1)S(1)}, bf16[128,256]{1,0:T(8,128)(2,1)S(1)}, u32[]{:S(2)}, u32[]{:S(2)}) collective-permute-start(bf16[128,256]{1,0:T(8,128)(2,1)S(1)} %get-tuple-element.59), channel_id=1, source_target_pairs={{0,6},{1,7},{2,4},{3,5},{4,10},{5,11},{6,8},{7,9},{8,14},{9,15},{1... | collective-permute-start | bytes 196616 | tf_op jit(solution)/shard_map/ppermute | solution.py:199
  36.7 2.9 %collective-permute-done.7 = bf16[128,256]{1,0:T(8,128)(2,1)S(1)} collective-permute-done((bf16[128,256]{1,0:T(8,128)(2,1)S(1)}, bf16[128,256]{1,0:T(8,128)(2,1)S(1)}, u32[]{:S(2)}, u32[]{:S(2)}) %collective-permute-start.7) | collective-permute-done | bytes 65568 | tf_op jit(solution)/shard_map/ppermute | solution.py:199
  39.6 4.1 %collective-permute-done.9 = bf16[128,256]{1,0:T(8,128)(2,1)S(1)} collective-permute-done((bf16[128,256]{1,0:T(8,128)(2,1)S(1)}, bf16[128,256]{1,0:T(8,128)(2,1)S(1)}, u32[]{:S(2)}, u32[]{:S(2)}) %collective-permute-start.9) | collective-permute-done | bytes 65568 | tf_op jit(solution)/shard_map/ppermute | solution.py:199
  43.6 0.3 collective-permute-done.10
  43.9 0.8 %shard_map.87 = (bf16[512,256]{1,0:T(8,128)(2,1)}, bf16[128,128]{1,0:T(8,128)(2,1)}, bf16[128,128]{1,0:T(8,128)(2,1)}) custom-call(f32[128,256]{1,0:T(8,128)S(1)} %convert_add_fusion.1.refs_0_, f32[128,256]{1,0:T(8,128)S(1)} %convert_add_fusion.refs_1_, f32[512,256]{1,0:T(8,128)S(1)} %shard_map.85.refs_2_, bf16[512,256]{1,0:T(8,128)(2,1)S(1)} %collective-permute-done.11.refs_3_), custom_call_target="tpu_custom_call" | custom-call | bytes 1048576 | tf_op jit(solution)/shard_map/pallas_call | solution.py:28
  (8 shorter events, 0.1 us)
Async XLA Ops:
  1.8 13.2 %collective-permute-start = (bf16[512,512]{1,0:T(8,128)(2,1)S(1)}, bf16[512,512]{1,0:T(8,128)(2,1)S(1)}, u32[]{:S(2)}, u32[]{:S(2)}) collective-permute-start(bf16[512,512]{1,0:T(8,128)(2,1)S(1)} %get-tuple-element.32.refs_1_.refs_2_), channel_id=1, source_target_pairs={{0,1},{1,0},{2,3},{3,2},{4,5},{5,4},{6,7},{7,6},{8,9},{9,8},{10,11... | collective-permute-start | bytes 1572872 | tf_op jit(solution)/shard_map/ppermute | solution.py:202
  5.2 10.8 %collective-permute-start.3 = (bf16[256,256]{1,0:T(8,128)(2,1)S(1)}, bf16[256,256]{1,0:T(8,128)(2,1)S(1)}, u32[]{:S(2)}, u32[]{:S(2)}) collective-permute-start(bf16[256,256]{1,0:T(8,128)(2,1)S(1)} %get-tuple-element.33.refs_3_.refs_4_), channel_id=1, source_target_pairs={{0,248},{1,249},{2,250},{3,251},{4,252},{5,253},{6,254},{7,255},{8... | collective-permute-start | bytes 393224 | tf_op jit(solution)/shard_map/ppermute | solution.py:199
  11.2 6.1 %collective-permute-start.2 = (bf16[256,256]{1,0:T(8,128)(2,1)S(1)}, bf16[256,256]{1,0:T(8,128)(2,1)S(1)}, u32[]{:S(2)}, u32[]{:S(2)}) collective-permute-start(bf16[256,256]{1,0:T(8,128)(2,1)S(1)} %get-tuple-element.33.refs_3_.refs_4_), channel_id=1, source_target_pairs={{0,254},{1,255},{2,252},{3,253},{4,2},{5,3},{6,0},{7,1},{8,6},{9,7... | collective-permute-start | bytes 393224 | tf_op jit(solution)/shard_map/ppermute | solution.py:199
  14.4 6.5 %collective-permute-start.1 = (bf16[256,256]{1,0:T(8,128)(2,1)S(1)}, bf16[256,256]{1,0:T(8,128)(2,1)S(1)}, u32[]{:S(2)}, u32[]{:S(2)}) collective-permute-start(bf16[256,256]{1,0:T(8,128)(2,1)S(1)} %get-tuple-element.33.refs_3_.refs_4_), channel_id=1, source_target_pairs={{0,246},{1,247},{2,244},{3,245},{4,250},{5,251},{6,248},{7,249},{8... | collective-permute-start | bytes 393224 | tf_op jit(solution)/shard_map/ppermute | solution.py:199
  21.9 2.5 %collective-permute-start.4 = (f32[8,2048]{1,0:T(8,128)S(1)}, f32[8,2048]{1,0:T(8,128)S(1)}, u32[]{:S(2)}, u32[]{:S(2)}) collective-permute-start(f32[8,2048]{1,0:T(8,128)S(1)} %get-tuple-element.48.refs_0_.refs_6_), channel_id=1, source_target_pairs={{0,1},{1,0},{2,3},{3,2},{4,5},{5,4},{6,7},{7,6},{8,9},{9,8},{10,11... | collective-permute-start | bytes 196616 | tf_op jit(solution)/shard_map/ppermute | solution.py:202
  25.1 4.5 %collective-permute-start.5 = (bf16[128,256]{1,0:T(8,128)(2,1)S(1)}, bf16[128,256]{1,0:T(8,128)(2,1)S(1)}, u32[]{:S(2)}, u32[]{:S(2)}) collective-permute-start(bf16[128,256]{1,0:T(8,128)(2,1)S(1)} %get-tuple-element.40), channel_id=1, source_target_pairs={{0,2},{1,3},{2,0},{3,1},{4,6},{5,7},{6,4},{7,5},{8,10},{9,11},{10,... | collective-permute-start | bytes 196616 | tf_op jit(solution)/shard_map/ppermute | solution.py:202
  29.0 5.8 %collective-permute-start.8 = (bf16[256,256]{1,0:T(8,128)(2,1)S(1)}, bf16[256,256]{1,0:T(8,128)(2,1)S(1)}, u32[]{:S(2)}, u32[]{:S(2)}) collective-permute-start(bf16[256,256]{1,0:T(8,128)(2,1)S(1)} %get-tuple-element.46), channel_id=1, source_target_pairs={{0,2},{1,3},{2,0},{3,1},{4,6},{5,7},{6,4},{7,5},{8,10},{9,11},{10,... | collective-permute-start | bytes 393224 | tf_op jit(solution)/shard_map/ppermute | solution.py:202
  29.7 9.9 %collective-permute-start.7 = (bf16[128,256]{1,0:T(8,128)(2,1)S(1)}, bf16[128,256]{1,0:T(8,128)(2,1)S(1)}, u32[]{:S(2)}, u32[]{:S(2)}) collective-permute-start(bf16[128,256]{1,0:T(8,128)(2,1)S(1)} %add_convert_fusion.2), channel_id=1, source_target_pairs={{0,14},{1,15},{2,12},{3,13},{4,18},{5,19},{6,16},{7,17},{8,22},{9,... | collective-permute-start | bytes 196616 | tf_op jit(solution)/shard_map/ppermute | solution.py:199
  30.8 5.9 %collective-permute-start.6 = (bf16[128,256]{1,0:T(8,128)(2,1)S(1)}, bf16[128,256]{1,0:T(8,128)(2,1)S(1)}, u32[]{:S(2)}, u32[]{:S(2)}) collective-permute-start(bf16[128,256]{1,0:T(8,128)(2,1)S(1)} %get-tuple-element.52), channel_id=1, source_target_pairs={{0,2},{1,3},{2,0},{3,1},{4,6},{5,7},{6,4},{7,5},{8,10},{9,11},{10,... | collective-permute-start | bytes 196616 | tf_op jit(solution)/shard_map/ppermute | solution.py:202
  32.4 11.6 %collective-permute-start.11 = (bf16[512,256]{1,0:T(8,128)(2,1)S(1)}, bf16[512,256]{1,0:T(8,128)(2,1)S(1)}, u32[]{:S(2)}, u32[]{:S(2)}) collective-permute-start(bf16[512,256]{1,0:T(8,128)(2,1)S(1)} %shard_map.86), channel_id=1, source_target_pairs={{0,1},{1,0},{2,3},{3,2},{4,5},{5,4},{6,7},{7,6},{8,9},{9,8},{10,11... | collective-permute-start | bytes 786440 | tf_op jit(solution)/shard_map/ppermute | solution.py:202
  34.9 8.7 %collective-permute-start.9 = (bf16[128,256]{1,0:T(8,128)(2,1)S(1)}, bf16[128,256]{1,0:T(8,128)(2,1)S(1)}, u32[]{:S(2)}, u32[]{:S(2)}) collective-permute-start(bf16[128,256]{1,0:T(8,128)(2,1)S(1)} %get-tuple-element.59), channel_id=1, source_target_pairs={{0,6},{1,7},{2,4},{3,5},{4,10},{5,11},{6,8},{7,9},{8,14},{9,15},{1... | collective-permute-start | bytes 196616 | tf_op jit(solution)/shard_map/ppermute | solution.py:199
  36.7 7.2 %collective-permute-start.10 = (bf16[128,256]{1,0:T(8,128)(2,1)S(1)}, bf16[128,256]{1,0:T(8,128)(2,1)S(1)}, u32[]{:S(2)}, u32[]{:S(2)}) collective-permute-start(bf16[128,256]{1,0:T(8,128)(2,1)S(1)} %get-tuple-element.60), channel_id=1, source_target_pairs={{0,8},{1,9},{2,10},{3,11},{4,12},{5,13},{6,14},{7,15},{8,16},{9,17... | collective-permute-start | bytes 196616 | tf_op jit(solution)/shard_map/ppermute | solution.py:199

commit v6 on v4

--- a/solution.py
+++ b/solution.py
@@ -121,9 +121,9 @@
         stats_ref[2:3, cols] = delta
 
 
-def grads_body(pairs, own_ref, mate_ref, qa_ref, qb_ref, *refs):
+def grads_body(pairs, split, own_ref, mate_ref, qa_ref, qb_ref, *refs):
     kept, refs = refs[: 3 * pairs], refs[3 * pairs :]
-    ds_refs, keep_refs, give_ref = refs[:pairs], refs[pairs : 2 * pairs], refs[2 * pairs]
+    ds_refs, outs = refs[:pairs], refs[pairs:]
     toks = qa_ref.shape[0]
     sums = [None] * pairs
     for head in range(HEADS_CHIP):
@@ -153,8 +153,11 @@
     for i in range(pairs):
         both = jnp.concatenate([sums[i][0] * SCALE, sums[i][1]], axis=1)
         half = both.shape[0] // 2
-        keep_refs[i][...] = both[:half]
-        give_ref[i * half : (i + 1) * half, :] = both[half:].astype(BF16)
+        if split:
+            outs[i][...] = both[:half]
+            outs[pairs][i * half : (i + 1) * half, :] = both[half:].astype(BF16)
+        else:
+            outs[i][...] = both.astype(outs[i].dtype)
 
 
 def query_body(heads, parts, *refs):
@@ -240,28 +243,39 @@
         kept[k] = (p, dp, stats)
     stats_mate = swap(stats, 1)
     ds = {}
-    pushed = {}
-    seen = stats
-    for pair in ((3, 1), (2, 0)):
-        outs = call(
-            lambda *refs: grads_body(2, *refs),
-            [vmem((half, lanes), BF16)] * 2
-            + [vmem((half // 2, 2 * HD), F32)] * 2
-            + [vmem((half, 2 * HD), BF16)],
-            (seen, stats_mate, qg, qg_mate, *kept[pair[0]], *kept[pair[1]]),
-            flops=2 * flops,
+    quarter = half // 2
+
+    def grads(ks, split, outs, seen):
+        got = call(
+            lambda *refs: grads_body(len(ks), split, *refs),
+            [vmem((half, lanes), BF16)] * len(ks) + outs,
+            (seen, stats_mate, qg, qg_mate, *(v for k in ks for v in kept[k])),
+            flops=len(ks) * flops,
         )
-        ds[pair[0]], ds[pair[1]] = outs[:2]
-        keep, give = outs[2:4], outs[4]
-        got = swap(give, 2)
-        for i, k in enumerate(pair):
-            here = got[i * half // 2 : (i + 1) * half // 2].astype(F32)
-            if k:
-                pushed[k] = route((keep[i] + here).astype(BF16), k)
-            else:
-                mine = keep[i] + here
-
-    part = pushed[3].astype(F32) + pushed[1].astype(F32)
+        for k, value in zip(ks, got):
+            ds[k] = value
+        return got[len(ks) :]
+
+    keep3, keep2, give = grads(
+        (3, 2),
+        True,
+        [vmem((quarter, 2 * HD), F32)] * 2 + [vmem((half, 2 * HD), BF16)],
+        stats,
+    )
+    got = swap(give, 2)
+    seen, _ = lax.optimization_barrier((stats, give))
+    [one] = grads((1,), False, [vmem((half, 2 * HD), BF16)], seen)
+    one_got = route(one, 1)
+    seen, _ = lax.optimization_barrier((stats, one))
+    [zero] = grads((0,), False, [vmem((half, 2 * HD), F32)], seen)
+    low3 = (keep3 + got[:quarter].astype(F32)).astype(BF16)
+    low2 = (keep2 + got[quarter:].astype(F32)).astype(BF16)
+    pushed = [route(low3, 3), route(low2, 2)]
+    one_got, *_ = lax.optimization_barrier((one_got, low3, low2))
+    mine = zero[:quarter] + one_got[:quarter].astype(F32)
+    mine_got = swap((zero[quarter:] + one_got[quarter:].astype(F32)).astype(BF16), 2)
+
+    part = pushed[0].astype(F32) + pushed[1].astype(F32)
 
     def query_part(heads, kind):
         parts = [len(window[k]) for k in range(SPAN)]
@@ -279,7 +293,7 @@
             finish_body,
             [jax.ShapeDtypeStruct((toks, wide), BF16)]
             + [jax.ShapeDtypeStruct((half // 2, HD), BF16)] * 2,
-            (mine, part, *(pushed[k] for k in (2,)), dq_own, dq_got),
+            (mine, mine_got, part, dq_own, dq_got),
         )
     )
 

time: 45.8 us -> 44.8 us (0.978)
  waiting for transfers between devices: 13.1 us -> 12.5 us
  starting transfers between devices: 21.7 us -> 21.1 us
    ppermute x6, starting transfers between devices: 13.5 us -> 12.2 us  [route(): return lax.ppermute(value, ('blk', 'head'), pairs)]
    ppermute x5, starting transfers between devices: 8.27 us -> 8.96 us  [swap(): return lax.ppermute(value, 'head', [(h, h ^ bit) for h in range(heads)])]
    ppermute x6, waiting for transfers between devices: 12.2 us -> 11.6 us  [route(): return lax.ppermute(value, ('blk', 'head'), pairs)]
    pallas_call x10 -> x11, Pallas kernels: 8.77 us -> 8.86 us  [call(): pl.pallas_call(body, out_shape=outs, in_specs=[whole] * len(args), out_sp...]
  transfers between devices with their start and end apart: 11 -> 11, of which waited for: 5 -> 6; matrix products, arithmetic and copies ran while one was open for 0% -> 0% of each run, Pallas kernels for 12% -> 13%
where the time goes in v6:
time: 44.8 us; the launch traced here: 44.6 us
  starting transfers between devices  21.1 us (47%)
  waiting for transfers between devices  12.5 us (28%)
  Pallas kernels  10.1 us (23%)
  between operations  0.78 us (2%)
    ppermute x6, starting transfers between devices, route(): return lax.ppermute(value, ('blk', 'head'), pairs)  12.2 us
    ppermute x6, waiting for transfers between devices, route(): return lax.ppermute(value, ('blk', 'head'), pairs)  11.6 us
    ppermute x5, starting transfers between devices, swap(): return lax.ppermute(value, 'head', [(h, h ^ bit) for h in range(heads)])  8.96 us
    pallas_call x11, Pallas kernels, call(): pl.pallas_call(body, out_shape=outs, in_specs=[whole] * len(args), out_sp...  8.86 us
    pallas_call x1, Pallas kernels, shards(): pl.pallas_call(prepare, out_shape=[vmem((toks, 2 * wide), BF16), vmem((ha...  1.21 us
    ppermute x5, waiting for transfers between devices, swap(): return lax.ppermute(value, 'head', [(h, h ^ bit) for h in range(heads)])  0.91 us
  transfers between devices with their start and end apart: 11, of which 6 were waited for; matrix products, arithmetic and copies ran while one was open for 0% of the time, Pallas kernels for 13%

profile of v6, /device:TPU:1, one launch (start us, length us, event | category | flops | bytes accessed | tf_op | source)
XLA Modules:
  0.0 44.6 jit_solution(9885824588573788236)
XLA Ops:
  0.6 1.2 %shard_map.76 = (bf16[512,512]{1,0:T(8,128)(2,1)S(1)}, bf16[256,256]{1,0:T(8,128)(2,1)S(1)}, s32[24,128]{1,0:T(8,128)S(1)}) custom-call(bf16[512,256]{1,0:T(8,128)(2,1)} %q_hbm.1, bf16[512,256]{1,0:T(8,128)(2,1)} %g_hbm.1, bf16[512,128]{1,0:T(8,128)(2,1)} %k_hbm.1, bf16[512,128]{1,0:T(8,128)(2,1)} %v_hbm.1, s32[256,128]{1,0:T(8,128)} %bitcast.1), custom_call_target="tpu_custom_call" | custom-call | tf_op jit(solution)/shard_map/pallas_call | solution.py:214
  1.8 3.3 %collective-permute-start = (bf16[512,512]{1,0:T(8,128)(2,1)S(1)}, bf16[512,512]{1,0:T(8,128)(2,1)S(1)}, u32[]{:S(2)}, u32[]{:S(2)}) collective-permute-start(bf16[512,512]{1,0:T(8,128)(2,1)S(1)} %get-tuple-element.31.refs_1_.refs_2_), channel_id=1, source_target_pairs={{0,1},{1,0},{2,3},{3,2},{4,5},{5,4},{6,7},{7,6},{8,9},{9,8},{10,11... | collective-permute-start | bytes 1572872 | tf_op jit(solution)/shard_map/ppermute | solution.py:205
  5.2 6.0 %collective-permute-start.3 = (bf16[256,256]{1,0:T(8,128)(2,1)S(1)}, bf16[256,256]{1,0:T(8,128)(2,1)S(1)}, u32[]{:S(2)}, u32[]{:S(2)}) collective-permute-start(bf16[256,256]{1,0:T(8,128)(2,1)S(1)} %get-tuple-element.32.refs_3_.refs_4_), channel_id=1, source_target_pairs={{0,248},{1,249},{2,250},{3,251},{4,252},{5,253},{6,254},{7,255},{8... | collective-permute-start | bytes 393224 | tf_op jit(solution)/shard_map/ppermute | solution.py:202
  11.2 3.2 %collective-permute-start.2 = (bf16[256,256]{1,0:T(8,128)(2,1)S(1)}, bf16[256,256]{1,0:T(8,128)(2,1)S(1)}, u32[]{:S(2)}, u32[]{:S(2)}) collective-permute-start(bf16[256,256]{1,0:T(8,128)(2,1)S(1)} %get-tuple-element.32.refs_3_.refs_4_), channel_id=1, source_target_pairs={{0,254},{1,255},{2,252},{3,253},{4,2},{5,3},{6,0},{7,1},{8,6},{9,7... | collective-permute-start | bytes 393224 | tf_op jit(solution)/shard_map/ppermute | solution.py:202
  14.4 0.4 %collective-permute-start.1 = (bf16[256,256]{1,0:T(8,128)(2,1)S(1)}, bf16[256,256]{1,0:T(8,128)(2,1)S(1)}, u32[]{:S(2)}, u32[]{:S(2)}) collective-permute-start(bf16[256,256]{1,0:T(8,128)(2,1)S(1)} %get-tuple-element.32.refs_3_.refs_4_), channel_id=1, source_target_pairs={{0,246},{1,247},{2,244},{3,245},{4,250},{5,251},{6,248},{7,249},{8... | collective-permute-start | bytes 393224 | tf_op jit(solution)/shard_map/ppermute | solution.py:202
  14.9 0.2 shard_map.77.refs_0_
  15.1 0.0 collective-permute-done.refs_2_.refs_3_
  15.1 0.9 %shard_map.78 = (f32[256,2048]{1,0:T(8,128)S(1)}, f32[256,2048]{1,0:T(8,128)S(1)}, f32[8,2048]{1,0:T(8,128)S(1)}) custom-call(f32[1024,512]{1,0:T(8,128)S(1)} %shard_map.77.refs_0_, bf16[512,512]{1,0:T(8,128)(2,1)S(1)} %get-tuple-element.31.refs_1_.refs_2_, bf16[512,512]{1,0:T(8,128)(2,1)S(1)} %collective-permute-done.refs_2_.refs_3_, ...), custom_call_target="tpu_custom_call" | custom-call | flops 268435456 | bytes 1048576 | tf_op jit(solution)/shard_map/pallas_call | solution.py:28
  16.0 0.0 collective-permute-done.3.refs_3_.refs_6_
  16.0 0.9 %shard_map.79 = (f32[256,2048]{1,0:T(8,128)S(1)}, f32[256,2048]{1,0:T(8,128)S(1)}, f32[8,2048]{1,0:T(8,128)S(1)}) custom-call(f32[1024,512]{1,0:T(8,128)S(1)} %shard_map.77.refs_0_, bf16[512,512]{1,0:T(8,128)(2,1)S(1)} %get-tuple-element.31.refs_1_.refs_2_, bf16[512,512]{1,0:T(8,128)(2,1)S(1)} %collective-permute-done.refs_2_.refs_3_, ...), custom_call_target="tpu_custom_call" | custom-call | flops 268435456 | bytes 1048576 | tf_op jit(solution)/shard_map/pallas_call | solution.py:28
  16.9 0.4 collective-permute-done.2.refs_3_.refs_5_
  17.3 0.9 %shard_map.80 = (f32[256,2048]{1,0:T(8,128)S(1)}, f32[256,2048]{1,0:T(8,128)S(1)}, f32[8,2048]{1,0:T(8,128)S(1)}) custom-call(f32[1024,512]{1,0:T(8,128)S(1)} %shard_map.77.refs_0_, bf16[512,512]{1,0:T(8,128)(2,1)S(1)} %get-tuple-element.31.refs_1_.refs_2_, bf16[512,512]{1,0:T(8,128)(2,1)S(1)} %collective-permute-done.refs_2_.refs_3_, ...), custom_call_target="tpu_custom_call" | custom-call | flops 268435456 | bytes 1048576 | tf_op jit(solution)/shard_map/pallas_call | solution.py:28
  18.2 2.7 %collective-permute-done.1.refs_3_.refs_7_ = bf16[256,256]{1,0:T(8,128)(2,1)S(1)} collective-permute-done((bf16[256,256]{1,0:T(8,128)(2,1)S(1)}, bf16[256,256]{1,0:T(8,128)(2,1)S(1)}, u32[]{:S(2)}, u32[]{:S(2)}) %collective-permute-start.1) | collective-permute-done | bytes 131104 | tf_op jit(solution)/shard_map/ppermute | solution.py:202
  20.9 0.9 %shard_map.81 = (f32[256,2048]{1,0:T(8,128)S(1)}, f32[256,2048]{1,0:T(8,128)S(1)}, f32[8,2048]{1,0:T(8,128)S(1)}) custom-call(f32[1024,512]{1,0:T(8,128)S(1)} %shard_map.77.refs_0_, bf16[512,512]{1,0:T(8,128)(2,1)S(1)} %get-tuple-element.31.refs_1_.refs_2_, bf16[512,512]{1,0:T(8,128)(2,1)S(1)} %collective-permute-done.refs_2_.refs_3_, ...), custom_call_target="tpu_custom_call" | custom-call | flops 268435456 | bytes 1048576 | tf_op jit(solution)/shard_map/pallas_call | solution.py:28
  21.9 1.6 %collective-permute-start.4 = (f32[8,2048]{1,0:T(8,128)S(1)}, f32[8,2048]{1,0:T(8,128)S(1)}, u32[]{:S(2)}, u32[]{:S(2)}) collective-permute-start(f32[8,2048]{1,0:T(8,128)S(1)} %get-tuple-element.46.refs_0_.refs_6_), channel_id=1, source_target_pairs={{0,1},{1,0},{2,3},{3,2},{4,5},{5,4},{6,7},{7,6},{8,9},{9,8},{10,11... | collective-permute-start | bytes 196616 | tf_op jit(solution)/shard_map/ppermute | solution.py:205
  23.4 0.9 %collective-permute-done.4.refs_1_ = f32[8,2048]{1,0:T(8,128)S(1)} collective-permute-done((f32[8,2048]{1,0:T(8,128)S(1)}, f32[8,2048]{1,0:T(8,128)S(1)}, u32[]{:S(2)}, u32[]{:S(2)}) %collective-permute-start.4) | collective-permute-done | bytes 65568 | tf_op jit(solution)/shard_map/ppermute | solution.py:205
  24.3 1.5 %shard_map.82 = (bf16[256,2048]{1,0:T(8,128)(2,1)S(1)}, bf16[256,2048]{1,0:T(8,128)(2,1)S(1)}, f32[128,256]{1,0:T(8,128)S(1)}, f32[128,256]{1,0:T(8,128)S(1)}, bf16[256,256]{1,0:T(8,128)(2,1)S(1)}) custom-call(f32[8,2048]{1,0:T(8,128)S(1)} %get-tuple-element.46.refs_0_.refs_6_, f32[8,2048]{1,0:T(8,128)S(1)} %collective-permute-done.4.refs_1_, ...), custom_call_target="tpu_custom_call" | custom-call | flops 536870912 | bytes 1048576 | tf_op jit(solution)/shard_map/pallas_call | solution.py:28
  25.8 2.4 %collective-permute-start.6 = (bf16[256,256]{1,0:T(8,128)(2,1)S(1)}, bf16[256,256]{1,0:T(8,128)(2,1)S(1)}, u32[]{:S(2)}, u32[]{:S(2)}) collective-permute-start(bf16[256,256]{1,0:T(8,128)(2,1)S(1)} %get-tuple-element.41), channel_id=1, source_target_pairs={{0,2},{1,3},{2,0},{3,1},{4,6},{5,7},{6,4},{7,5},{8,10},{9,11},{10,... | collective-permute-start | bytes 393224 | tf_op jit(solution)/shard_map/ppermute | solution.py:205
  28.2 0.8 %shard_map.83 = (bf16[256,2048]{1,0:T(8,128)(2,1)S(1)}, bf16[256,256]{1,0:T(8,128)(2,1)S(1)}) custom-call(f32[8,2048]{1,0:T(8,128)S(1)} %get-tuple-element.46.refs_0_.refs_6_, f32[8,2048]{1,0:T(8,128)S(1)} %collective-permute-done.4.refs_1_, bf16[512,512]{1,0:T(8,128)(2,1)S(1)} %get-tuple-element.31.refs_1_.refs_2_, ...), custom_call_target="tpu_custom_call" | custom-call | flops 268435456 | bytes 1048576 | tf_op jit(solution)/shard_map/pallas_call | solution.py:28
  29.0 2.1 %collective-permute-start.5 = (bf16[256,256]{1,0:T(8,128)(2,1)S(1)}, bf16[256,256]{1,0:T(8,128)(2,1)S(1)}, u32[]{:S(2)}, u32[]{:S(2)}) collective-permute-start(bf16[256,256]{1,0:T(8,128)(2,1)S(1)} %get-tuple-element.45), channel_id=1, source_target_pairs={{0,6},{1,7},{2,4},{3,5},{4,10},{5,11},{6,8},{7,9},{8,14},{9,15},{1... | collective-permute-start | bytes 393224 | tf_op jit(solution)/shard_map/ppermute | solution.py:202
  31.1 0.8 %shard_map.84 = (bf16[256,2048]{1,0:T(8,128)(2,1)S(1)}, f32[256,256]{1,0:T(8,128)S(1)}) custom-call(f32[8,2048]{1,0:T(8,128)S(1)} %get-tuple-element.46.refs_0_.refs_6_, f32[8,2048]{1,0:T(8,128)S(1)} %collective-permute-done.4.refs_1_, bf16[512,512]{1,0:T(8,128)(2,1)S(1)} %get-tuple-element.31.refs_1_.refs_2_, ...), custom_call_target="tpu_custom_call" | custom-call | flops 268435456 | bytes 1048576 | tf_op jit(solution)/shard_map/pallas_call | solution.py:28
  31.9 0.6 %shard_map.86 = bf16[512,256]{1,0:T(8,128)(2,1)S(1)} custom-call(bf16[256,2048]{1,0:T(8,128)(2,1)S(1)} %get-tuple-element.53.refs_0_, bf16[256,2048]{1,0:T(8,128)(2,1)S(1)} %get-tuple-element.54.refs_1_, bf16[256,2048]{1,0:T(8,128)(2,1)S(1)} %get-tuple-element.55.refs_2_, bf16[256,2048]{1,0:T(8,128)(2,1)S(1)} %get-tuple-element.56.refs_3_, ...), custom_call_target="tpu_custom_call" | custom-call | flops 268435456 | bytes 1048576 | tf_op jit(solution)/shard_map/pallas_call | solution.py:28
  32.5 0.7 %collective-permute-start.10 = (bf16[512,256]{1,0:T(8,128)(2,1)S(1)}, bf16[512,256]{1,0:T(8,128)(2,1)S(1)}, u32[]{:S(2)}, u32[]{:S(2)}) collective-permute-start(bf16[512,256]{1,0:T(8,128)(2,1)S(1)} %shard_map.86), channel_id=1, source_target_pairs={{0,1},{1,0},{2,3},{3,2},{4,5},{5,4},{6,7},{7,6},{8,9},{9,8},{10,11... | collective-permute-start | bytes 786440 | tf_op jit(solution)/shard_map/ppermute | solution.py:205
  33.2 0.6 %shard_map.85.refs_3_ = f32[512,256]{1,0:T(8,128)S(1)} custom-call(bf16[256,2048]{1,0:T(8,128)(2,1)S(1)} %get-tuple-element.53.refs_0_, bf16[256,2048]{1,0:T(8,128)(2,1)S(1)} %get-tuple-element.54.refs_1_, bf16[256,2048]{1,0:T(8,128)(2,1)S(1)} %get-tuple-element.55.refs_2_, bf16[256,2048]{1,0:T(8,128)(2,1)S(1)} %get-tuple-element.56.refs_3_, ...), custom_call_target="tpu_custom_call" | custom-call | flops 268435456 | bytes 1048576 | tf_op jit(solution)/shard_map/pallas_call | solution.py:28
  33.8 0.1 collective-permute-start.9
  33.9 0.3 collective-permute-start.8
  34.2 5.4 %collective-permute-done.5 = bf16[256,256]{1,0:T(8,128)(2,1)S(1)} collective-permute-done((bf16[256,256]{1,0:T(8,128)(2,1)S(1)}, bf16[256,256]{1,0:T(8,128)(2,1)S(1)}, u32[]{:S(2)}, u32[]{:S(2)}) %collective-permute-start.5) | collective-permute-done | bytes 131104 | tf_op jit(solution)/shard_map/ppermute | solution.py:202
  39.7 1.0 %collective-permute-start.7 = (bf16[128,256]{1,0:T(8,128)(2,1)S(1)}, bf16[128,256]{1,0:T(8,128)(2,1)S(1)}, u32[]{:S(2)}, u32[]{:S(2)}) collective-permute-start(bf16[128,256]{1,0:T(8,128)(2,1)S(1)} %get-tuple-element.57), channel_id=1, source_target_pairs={{0,2},{1,3},{2,0},{3,1},{4,6},{5,7},{6,4},{7,5},{8,10},{9,11},{10,... | collective-permute-start | bytes 196616 | tf_op jit(solution)/shard_map/ppermute | solution.py:205
  40.6 1.3 %collective-permute-done.9 = bf16[128,256]{1,0:T(8,128)(2,1)S(1)} collective-permute-done((bf16[128,256]{1,0:T(8,128)(2,1)S(1)}, bf16[128,256]{1,0:T(8,128)(2,1)S(1)}, u32[]{:S(2)}, u32[]{:S(2)}) %collective-permute-start.9) | collective-permute-done | bytes 65568 | tf_op jit(solution)/shard_map/ppermute | solution.py:202
  41.9 1.9 %collective-permute-done.8 = bf16[128,256]{1,0:T(8,128)(2,1)S(1)} collective-permute-done((bf16[128,256]{1,0:T(8,128)(2,1)S(1)}, bf16[128,256]{1,0:T(8,128)(2,1)S(1)}, u32[]{:S(2)}, u32[]{:S(2)}) %collective-permute-start.8) | collective-permute-done | bytes 65568 | tf_op jit(solution)/shard_map/ppermute | solution.py:202
  43.8 0.0 collective-permute-done.7.refs_1_
  43.8 0.8 %shard_map.87 = (bf16[512,256]{1,0:T(8,128)(2,1)}, bf16[128,128]{1,0:T(8,128)(2,1)}, bf16[128,128]{1,0:T(8,128)(2,1)}) custom-call(f32[128,256]{1,0:T(8,128)S(1)} %get-tuple-element.58.refs_0_, bf16[128,256]{1,0:T(8,128)(2,1)S(1)} %collective-permute-done.7.refs_1_, f32[128,256]{1,0:T(8,128)S(1)} %convert_add_fusion.refs_2_, ...), custom_call_target="tpu_custom_call" | custom-call | bytes 1048576 | tf_op jit(solution)/shard_map/pallas_call | solution.py:28
  (5 shorter events, 0.1 us)
Async XLA Ops:
  1.8 13.2 %collective-permute-start = (bf16[512,512]{1,0:T(8,128)(2,1)S(1)}, bf16[512,512]{1,0:T(8,128)(2,1)S(1)}, u32[]{:S(2)}, u32[]{:S(2)}) collective-permute-start(bf16[512,512]{1,0:T(8,128)(2,1)S(1)} %get-tuple-element.31.refs_1_.refs_2_), channel_id=1, source_target_pairs={{0,1},{1,0},{2,3},{3,2},{4,5},{5,4},{6,7},{7,6},{8,9},{9,8},{10,11... | collective-permute-start | bytes 1572872 | tf_op jit(solution)/shard_map/ppermute | solution.py:205
  5.2 10.8 %collective-permute-start.3 = (bf16[256,256]{1,0:T(8,128)(2,1)S(1)}, bf16[256,256]{1,0:T(8,128)(2,1)S(1)}, u32[]{:S(2)}, u32[]{:S(2)}) collective-permute-start(bf16[256,256]{1,0:T(8,128)(2,1)S(1)} %get-tuple-element.32.refs_3_.refs_4_), channel_id=1, source_target_pairs={{0,248},{1,249},{2,250},{3,251},{4,252},{5,253},{6,254},{7,255},{8... | collective-permute-start | bytes 393224 | tf_op jit(solution)/shard_map/ppermute | solution.py:202
  11.2 6.1 %collective-permute-start.2 = (bf16[256,256]{1,0:T(8,128)(2,1)S(1)}, bf16[256,256]{1,0:T(8,128)(2,1)S(1)}, u32[]{:S(2)}, u32[]{:S(2)}) collective-permute-start(bf16[256,256]{1,0:T(8,128)(2,1)S(1)} %get-tuple-element.32.refs_3_.refs_4_), channel_id=1, source_target_pairs={{0,254},{1,255},{2,252},{3,253},{4,2},{5,3},{6,0},{7,1},{8,6},{9,7... | collective-permute-start | bytes 393224 | tf_op jit(solution)/shard_map/ppermute | solution.py:202
  14.4 6.5 %collective-permute-start.1 = (bf16[256,256]{1,0:T(8,128)(2,1)S(1)}, bf16[256,256]{1,0:T(8,128)(2,1)S(1)}, u32[]{:S(2)}, u32[]{:S(2)}) collective-permute-start(bf16[256,256]{1,0:T(8,128)(2,1)S(1)} %get-tuple-element.32.refs_3_.refs_4_), channel_id=1, source_target_pairs={{0,246},{1,247},{2,244},{3,245},{4,250},{5,251},{6,248},{7,249},{8... | collective-permute-start | bytes 393224 | tf_op jit(solution)/shard_map/ppermute | solution.py:202
  21.9 2.5 %collective-permute-start.4 = (f32[8,2048]{1,0:T(8,128)S(1)}, f32[8,2048]{1,0:T(8,128)S(1)}, u32[]{:S(2)}, u32[]{:S(2)}) collective-permute-start(f32[8,2048]{1,0:T(8,128)S(1)} %get-tuple-element.46.refs_0_.refs_6_), channel_id=1, source_target_pairs={{0,1},{1,0},{2,3},{3,2},{4,5},{5,4},{6,7},{7,6},{8,9},{9,8},{10,11... | collective-permute-start | bytes 196616 | tf_op jit(solution)/shard_map/ppermute | solution.py:205
  25.8 7.9 %collective-permute-start.6 = (bf16[256,256]{1,0:T(8,128)(2,1)S(1)}, bf16[256,256]{1,0:T(8,128)(2,1)S(1)}, u32[]{:S(2)}, u32[]{:S(2)}) collective-permute-start(bf16[256,256]{1,0:T(8,128)(2,1)S(1)} %get-tuple-element.41), channel_id=1, source_target_pairs={{0,2},{1,3},{2,0},{3,1},{4,6},{5,7},{6,4},{7,5},{8,10},{9,11},{10,... | collective-permute-start | bytes 393224 | tf_op jit(solution)/shard_map/ppermute | solution.py:205
  29.0 10.6 %collective-permute-start.5 = (bf16[256,256]{1,0:T(8,128)(2,1)S(1)}, bf16[256,256]{1,0:T(8,128)(2,1)S(1)}, u32[]{:S(2)}, u32[]{:S(2)}) collective-permute-start(bf16[256,256]{1,0:T(8,128)(2,1)S(1)} %get-tuple-element.45), channel_id=1, source_target_pairs={{0,6},{1,7},{2,4},{3,5},{4,10},{5,11},{6,8},{7,9},{8,14},{9,15},{1... | collective-permute-start | bytes 393224 | tf_op jit(solution)/shard_map/ppermute | solution.py:202
  32.5 11.3 %collective-permute-start.10 = (bf16[512,256]{1,0:T(8,128)(2,1)S(1)}, bf16[512,256]{1,0:T(8,128)(2,1)S(1)}, u32[]{:S(2)}, u32[]{:S(2)}) collective-permute-start(bf16[512,256]{1,0:T(8,128)(2,1)S(1)} %shard_map.86), channel_id=1, source_target_pairs={{0,1},{1,0},{2,3},{3,2},{4,5},{5,4},{6,7},{7,6},{8,9},{9,8},{10,11... | collective-permute-start | bytes 786440 | tf_op jit(solution)/shard_map/ppermute | solution.py:205
  33.8 8.1 %collective-permute-start.9 = (bf16[128,256]{1,0:T(8,128)(2,1)S(1)}, bf16[128,256]{1,0:T(8,128)(2,1)S(1)}, u32[]{:S(2)}, u32[]{:S(2)}) collective-permute-start(bf16[128,256]{1,0:T(8,128)(2,1)S(1)} %get-tuple-element.59), channel_id=1, source_target_pairs={{0,8},{1,9},{2,10},{3,11},{4,12},{5,13},{6,14},{7,15},{8,16},{9,17... | collective-permute-start | bytes 196616 | tf_op jit(solution)/shard_map/ppermute | solution.py:202
  33.9 9.9 %collective-permute-start.8 = (bf16[128,256]{1,0:T(8,128)(2,1)S(1)}, bf16[128,256]{1,0:T(8,128)(2,1)S(1)}, u32[]{:S(2)}, u32[]{:S(2)}) collective-permute-start(bf16[128,256]{1,0:T(8,128)(2,1)S(1)} %get-tuple-element.60), channel_id=1, source_target_pairs={{0,14},{1,15},{2,12},{3,13},{4,18},{5,19},{6,16},{7,17},{8,22},{9,... | collective-permute-start | bytes 196616 | tf_op jit(solution)/shard_map/ppermute | solution.py:202
  39.7 4.2 %collective-permute-start.7 = (bf16[128,256]{1,0:T(8,128)(2,1)S(1)}, bf16[128,256]{1,0:T(8,128)(2,1)S(1)}, u32[]{:S(2)}, u32[]{:S(2)}) collective-permute-start(bf16[128,256]{1,0:T(8,128)(2,1)S(1)} %get-tuple-element.57), channel_id=1, source_target_pairs={{0,2},{1,3},{2,0},{3,1},{4,6},{5,7},{6,4},{7,5},{8,10},{9,11},{10,... | collective-permute-start | bytes 196616 | tf_op jit(solution)/shard_map/ppermute | solution.py:205

commit v7 on v5

--- a/solution.py
+++ b/solution.py
@@ -41,12 +41,10 @@
     return ref[:, at : at + HD]
 
 
-def prepare(q_hbm, g_hbm, k_hbm, v_hbm, pos_hbm, qg_ref, kv_ref, pos_ref, sems):
+def prepare(q_hbm, g_hbm, k_hbm, v_hbm, qg_ref, kv_ref, sems):
     wide = q_hbm.shape[1]
     core = lax.axis_index("head") % 2
     chip = lax.axis_index("head") // 2
-    block = lax.axis_index("blk") * (q_hbm.shape[0] // HD) // 8
-    blocks = pos_hbm.shape[0] // 8
     copies = []
     for half in range(2):
         source = pl.ds(pl.multiple_of((chip ^ half) * 256 + core * 128, 128), 128)
@@ -55,9 +53,6 @@
         copies.append((v_hbm.at[source, :], kv_ref.at[target, pl.ds(HD, HD)]))
     copies.append((q_hbm, qg_ref.at[:, pl.ds(0, wide)]))
     copies.append((g_hbm, qg_ref.at[:, pl.ds(wide, wide)]))
-    for i in range(3):
-        row = pl.multiple_of((block + i) % blocks * 8, 8)
-        copies.append((pos_hbm.at[pl.ds(row, 8), :], pos_ref.at[pl.ds(i * 8, 8), :]))
     copies = [
         pltpu.make_async_copy(source, target, sems.at[i])
         for i, (source, target) in enumerate(copies)
@@ -68,7 +63,18 @@
         copy.wait()
 
 
-def mask_body(pos_ref, bias_ref):
+def mask_body(pos_hbm, bias_ref, pos_ref, sems):
+    block = lax.axis_index("blk") * (bias_ref.shape[1] // HD) // 8
+    blocks = pos_hbm.shape[0] // 8
+    copies = []
+    for i in range(3):
+        row = pl.multiple_of((block + i) % blocks * 8, 8)
+        source, target = pos_hbm.at[pl.ds(row, 8), :], pos_ref.at[pl.ds(i * 8, 8), :]
+        copies.append(pltpu.make_async_copy(source, target, sems.at[i]))
+    for copy in copies:
+        copy.start()
+    for copy in copies:
+        copy.wait()
     core = lax.axis_index("head") % 2
     chip = lax.axis_index("head") // 2
     toks = bias_ref.shape[1]
@@ -208,20 +214,29 @@
     lanes = HEADS_CHIP * toks
     hbm = pl.BlockSpec(memory_space=pltpu.HBM)
     whole = pl.BlockSpec(memory_space=pltpu.VMEM)
-    qg, kv, pos = pl.pallas_call(
+    def fetch(body, outs, scratch, inputs):
+        return pl.pallas_call(
+            body,
+            out_shape=outs,
+            in_specs=[hbm] * len(inputs),
+            out_specs=[whole] * len(outs),
+            scratch_shapes=scratch,
+            compiler_params=pltpu.CompilerParams(vmem_limit_bytes=16 * 1024 * 1024),
+        )(*(pltpu.with_memory_space_constraint(v, pltpu.HBM) for v in inputs))
+
+    qg, kv = fetch(
         prepare,
-        out_shape=[
-            vmem((toks, 2 * wide), BF16),
-            vmem((half, 2 * HD), BF16),
-            vmem((24, HD), jnp.int32),
-        ],
-        in_specs=[hbm] * 5,
-        out_specs=[whole] * 3,
-        scratch_shapes=[pltpu.SemaphoreType.DMA((9,))],
-        compiler_params=pltpu.CompilerParams(vmem_limit_bytes=16 * 1024 * 1024),
-    )(*(pltpu.with_memory_space_constraint(v, pltpu.HBM) for v in (queries, grad_out, key_rows, value_rows, pos)))
+        [vmem((toks, 2 * wide), BF16), vmem((half, 2 * HD), BF16)],
+        [pltpu.SemaphoreType.DMA((6,))],
+        (queries, grad_out, key_rows, value_rows),
+    )
     qg_mate = swap(qg, 1)
-    [bias] = call(mask_body, [vmem((SPAN * half, toks), F32)], (pos,))
+    [bias] = fetch(
+        mask_body,
+        [vmem((SPAN * half, toks), F32)],
+        [pltpu.VMEM((24, HD), jnp.int32), pltpu.SemaphoreType.DMA((3,))],
+        (pos,),
+    )
     window = {0: (kv,)}
     for k in (2, 1, 3):
         window[k] = (route(kv, -k),)

time: 45 us -> 45 us (level)
  waiting for transfers between devices: 11.8 us -> 11 us
  Pallas kernels: 10.1 us -> 10.8 us
    pallas_call x1 -> x2, Pallas kernels: 1.21 us -> 2.13 us  [fetch(): pl.pallas_call(body, out_shape=outs, in_specs=[hbm] * len(inputs), out_sp...]
    ppermute x6, waiting for transfers between devices: 10.3 us -> 9.53 us  [route(): return lax.ppermute(value, ('blk', 'head'), pairs)]
    pallas_call x11 -> x10, Pallas kernels: 8.85 us -> 8.65 us  [call(): pl.pallas_call(body, out_shape=outs, in_specs=[whole] * len(args), out_sp...]
  transfers between devices with their start and end apart: 12 -> 12, of which waited for: 7 -> 6; matrix products, arithmetic and copies ran while one was open for 0% -> 0% of each run, Pallas kernels for 14% -> 16%
where the time goes in v7:
time: 45 us; the launch traced here: 44.7 us
  starting transfers between devices  22 us (49%)
  waiting for transfers between devices  11 us (24%)
  Pallas kernels  10.8 us (24%)
  between operations  0.78 us (2%)
    ppermute x6, starting transfers between devices, route(): return lax.ppermute(value, ('blk', 'head'), pairs)  11.7 us
    ppermute x6, starting transfers between devices, swap(): return lax.ppermute(value, 'head', [(h, h ^ bit) for h in range(heads)])  10.3 us
    ppermute x6, waiting for transfers between devices, route(): return lax.ppermute(value, ('blk', 'head'), pairs)  9.53 us
    pallas_call x10, Pallas kernels, call(): pl.pallas_call(body, out_shape=outs, in_specs=[whole] * len(args), out_sp...  8.65 us
    pallas_call x2, Pallas kernels, fetch(): pl.pallas_call(body, out_shape=outs, in_specs=[hbm] * len(inputs), out_sp...  2.13 us
    ppermute x6, waiting for transfers between devices, swap(): return lax.ppermute(value, 'head', [(h, h ^ bit) for h in range(heads)])  1.49 us
  transfers between devices with their start and end apart: 12, of which 6 were waited for; matrix products, arithmetic and copies ran while one was open for 0% of the time, Pallas kernels for 16%

profile of v7, /device:TPU:1, one launch (start us, length us, event | category | flops | bytes accessed | tf_op | source)
XLA Modules:
  0.0 44.7 jit_solution(4809385830741798508)
XLA Ops:
  0.6 1.2 %shard_map.77 = (bf16[512,512]{1,0:T(8,128)(2,1)S(1)}, bf16[256,256]{1,0:T(8,128)(2,1)S(1)}) custom-call(bf16[512,256]{1,0:T(8,128)(2,1)} %q_hbm.1, bf16[512,256]{1,0:T(8,128)(2,1)} %g_hbm.1, bf16[512,128]{1,0:T(8,128)(2,1)} %k_hbm.1, bf16[512,128]{1,0:T(8,128)(2,1)} %v_hbm.1), custom_call_target="tpu_custom_call" | custom-call | tf_op jit(solution)/shard_map/pallas_call | solution.py:218
  1.8 3.3 %collective-permute-start = (bf16[512,512]{1,0:T(8,128)(2,1)S(1)}, bf16[512,512]{1,0:T(8,128)(2,1)S(1)}, u32[]{:S(2)}, u32[]{:S(2)}) collective-permute-start(bf16[512,512]{1,0:T(8,128)(2,1)S(1)} %get-tuple-element.30.refs_1_.refs_2_), channel_id=1, source_target_pairs={{0,1},{1,0},{2,3},{3,2},{4,5},{5,4},{6,7},{7,6},{8,9},{9,8},{10,11... | collective-permute-start | bytes 1572872 | tf_op jit(solution)/shard_map/ppermute | solution.py:208
  5.1 6.0 %collective-permute-start.3 = (bf16[256,256]{1,0:T(8,128)(2,1)S(1)}, bf16[256,256]{1,0:T(8,128)(2,1)S(1)}, u32[]{:S(2)}, u32[]{:S(2)}) collective-permute-start(bf16[256,256]{1,0:T(8,128)(2,1)S(1)} %get-tuple-element.31.refs_3_.refs_4_), channel_id=1, source_target_pairs={{0,248},{1,249},{2,250},{3,251},{4,252},{5,253},{6,254},{7,255},{8... | collective-permute-start | bytes 393224 | tf_op jit(solution)/shard_map/ppermute | solution.py:205
  11.2 3.2 %collective-permute-start.2 = (bf16[256,256]{1,0:T(8,128)(2,1)S(1)}, bf16[256,256]{1,0:T(8,128)(2,1)S(1)}, u32[]{:S(2)}, u32[]{:S(2)}) collective-permute-start(bf16[256,256]{1,0:T(8,128)(2,1)S(1)} %get-tuple-element.31.refs_3_.refs_4_), channel_id=1, source_target_pairs={{0,254},{1,255},{2,252},{3,253},{4,2},{5,3},{6,0},{7,1},{8,6},{9,7... | collective-permute-start | bytes 393224 | tf_op jit(solution)/shard_map/ppermute | solution.py:205
  14.4 0.4 %collective-permute-start.1 = (bf16[256,256]{1,0:T(8,128)(2,1)S(1)}, bf16[256,256]{1,0:T(8,128)(2,1)S(1)}, u32[]{:S(2)}, u32[]{:S(2)}) collective-permute-start(bf16[256,256]{1,0:T(8,128)(2,1)S(1)} %get-tuple-element.31.refs_3_.refs_4_), channel_id=1, source_target_pairs={{0,246},{1,247},{2,244},{3,245},{4,250},{5,251},{6,248},{7,249},{8... | collective-permute-start | bytes 393224 | tf_op jit(solution)/shard_map/ppermute | solution.py:205
  14.8 1.0 %shard_map.76.refs_0_ = f32[1024,512]{1,0:T(8,128)S(1)} custom-call(s32[256,128]{1,0:T(8,128)} %bitcast.1), custom_call_target="tpu_custom_call" | custom-call | tf_op jit(solution)/shard_map/pallas_call | solution.py:218
  15.8 0.0 collective-permute-done.refs_2_.refs_3_
  15.8 0.9 %shard_map.78 = (f32[256,2048]{1,0:T(8,128)S(1)}, f32[256,2048]{1,0:T(8,128)S(1)}, f32[8,2048]{1,0:T(8,128)S(1)}) custom-call(f32[1024,512]{1,0:T(8,128)S(1)} %shard_map.76.refs_0_, bf16[512,512]{1,0:T(8,128)(2,1)S(1)} %get-tuple-element.30.refs_1_.refs_2_, bf16[512,512]{1,0:T(8,128)(2,1)S(1)} %collective-permute-done.refs_2_.refs_3_, ...), custom_call_target="tpu_custom_call" | custom-call | flops 268435456 | bytes 1048576 | tf_op jit(solution)/shard_map/pallas_call | solution.py:28
  16.7 0.0 collective-permute-done.3.refs_3_.refs_6_
  16.7 0.9 %shard_map.79 = (f32[256,2048]{1,0:T(8,128)S(1)}, f32[256,2048]{1,0:T(8,128)S(1)}, f32[8,2048]{1,0:T(8,128)S(1)}) custom-call(f32[1024,512]{1,0:T(8,128)S(1)} %shard_map.76.refs_0_, bf16[512,512]{1,0:T(8,128)(2,1)S(1)} %get-tuple-element.30.refs_1_.refs_2_, bf16[512,512]{1,0:T(8,128)(2,1)S(1)} %collective-permute-done.refs_2_.refs_3_, ...), custom_call_target="tpu_custom_call" | custom-call | flops 268435456 | bytes 1048576 | tf_op jit(solution)/shard_map/pallas_call | solution.py:28
  17.6 0.9 %shard_map.80 = (f32[256,2048]{1,0:T(8,128)S(1)}, f32[256,2048]{1,0:T(8,128)S(1)}, f32[8,2048]{1,0:T(8,128)S(1)}) custom-call(f32[1024,512]{1,0:T(8,128)S(1)} %shard_map.76.refs_0_, bf16[512,512]{1,0:T(8,128)(2,1)S(1)} %get-tuple-element.30.refs_1_.refs_2_, bf16[512,512]{1,0:T(8,128)(2,1)S(1)} %collective-permute-done.refs_2_.refs_3_, ...), custom_call_target="tpu_custom_call" | custom-call | flops 268435456 | bytes 1048576 | tf_op jit(solution)/shard_map/pallas_call | solution.py:28
  18.6 2.3 %collective-permute-done.1.refs_3_.refs_7_ = bf16[256,256]{1,0:T(8,128)(2,1)S(1)} collective-permute-done((bf16[256,256]{1,0:T(8,128)(2,1)S(1)}, bf16[256,256]{1,0:T(8,128)(2,1)S(1)}, u32[]{:S(2)}, u32[]{:S(2)}) %collective-permute-start.1) | collective-permute-done | bytes 131104 | tf_op jit(solution)/shard_map/ppermute | solution.py:205
  20.9 0.9 %shard_map.81 = (f32[256,2048]{1,0:T(8,128)S(1)}, f32[256,2048]{1,0:T(8,128)S(1)}, f32[8,2048]{1,0:T(8,128)S(1)}) custom-call(f32[1024,512]{1,0:T(8,128)S(1)} %shard_map.76.refs_0_, bf16[512,512]{1,0:T(8,128)(2,1)S(1)} %get-tuple-element.30.refs_1_.refs_2_, bf16[512,512]{1,0:T(8,128)(2,1)S(1)} %collective-permute-done.refs_2_.refs_3_, ...), custom_call_target="tpu_custom_call" | custom-call | flops 268435456 | bytes 1048576 | tf_op jit(solution)/shard_map/pallas_call | solution.py:28
  21.8 1.6 %collective-permute-start.4 = (f32[8,2048]{1,0:T(8,128)S(1)}, f32[8,2048]{1,0:T(8,128)S(1)}, u32[]{:S(2)}, u32[]{:S(2)}) collective-permute-start(f32[8,2048]{1,0:T(8,128)S(1)} %get-tuple-element.46.refs_0_.refs_6_), channel_id=1, source_target_pairs={{0,1},{1,0},{2,3},{3,2},{4,5},{5,4},{6,7},{7,6},{8,9},{9,8},{10,11... | collective-permute-start | bytes 196616 | tf_op jit(solution)/shard_map/ppermute | solution.py:208
  23.4 0.9 %collective-permute-done.4.refs_1_ = f32[8,2048]{1,0:T(8,128)S(1)} collective-permute-done((f32[8,2048]{1,0:T(8,128)S(1)}, f32[8,2048]{1,0:T(8,128)S(1)}, u32[]{:S(2)}, u32[]{:S(2)}) %collective-permute-start.4) | collective-permute-done | bytes 65568 | tf_op jit(solution)/shard_map/ppermute | solution.py:208
  24.3 0.8 %shard_map.82 = (bf16[256,2048]{1,0:T(8,128)(2,1)S(1)}, f32[128,256]{1,0:T(8,128)S(1)}, bf16[128,256]{1,0:T(8,128)(2,1)S(1)}) custom-call(f32[8,2048]{1,0:T(8,128)S(1)} %get-tuple-element.46.refs_0_.refs_6_, f32[8,2048]{1,0:T(8,128)S(1)} %collective-permute-done.4.refs_1_, bf16[512,512]{1,0:T(8,128)(2,1)S(1)} %get-tuple-element.30.refs_1_.refs_2_, ...), custom_call_target="tpu_custom_call" | custom-call | flops 268435456 | bytes 1048576 | tf_op jit(solution)/shard_map/pallas_call | solution.py:28
  25.1 2.4 %collective-permute-start.5 = (bf16[128,256]{1,0:T(8,128)(2,1)S(1)}, bf16[128,256]{1,0:T(8,128)(2,1)S(1)}, u32[]{:S(2)}, u32[]{:S(2)}) collective-permute-start(bf16[128,256]{1,0:T(8,128)(2,1)S(1)} %get-tuple-element.38), channel_id=1, source_target_pairs={{0,2},{1,3},{2,0},{3,1},{4,6},{5,7},{6,4},{7,5},{8,10},{9,11},{10,... | collective-permute-start | bytes 196616 | tf_op jit(solution)/shard_map/ppermute | solution.py:208
  27.5 1.5 %shard_map.83 = (bf16[256,2048]{1,0:T(8,128)(2,1)S(1)}, bf16[256,2048]{1,0:T(8,128)(2,1)S(1)}, f32[128,256]{1,0:T(8,128)S(1)}, f32[128,256]{1,0:T(8,128)S(1)}, bf16[256,256]{1,0:T(8,128)(2,1)S(1)}) custom-call(f32[8,2048]{1,0:T(8,128)S(1)} %get-tuple-element.46.refs_0_.refs_6_, f32[8,2048]{1,0:T(8,128)S(1)} %collective-permute-done.4.refs_1_, ...), custom_call_target="tpu_custom_call" | custom-call | flops 536870912 | bytes 1048576 | tf_op jit(solution)/shard_map/pallas_call | solution.py:28
  29.0 0.1 collective-permute-start.8
  29.1 0.6 %collective-permute-done.5 = bf16[128,256]{1,0:T(8,128)(2,1)S(1)} collective-permute-done((bf16[128,256]{1,0:T(8,128)(2,1)S(1)}, bf16[128,256]{1,0:T(8,128)(2,1)S(1)}, u32[]{:S(2)}, u32[]{:S(2)}) %collective-permute-start.5) | collective-permute-done | bytes 65568 | tf_op jit(solution)/shard_map/ppermute | solution.py:208
  29.7 0.3 collective-permute-start.7
  29.9 0.8 %shard_map.84 = (bf16[256,2048]{1,0:T(8,128)(2,1)S(1)}, f32[128,256]{1,0:T(8,128)S(1)}, bf16[128,256]{1,0:T(8,128)(2,1)S(1)}) custom-call(f32[8,2048]{1,0:T(8,128)S(1)} %get-tuple-element.46.refs_0_.refs_6_, f32[8,2048]{1,0:T(8,128)S(1)} %collective-permute-done.4.refs_1_, bf16[512,512]{1,0:T(8,128)(2,1)S(1)} %get-tuple-element.30.refs_1_.refs_2_, ...), custom_call_target="tpu_custom_call" | custom-call | flops 268435456 | bytes 1048576 | tf_op jit(solution)/shard_map/pallas_call | solution.py:28
  30.7 1.0 %collective-permute-start.6 = (bf16[128,256]{1,0:T(8,128)(2,1)S(1)}, bf16[128,256]{1,0:T(8,128)(2,1)S(1)}, u32[]{:S(2)}, u32[]{:S(2)}) collective-permute-start(bf16[128,256]{1,0:T(8,128)(2,1)S(1)} %get-tuple-element.50), channel_id=1, source_target_pairs={{0,2},{1,3},{2,0},{3,1},{4,6},{5,7},{6,4},{7,5},{8,10},{9,11},{10,... | collective-permute-start | bytes 196616 | tf_op jit(solution)/shard_map/ppermute | solution.py:208
  31.8 0.6 %shard_map.86 = bf16[512,256]{1,0:T(8,128)(2,1)S(1)} custom-call(bf16[256,2048]{1,0:T(8,128)(2,1)S(1)} %get-tuple-element.53.refs_0_, bf16[256,2048]{1,0:T(8,128)(2,1)S(1)} %get-tuple-element.54.refs_1_, bf16[256,2048]{1,0:T(8,128)(2,1)S(1)} %get-tuple-element.55.refs_2_, bf16[256,2048]{1,0:T(8,128)(2,1)S(1)} %get-tuple-element.56.refs_3_, ...), custom_call_target="tpu_custom_call" | custom-call | flops 268435456 | bytes 1048576 | tf_op jit(solution)/shard_map/pallas_call | solution.py:28
  32.3 1.9 %collective-permute-start.11 = (bf16[512,256]{1,0:T(8,128)(2,1)S(1)}, bf16[512,256]{1,0:T(8,128)(2,1)S(1)}, u32[]{:S(2)}, u32[]{:S(2)}) collective-permute-start(bf16[512,256]{1,0:T(8,128)(2,1)S(1)} %shard_map.86), channel_id=1, source_target_pairs={{0,1},{1,0},{2,3},{3,2},{4,5},{5,4},{6,7},{7,6},{8,9},{9,8},{10,11... | collective-permute-start | bytes 786440 | tf_op jit(solution)/shard_map/ppermute | solution.py:208
  34.2 0.6 %shard_map.85.refs_2_ = f32[512,256]{1,0:T(8,128)S(1)} custom-call(bf16[256,2048]{1,0:T(8,128)(2,1)S(1)} %get-tuple-element.53.refs_0_, bf16[256,2048]{1,0:T(8,128)(2,1)S(1)} %get-tuple-element.54.refs_1_, bf16[256,2048]{1,0:T(8,128)(2,1)S(1)} %get-tuple-element.55.refs_2_, bf16[256,2048]{1,0:T(8,128)(2,1)S(1)} %get-tuple-element.56.refs_3_, ...), custom_call_target="tpu_custom_call" | custom-call | flops 268435456 | bytes 1048576 | tf_op jit(solution)/shard_map/pallas_call | solution.py:28
  34.8 0.0 collective-permute-done.8
  34.8 1.8 %collective-permute-start.9 = (bf16[128,256]{1,0:T(8,128)(2,1)S(1)}, bf16[128,256]{1,0:T(8,128)(2,1)S(1)}, u32[]{:S(2)}, u32[]{:S(2)}) collective-permute-start(bf16[128,256]{1,0:T(8,128)(2,1)S(1)} %get-tuple-element.57), channel_id=1, source_target_pairs={{0,6},{1,7},{2,4},{3,5},{4,10},{5,11},{6,8},{7,9},{8,14},{9,15},{1... | collective-permute-start | bytes 196616 | tf_op jit(solution)/shard_map/ppermute | solution.py:205
  36.6 2.9 %collective-permute-done.7 = bf16[128,256]{1,0:T(8,128)(2,1)S(1)} collective-permute-done((bf16[128,256]{1,0:T(8,128)(2,1)S(1)}, bf16[128,256]{1,0:T(8,128)(2,1)S(1)}, u32[]{:S(2)}, u32[]{:S(2)}) %collective-permute-start.7) | collective-permute-done | bytes 65568 | tf_op jit(solution)/shard_map/ppermute | solution.py:205
  39.5 4.1 %collective-permute-done.9 = bf16[128,256]{1,0:T(8,128)(2,1)S(1)} collective-permute-done((bf16[128,256]{1,0:T(8,128)(2,1)S(1)}, bf16[128,256]{1,0:T(8,128)(2,1)S(1)}, u32[]{:S(2)}, u32[]{:S(2)}) %collective-permute-start.9) | collective-permute-done | bytes 65568 | tf_op jit(solution)/shard_map/ppermute | solution.py:205
  43.6 0.3 collective-permute-done.10
  43.9 0.8 %shard_map.87 = (bf16[512,256]{1,0:T(8,128)(2,1)}, bf16[128,128]{1,0:T(8,128)(2,1)}, bf16[128,128]{1,0:T(8,128)(2,1)}) custom-call(f32[128,256]{1,0:T(8,128)S(1)} %convert_add_fusion.1.refs_0_, f32[128,256]{1,0:T(8,128)S(1)} %convert_add_fusion.refs_1_, f32[512,256]{1,0:T(8,128)S(1)} %shard_map.85.refs_2_, bf16[512,256]{1,0:T(8,128)(2,1)S(1)} %collective-permute-done.11.refs_3_), custom_call_target="tpu_custom_call" | custom-call | bytes 1048576 | tf_op jit(solution)/shard_map/pallas_call | solution.py:28
  (8 shorter events, 0.1 us)
Async XLA Ops:
  1.8 14.0 %collective-permute-start = (bf16[512,512]{1,0:T(8,128)(2,1)S(1)}, bf16[512,512]{1,0:T(8,128)(2,1)S(1)}, u32[]{:S(2)}, u32[]{:S(2)}) collective-permute-start(bf16[512,512]{1,0:T(8,128)(2,1)S(1)} %get-tuple-element.30.refs_1_.refs_2_), channel_id=1, source_target_pairs={{0,1},{1,0},{2,3},{3,2},{4,5},{5,4},{6,7},{7,6},{8,9},{9,8},{10,11... | collective-permute-start | bytes 1572872 | tf_op jit(solution)/shard_map/ppermute | solution.py:208
  5.1 11.5 %collective-permute-start.3 = (bf16[256,256]{1,0:T(8,128)(2,1)S(1)}, bf16[256,256]{1,0:T(8,128)(2,1)S(1)}, u32[]{:S(2)}, u32[]{:S(2)}) collective-permute-start(bf16[256,256]{1,0:T(8,128)(2,1)S(1)} %get-tuple-element.31.refs_3_.refs_4_), channel_id=1, source_target_pairs={{0,248},{1,249},{2,250},{3,251},{4,252},{5,253},{6,254},{7,255},{8... | collective-permute-start | bytes 393224 | tf_op jit(solution)/shard_map/ppermute | solution.py:205
  11.2 6.4 %collective-permute-start.2 = (bf16[256,256]{1,0:T(8,128)(2,1)S(1)}, bf16[256,256]{1,0:T(8,128)(2,1)S(1)}, u32[]{:S(2)}, u32[]{:S(2)}) collective-permute-start(bf16[256,256]{1,0:T(8,128)(2,1)S(1)} %get-tuple-element.31.refs_3_.refs_4_), channel_id=1, source_target_pairs={{0,254},{1,255},{2,252},{3,253},{4,2},{5,3},{6,0},{7,1},{8,6},{9,7... | collective-permute-start | bytes 393224 | tf_op jit(solution)/shard_map/ppermute | solution.py:205
  14.4 6.5 %collective-permute-start.1 = (bf16[256,256]{1,0:T(8,128)(2,1)S(1)}, bf16[256,256]{1,0:T(8,128)(2,1)S(1)}, u32[]{:S(2)}, u32[]{:S(2)}) collective-permute-start(bf16[256,256]{1,0:T(8,128)(2,1)S(1)} %get-tuple-element.31.refs_3_.refs_4_), channel_id=1, source_target_pairs={{0,246},{1,247},{2,244},{3,245},{4,250},{5,251},{6,248},{7,249},{8... | collective-permute-start | bytes 393224 | tf_op jit(solution)/shard_map/ppermute | solution.py:205
  21.8 2.5 %collective-permute-start.4 = (f32[8,2048]{1,0:T(8,128)S(1)}, f32[8,2048]{1,0:T(8,128)S(1)}, u32[]{:S(2)}, u32[]{:S(2)}) collective-permute-start(f32[8,2048]{1,0:T(8,128)S(1)} %get-tuple-element.46.refs_0_.refs_6_), channel_id=1, source_target_pairs={{0,1},{1,0},{2,3},{3,2},{4,5},{5,4},{6,7},{7,6},{8,9},{9,8},{10,11... | collective-permute-start | bytes 196616 | tf_op jit(solution)/shard_map/ppermute | solution.py:208
  25.1 4.5 %collective-permute-start.5 = (bf16[128,256]{1,0:T(8,128)(2,1)S(1)}, bf16[128,256]{1,0:T(8,128)(2,1)S(1)}, u32[]{:S(2)}, u32[]{:S(2)}) collective-permute-start(bf16[128,256]{1,0:T(8,128)(2,1)S(1)} %get-tuple-element.38), channel_id=1, source_target_pairs={{0,2},{1,3},{2,0},{3,1},{4,6},{5,7},{6,4},{7,5},{8,10},{9,11},{10,... | collective-permute-start | bytes 196616 | tf_op jit(solution)/shard_map/ppermute | solution.py:208
  29.0 5.8 %collective-permute-start.8 = (bf16[256,256]{1,0:T(8,128)(2,1)S(1)}, bf16[256,256]{1,0:T(8,128)(2,1)S(1)}, u32[]{:S(2)}, u32[]{:S(2)}) collective-permute-start(bf16[256,256]{1,0:T(8,128)(2,1)S(1)} %get-tuple-element.44), channel_id=1, source_target_pairs={{0,2},{1,3},{2,0},{3,1},{4,6},{5,7},{6,4},{7,5},{8,10},{9,11},{10,... | collective-permute-start | bytes 393224 | tf_op jit(solution)/shard_map/ppermute | solution.py:208
  29.7 9.9 %collective-permute-start.7 = (bf16[128,256]{1,0:T(8,128)(2,1)S(1)}, bf16[128,256]{1,0:T(8,128)(2,1)S(1)}, u32[]{:S(2)}, u32[]{:S(2)}) collective-permute-start(bf16[128,256]{1,0:T(8,128)(2,1)S(1)} %add_convert_fusion.2), channel_id=1, source_target_pairs={{0,14},{1,15},{2,12},{3,13},{4,18},{5,19},{6,16},{7,17},{8,22},{9,... | collective-permute-start | bytes 196616 | tf_op jit(solution)/shard_map/ppermute | solution.py:205
  30.7 5.9 %collective-permute-start.6 = (bf16[128,256]{1,0:T(8,128)(2,1)S(1)}, bf16[128,256]{1,0:T(8,128)(2,1)S(1)}, u32[]{:S(2)}, u32[]{:S(2)}) collective-permute-start(bf16[128,256]{1,0:T(8,128)(2,1)S(1)} %get-tuple-element.50), channel_id=1, source_target_pairs={{0,2},{1,3},{2,0},{3,1},{4,6},{5,7},{6,4},{7,5},{8,10},{9,11},{10,... | collective-permute-start | bytes 196616 | tf_op jit(solution)/shard_map/ppermute | solution.py:208
  32.3 11.5 %collective-permute-start.11 = (bf16[512,256]{1,0:T(8,128)(2,1)S(1)}, bf16[512,256]{1,0:T(8,128)(2,1)S(1)}, u32[]{:S(2)}, u32[]{:S(2)}) collective-permute-start(bf16[512,256]{1,0:T(8,128)(2,1)S(1)} %shard_map.86), channel_id=1, source_target_pairs={{0,1},{1,0},{2,3},{3,2},{4,5},{5,4},{6,7},{7,6},{8,9},{9,8},{10,11... | collective-permute-start | bytes 786440 | tf_op jit(solution)/shard_map/ppermute | solution.py:208
  34.8 8.7 %collective-permute-start.9 = (bf16[128,256]{1,0:T(8,128)(2,1)S(1)}, bf16[128,256]{1,0:T(8,128)(2,1)S(1)}, u32[]{:S(2)}, u32[]{:S(2)}) collective-permute-start(bf16[128,256]{1,0:T(8,128)(2,1)S(1)} %get-tuple-element.57), channel_id=1, source_target_pairs={{0,6},{1,7},{2,4},{3,5},{4,10},{5,11},{6,8},{7,9},{8,14},{9,15},{1... | collective-permute-start | bytes 196616 | tf_op jit(solution)/shard_map/ppermute | solution.py:205
  36.6 7.2 %collective-permute-start.10 = (bf16[128,256]{1,0:T(8,128)(2,1)S(1)}, bf16[128,256]{1,0:T(8,128)(2,1)S(1)}, u32[]{:S(2)}, u32[]{:S(2)}) collective-permute-start(bf16[128,256]{1,0:T(8,128)(2,1)S(1)} %get-tuple-element.58), channel_id=1, source_target_pairs={{0,8},{1,9},{2,10},{3,11},{4,12},{5,13},{6,14},{7,15},{8,16},{9,17... | collective-permute-start | bytes 196616 | tf_op jit(solution)/shard_map/ppermute | solution.py:205
